TPU v7x, 512 devices: a whole 4x4x16 slice. The times are simulated.
512 devices in a mesh: gz: 32 (over y_hi, z), gy: 16 (over y_lo, x, core).
Axes of the slice: x: 4, y: 4 (y_hi: 2, y_lo: 2; y = y_hi * 2 + y_lo), z: 16, core: 2. Of those that a mesh axis runs over, the one named last changes fastest.
Arguments:
- observed: float32 [128, 512, 1024], P('gz', 'gy'), may hold values from 0.15 to 6.5
- estimate: float32 [128, 512, 1024], P('gz', 'gy'), may hold values from 0.35 to 2.6
- psf_lateral: float32 [31], replicated, may hold values from 0.1 to 1
- psf_axial: float32 [129], replicated, may hold values from 0.05 to 1
Outputs:
- restored: float32 [128, 512, 1024], P('gz', 'gy')
All inputs are finite; a program needn't handle non-finite values.
Results may differ from a plain program's by a relative error of at most 0.0003.
Values sent between devices are 32-bit elements; how exact they have to be, the bound alone decides.
No kernel may reach another device: no remote copies, remote signals or barrier semaphores. Data moves between devices by JAX's collectives and lax.ppermute only.
A program may use at most 64 MiB of HBM per device.

v0:
```python
import jax
import jax.numpy as jnp
from jax import lax
from jax.sharding import PartitionSpec as P

ITERS = 2


def extended(shard, sides, width):
    for axis, dim in sides:
        size, length = (lax.axis_size(axis), shard.shape[dim])
        up = [(i, (i + 1) % size) for i in range(size - 1)]
        down = [(j, i) for i, j in up]
        last = lax.slice_in_dim(shard, length - width, length, axis=dim)
        initial = lax.slice_in_dim(shard, 0, width, axis=dim)
        before = lax.ppermute(last, axis, up)
        after = lax.ppermute(initial, axis, down)
        shard = jnp.concatenate([before, shard, after], axis=dim)
    return shard


def axial_matrix(weights, planes):
    radius = (weights.shape[0] - 1) // 2
    padded = jnp.pad(weights, (planes, planes))

    def one_row(plane):
        return lax.dynamic_slice(padded, (radius + planes - plane,), (planes,))

    return jax.vmap(one_row)(jnp.arange(planes, dtype=jnp.int32))


def lateral(volume, weights):
    radius = (weights.shape[0] - 1) // 2
    rows_y = volume.shape[1]
    cols_x = volume.shape[2]
    padded = extended(volume, (("gy", 1),), radius)
    summed = jnp.zeros(volume.shape, volume.dtype)
    for tap in range(weights.shape[0]):
        summed = summed + weights[tap] * padded[:, tap : tap + rows_y, :]
    padded = jnp.pad(summed, ((0, 0), (0, 0), (radius, radius)))
    result = jnp.zeros(volume.shape, volume.dtype)
    for tap in range(weights.shape[0]):
        result = result + weights[tap] * padded[:, :, tap : tap + cols_x]
    return result


def apply_axial(matrix, block):
    flat = jnp.dot(matrix, block.reshape(block.shape[0], -1), precision=lax.Precision.HIGHEST)
    return flat.reshape(block.shape)


def local(observed, estimate, psf_lateral, psf_axial):
    lateral_taps = psf_lateral / jnp.sum(psf_lateral)
    axial_taps = psf_axial / jnp.sum(psf_axial)
    flipped = lateral_taps[::-1]
    planes = estimate.shape[0] * lax.axis_size("gz")
    matrix = axial_matrix(axial_taps, planes)
    back_matrix = matrix.T
    current = estimate
    for step in range(ITERS):
        spread = lateral(current, lateral_taps)
        blurred = lax.all_to_all(
            apply_axial(
                matrix, lax.all_to_all(spread, "gz", split_axis=1, concat_axis=0, tiled=True)
            ),
            "gz",
            split_axis=0,
            concat_axis=1,
            tiled=True,
        )
        quotient = observed / blurred
        columns = lax.all_to_all(
            apply_axial(
                back_matrix, lax.all_to_all(quotient, "gz", split_axis=1, concat_axis=0, tiled=True)
            ),
            "gz",
            split_axis=0,
            concat_axis=1,
            tiled=True,
        )
        correction = lateral(columns, flipped)
        current = current * correction
    return current


def solution(mesh):
    in_specs = (P("gz", "gy", None), P("gz", "gy", None), P(), P())
    out_specs = P("gz", "gy", None)
    return jax.shard_map(local, mesh=mesh, in_specs=in_specs, out_specs=out_specs, check_vma=False)
```

profile of v0, /device:TPU:7, one launch (start us, length us, event | category | flops | bytes accessed | tf_op | source)
XLA Modules:
  0.0 733.8 jit_solution(5909896761715456881)
XLA Ops:
  0.0 1.1 fusion.357
  1.3 3.7 collective-permute-start
  5.1 1.9 collective-permute-start.1
  11.5 3.2 collective-permute-done.1
  14.8 23.6 %fusion.264 = f32[4,32,1024]{2,0,1:T(4,128)S(1)} fusion(f32[4,47,1024]{2,0,1:T(4,128)S(1)} %constant_dynamic-update-slice_fusion.2, f32[4,47,1024]{2,0,1:T(4,128)S(1)} %get-tuple-element.27, f32[]{:T(128)} %bitcast.31, f32[]{:T(128)} %bitcast.30, f32[]{:T(128)} %bitcast.29, f32[]{:T(128)} %bitcast.28, f32[]{:T(128)} %bitcast.27, f32[]{:T(128)} %bitcast.26, ...), kind=kLoop, calls=%fused_computation.445 | loop fusion | flops 7995392 | bytes 16777340 | tf_op jit(solution)/shard_map/add | solution.py:39
  38.4 28.6 %multiply_add_fusion.1 = f32[4,32,1024]{2,0,1:T(4,128)} fusion(f32[4,32,1024]{2,0,1:T(4,128)S(1)} %fusion.264, f32[]{:T(128)} %bitcast.31, f32[]{:T(128)} %bitcast.30, f32[]{:T(128)} %bitcast.29, f32[]{:T(128)} %bitcast.28, f32[]{:T(128)} %bitcast.27, f32[]{:T(128)} %bitcast.26, f32[]{:T(128)} %bitcast.25, f32[]{:T(128)} %bitcast.24, f32[]{:T(128)} %bitcast.23, ...), kind=kLoop, calls=%fused_computation.578 | loop fusion | flops 7995392 | bytes 1048700 | tf_op jit(solution)/shard_map/add | solution.py:43
  67.0 17.5 %all-to-all-start = ((f32[4,32,1024]{2,0,1:T(4,128)}), f32[4,32,1024]{2,0,1:T(4,128)S(1)}, u32[]{:S(2)}, u32[]{:S(2)}) async-start(f32[4,32,1024]{2,0,1:T(4,128)} %multiply_add_fusion.1), calls=%async_computation | async-start | bytes 1048576 | tf_op jit(solution)/shard_map/all_to_all | solution.py:64
  84.6 182.0 %while.1 = (s32[]{:T(128)}, f32[385]{0:T(512)S(1)}, s32[128,1]{0,1:T(1,128)S(1)}, f32[128,128]{1,0:T(8,128)S(1)}, s32[]{:T(128)}, /*index=5*/s32[]{:T(128)}) while((s32[]{:T(128)}, f32[385]{0:T(512)S(1)}, s32[128,1]{0,1:T(1,128)S(1)}, f32[128,128]{1,0:T(8,128)S(1)}, s32[]{:T(128)}, /*index=5*/s32[]{:T(128)}) %tuple.80), condition=%wide.while_cond, body=%wide.while_body.sunk | while | flops 2 | bytes 2137 | solution.py:27
  85.2 0.7 dynamic-slice_bitcast_fusion.2
  88.1 0.7 dynamic-slice_bitcast_fusion.2
  89.5 0.7 dynamic-slice_bitcast_fusion.2
  90.9 0.7 dynamic-slice_bitcast_fusion.2
  93.8 0.7 dynamic-slice_bitcast_fusion.2
  95.2 0.7 dynamic-slice_bitcast_fusion.2
  96.6 0.7 dynamic-slice_bitcast_fusion.2
  99.4 0.7 dynamic-slice_bitcast_fusion.2
  100.9 0.7 dynamic-slice_bitcast_fusion.2
  102.3 0.7 dynamic-slice_bitcast_fusion.2
  103.7 0.7 dynamic-slice_bitcast_fusion.2
  105.1 0.7 dynamic-slice_bitcast_fusion.2
  106.6 0.7 dynamic-slice_bitcast_fusion.2
  109.4 0.7 dynamic-slice_bitcast_fusion.2
  110.8 0.7 dynamic-slice_bitcast_fusion.2
  268.0 45.6 %all_to_all.132 = f32[128,1,1024]{2,1,0:T(1,128)S(1)} all-to-all(f32[128,1,1024]{2,1,0:T(1,128)S(1)} %copy.22), channel_id=1, replica_groups=mesh['gz'=32,'gy'=16] {'gz'}, dimensions={0} | all-to-all | bytes 1048576 | tf_op jit(solution)/shard_map/all_to_all | solution.py:62
  314.0 37.3 %all_to_all.133 = f32[4,32,1024]{2,0,1:T(4,128)S(1)} all-to-all(f32[4,32,1024]{2,0,1:T(4,128)S(1)} %bitcast_divide_fusion.1), channel_id=1, replica_groups=mesh['gz'=32,'gy'=16] {'gz'}, dimensions={1} | all-to-all | bytes 1048576 | tf_op jit(solution)/shard_map/all_to_all | solution.py:74
  352.7 37.1 %all_to_all.134 = f32[128,1,1024]{2,1,0:T(1,128)S(1)} all-to-all(f32[128,1,1024]{2,1,0:T(1,128)S(1)} %copy.25), channel_id=1, replica_groups=mesh['gz'=32,'gy'=16] {'gz'}, dimensions={0} | all-to-all | bytes 1048576 | tf_op jit(solution)/shard_map/all_to_all | solution.py:72
  389.8 1.2 reduce
  391.2 1.9 collective-permute-start.2
  393.2 4.1 collective-permute-start.3
  398.7 4.1 collective-permute-done.3
  402.8 23.6 %fusion.175 = f32[4,32,1024]{2,0,1:T(4,128)S(1)} fusion(f32[4,32,1024]{2,0,1:T(4,128)S(1)} %bitcast.122, f32[4,15,1024]{2,0,1:T(4,128)S(1)} %collective-permute-done.3, f32[4,15,1024]{2,0,1:T(4,128)S(1)} %collective-permute-done.2, f32[]{:T(128)} %bitcast.73, f32[]{:T(128)} %bitcast.72, f32[]{:T(128)} %bitcast.71, f32[]{:T(128)} %bitcast.70, f32[]{:T(128)} %bitcast.69, ...), kind=kLoop, calls=%fused_computation.349 | loop fusion | flops 11927552 | bytes 1540220 | tf_op jit(solution)/shard_map/add | solution.py:39
  426.3 27.9 %add_multiply_fusion.1 = f32[4,32,1024]{2,0,1:T(4,128)S(1)} fusion(f32[4,32,1024]{2,0,1:T(4,128)S(1)} %fusion.175, f32[]{:T(128)} %bitcast.73, f32[]{:T(128)} %bitcast.72, f32[]{:T(128)} %bitcast.71, f32[]{:T(128)} %bitcast.70, f32[]{:T(128)} %bitcast.69, f32[]{:T(128)} %bitcast.68, f32[]{:T(128)} %bitcast.67, f32[]{:T(128)} %bitcast.66, f32[]{:T(128)} %bitcast.65, ...), kind=kLoop, calls=%fused_computation.554 | loop fusion | flops 8126464 | bytes 1572988 | tf_op jit(solution)/shard_map/mul | solution.py:82
  454.3 1.9 collective-permute-start.4
  456.2 2.4 collective-permute-start.5
  459.3 6.5 collective-permute-done.5
  465.8 23.6 %fusion.89 = f32[4,32,1024]{2,0,1:T(4,128)S(1)} fusion(f32[4,32,1024]{2,0,1:T(4,128)S(1)} %add_multiply_fusion.1, f32[4,15,1024]{2,0,1:T(4,128)S(1)} %collective-permute-done.5, f32[4,15,1024]{2,0,1:T(4,128)S(1)} %collective-permute-done.4, f32[]{:T(128)} %bitcast.31, f32[]{:T(128)} %bitcast.30, f32[]{:T(128)} %bitcast.29, f32[]{:T(128)} %bitcast.28, ...), kind=kLoop, calls=%fused_computation.263 | loop fusion | flops 11927552 | bytes 1540220 | tf_op jit(solution)/shard_map/add | solution.py:39
  489.5 28.0 %multiply_add_fusion = f32[4,32,1024]{2,0,1:T(4,128)S(1)} fusion(f32[4,32,1024]{2,0,1:T(4,128)S(1)} %fusion.89, f32[]{:T(128)} %bitcast.31, f32[]{:T(128)} %bitcast.30, f32[]{:T(128)} %bitcast.29, f32[]{:T(128)} %bitcast.28, f32[]{:T(128)} %bitcast.27, f32[]{:T(128)} %bitcast.26, f32[]{:T(128)} %bitcast.25, f32[]{:T(128)} %bitcast.24, f32[]{:T(128)} %bitcast.23, ...), kind=kLoop, calls=%fused_computation.530 | loop fusion | flops 7995392 | bytes 1048700 | tf_op jit(solution)/shard_map/add | solution.py:43
  517.4 36.6 %all_to_all.135 = f32[4,32,1024]{2,0,1:T(4,128)S(1)} all-to-all(f32[4,32,1024]{2,0,1:T(4,128)S(1)} %multiply_add_fusion), channel_id=1, replica_groups=mesh['gz'=32,'gy'=16] {'gz'}, dimensions={1} | all-to-all | bytes 1048576 | tf_op jit(solution)/shard_map/all_to_all | solution.py:64
  555.4 36.6 %all_to_all.136 = f32[128,1,1024]{2,1,0:T(1,128)S(1)} all-to-all(f32[128,1,1024]{2,1,0:T(1,128)S(1)} %copy.27), channel_id=1, replica_groups=mesh['gz'=32,'gy'=16] {'gz'}, dimensions={0} | all-to-all | bytes 1048576 | tf_op jit(solution)/shard_map/all_to_all | solution.py:62
  592.4 37.5 %all_to_all.137 = f32[4,32,1024]{2,0,1:T(4,128)S(1)} all-to-all(f32[4,32,1024]{2,0,1:T(4,128)S(1)} %bitcast_divide_fusion), channel_id=1, replica_groups=mesh['gz'=32,'gy'=16] {'gz'}, dimensions={1} | all-to-all | bytes 1048576 | tf_op jit(solution)/shard_map/all_to_all | solution.py:74
  631.2 37.1 %all_to_all.138 = f32[128,1,1024]{2,1,0:T(1,128)S(1)} all-to-all(f32[128,1,1024]{2,1,0:T(1,128)S(1)} %copy.30), channel_id=1, replica_groups=mesh['gz'=32,'gy'=16] {'gz'}, dimensions={0} | all-to-all | bytes 1048576 | tf_op jit(solution)/shard_map/all_to_all | solution.py:72
  668.3 1.2 reduce.1
  669.7 1.9 collective-permute-start.6
  671.6 4.1 collective-permute-start.7
  675.8 5.5 collective-permute-done.7
  681.3 23.6 %fusion.3 = f32[4,32,1024]{2,0,1:T(4,128)S(1)} fusion(f32[4,32,1024]{2,0,1:T(4,128)S(1)} %bitcast.124, f32[4,15,1024]{2,0,1:T(4,128)S(1)} %collective-permute-done.7, f32[4,15,1024]{2,0,1:T(4,128)S(1)} %collective-permute-done.6, f32[]{:T(128)} %bitcast.73, f32[]{:T(128)} %bitcast.72, f32[]{:T(128)} %bitcast.71, f32[]{:T(128)} %bitcast.70, f32[]{:T(128)} %bitcast.69, ...), kind=kLoop, calls=%fused_computation.177 | loop fusion | flops 11927552 | bytes 1540220 | tf_op jit(solution)/shard_map/add | solution.py:39
  704.8 27.9 %add_multiply_fusion = f32[4,32,1024]{2,0,1:T(4,128)S(1)} fusion(f32[4,32,1024]{2,0,1:T(4,128)S(1)} %add_multiply_fusion.1, f32[4,32,1024]{2,0,1:T(4,128)S(1)} %fusion.3, f32[]{:T(128)} %bitcast.73, f32[]{:T(128)} %bitcast.72, f32[]{:T(128)} %bitcast.71, f32[]{:T(128)} %bitcast.70, f32[]{:T(128)} %bitcast.69, f32[]{:T(128)} %bitcast.68, f32[]{:T(128)} %bitcast.67, ...), kind=kLoop, calls=%fused_computation.506 | loop fusion | flops 8126464 | bytes 1572988 | tf_op jit(solution)/shard_map/mul | solution.py:82
  732.7 1.1 copy.31
  (418 shorter events, 183.9 us)
Async XLA Ops:
  1.1 6.0 copy-start.3
  1.1 6.7 copy-start.2
  1.3 9.8 %collective-permute-start = (f32[4,15,1024]{2,0,1:T(4,128)S(1)}, f32[4,15,1024]{2,0,1:T(4,128)S(1)}, u32[]{:S(2)}, u32[]{:S(2)}) collective-permute-start(f32[4,15,1024]{2,0,1:T(4,128)S(1)} %copy.43), channel_id=1, source_target_pairs={{0,1},{1,2},{2,3},{3,4},{4,5},{5,6},{6,7},{7,8},{8,9},{9,10},{10,1... | collective-permute-start | bytes 737288 | tf_op jit(solution)/shard_map/ppermute | solution.py:16
  5.0 6.1 copy-start
  5.1 9.6 %collective-permute-start.1 = (f32[4,15,1024]{2,0,1:T(4,128)S(1)}, f32[4,15,1024]{2,0,1:T(4,128)S(1)}, u32[]{:S(2)}, u32[]{:S(2)}) collective-permute-start(f32[4,15,1024]{2,0,1:T(4,128)S(1)} %copy.42), channel_id=1, source_target_pairs={{1,0},{2,1},{3,2},{4,3},{5,4},{6,5},{7,6},{8,7},{9,8},{10,9},{11,1... | collective-permute-start | bytes 737288 | tf_op jit(solution)/shard_map/ppermute | solution.py:17
  67.0 199.6 %all-to-all-start = ((f32[4,32,1024]{2,0,1:T(4,128)}), f32[4,32,1024]{2,0,1:T(4,128)S(1)}, u32[]{:S(2)}, u32[]{:S(2)}) async-start(f32[4,32,1024]{2,0,1:T(4,128)} %multiply_add_fusion.1), calls=%async_computation | async-start | bytes 1048576 | tf_op jit(solution)/shard_map/all_to_all | solution.py:64
  267.9 45.7 %copy-start.1 = (f32[4,32,1024]{2,1,0:T(8,128)S(1)}, f32[4,32,1024]{2,1,0:T(8,128)}, u32[]{:S(2)}) copy-start(f32[4,32,1024]{2,1,0:T(8,128)} %param.4) | copy-start | bytes 1572868
  391.2 7.5 %collective-permute-start.2 = (f32[4,15,1024]{2,0,1:T(4,128)S(1)}, f32[4,15,1024]{2,0,1:T(4,128)S(1)}, u32[]{:S(2)}, u32[]{:S(2)}) collective-permute-start(f32[4,15,1024]{2,0,1:T(4,128)S(1)} %get-tuple-element.25), channel_id=1, source_target_pairs={{0,1},{1,2},{2,3},{3,4},{4,5},{5,6},{6,7},{7,8},{8,9},{9,10},{10,1... | collective-permute-start | bytes 737288 | tf_op jit(solution)/shard_map/ppermute | solution.py:16
  393.2 9.6 %collective-permute-start.3 = (f32[4,15,1024]{2,0,1:T(4,128)S(1)}, f32[4,15,1024]{2,0,1:T(4,128)S(1)}, u32[]{:S(2)}, u32[]{:S(2)}) collective-permute-start(f32[4,15,1024]{2,0,1:T(4,128)S(1)} %get-tuple-element.26), channel_id=1, source_target_pairs={{1,0},{2,1},{3,2},{4,3},{5,4},{6,5},{7,6},{8,7},{9,8},{10,9},{11,1... | collective-permute-start | bytes 737288 | tf_op jit(solution)/shard_map/ppermute | solution.py:17
  454.3 5.0 collective-permute-start.4
  456.2 9.6 %collective-permute-start.5 = (f32[4,15,1024]{2,0,1:T(4,128)S(1)}, f32[4,15,1024]{2,0,1:T(4,128)S(1)}, u32[]{:S(2)}, u32[]{:S(2)}) collective-permute-start(f32[4,15,1024]{2,0,1:T(4,128)S(1)} %get-tuple-element.24), channel_id=1, source_target_pairs={{1,0},{2,1},{3,2},{4,3},{5,4},{6,5},{7,6},{8,7},{9,8},{10,9},{11,1... | collective-permute-start | bytes 737288 | tf_op jit(solution)/shard_map/ppermute | solution.py:17
  669.7 6.1 collective-permute-start.6
  671.6 9.6 %collective-permute-start.7 = (f32[4,15,1024]{2,0,1:T(4,128)S(1)}, f32[4,15,1024]{2,0,1:T(4,128)S(1)}, u32[]{:S(2)}, u32[]{:S(2)}) collective-permute-start(f32[4,15,1024]{2,0,1:T(4,128)S(1)} %get-tuple-element.22), channel_id=1, source_target_pairs={{1,0},{2,1},{3,2},{4,3},{5,4},{6,5},{7,6},{8,7},{9,8},{10,9},{11,1... | collective-permute-start | bytes 737288 | tf_op jit(solution)/shard_map/ppermute | solution.py:17
where the time goes:
time: 740 us; the launch traced here: 734 us
  blocking collectives  268 us (36%)
  other arithmetic  212 us (29%)
  local copies, waits for them, and re-layouts  191 us (26%)
  starting transfers between devices  39.5 us (5%)
  waiting for transfers between devices  20 us (3%)
    gather x384, local copies, waits for them, and re-layouts  182 us
    add x4, other arithmetic, lateral(): summed = summed + weights[tap] * padded[:, tap:tap + rows_y, :]  94.3 us
    all_to_all x2, blocking collectives, local(): lax.all_to_all(apply_axial(matrix, lax.all_to_all(spread, 'gz', split_axi...  82.2 us
    all_to_all x2, blocking collectives, local(): lax.all_to_all(quotient, 'gz', split_axis=1, concat_axis=0, tiled=True)  74.8 us
    all_to_all x2, blocking collectives, local(): lax.all_to_all(apply_axial(back_matrix, lax.all_to_all(quotient, 'gz', sp...  74.2 us
    add x2, other arithmetic, lateral(): result = result + weights[tap] * padded[:, :, tap:tap + cols_x]  56.6 us
    mul x2, other arithmetic, local(): current = current * correction  55.8 us
    all_to_all x1, blocking collectives, local(): lax.all_to_all(spread, 'gz', split_axis=1, concat_axis=0, tiled=True)  36.6 us
  transfers between devices with their start and end apart: 9, of which 5 were waited for; matrix products, arithmetic and copies ran while one was open for 26% of the time, Pallas kernels for 0%

commit v1 on v0

v1 whole, which is shorter than its diff:
```python
import functools
import jax
import jax.numpy as jnp
from jax import lax
from jax.experimental import pallas as pl
from jax.experimental.pallas import tpu as pltpu
from jax.sharding import PartitionSpec as P

ITERS = 2
F32 = jnp.float32
BF16 = jnp.bfloat16
H = 15
G = 64
T = 32
HALF = T // 2
NX = 1024
TILES = NX // T
NZ = 128
TILE = (T, T, NZ)
PART = (HALF, T, NZ)

VMEM = pl.BlockSpec(memory_space=pltpu.VMEM)
SMEM = pl.BlockSpec(memory_space=pltpu.SMEM)


def call(body, outs, operands, smem=(), flops=4_000_000, moved=2_000_000, scratch=()):
    return pl.pallas_call(
        body,
        out_shape=[jax.ShapeDtypeStruct(s, d) for s, d in outs],
        in_specs=[SMEM if i in smem else VMEM for i in range(len(operands))],
        out_specs=[VMEM] * len(outs),
        scratch_shapes=list(scratch),
        cost_estimate=pl.CostEstimate(flops=flops, bytes_accessed=moved, transcendentals=0),
        compiler_params=pltpu.CompilerParams(vmem_limit_bytes=24 * 1024 * 1024),
    )(*operands)


def split(v):
    hi = v.astype(BF16)
    return hi, (v - hi.astype(F32)).astype(BF16)


def swap_groups(rows):
    lane = lax.broadcasted_iota(jnp.int32, rows[0].shape, 1)
    low64, low32 = lane < 64, (lane & 32) == 0
    a, b, c, d = rows
    a, c = jnp.where(low64, a, pltpu.roll(c, 64, 1)), jnp.where(low64, pltpu.roll(a, 64, 1), c)
    b, d = jnp.where(low64, b, pltpu.roll(d, 64, 1)), jnp.where(low64, pltpu.roll(b, 64, 1), d)
    a, b = jnp.where(low32, a, pltpu.roll(b, 32, 1)), jnp.where(low32, pltpu.roll(a, 96, 1), b)
    c, d = jnp.where(low32, c, pltpu.roll(d, 32, 1)), jnp.where(low32, pltpu.roll(c, 96, 1), d)
    return a, b, c, d


def to_tiles_kernel(block_ref, out_ref):
    for z in range(4):
        for th in range(8):
            rows = [block_ref[z, pl.ds(8 * yh, 8), pl.ds(128 * th, 128)] for yh in range(4)]
            for tl, tile in enumerate(swap_groups(rows)):
                out_ref[4 * th + tl, z] = tile


def to_tiles_shifted_kernel(shift_ref, block_ref, out_ref, rolled):
    for z in range(4):
        rolled[z] = pltpu.roll(block_ref[z], shift_ref[0], 1)
    to_tiles_kernel(rolled, out_ref)


def from_tiles_kernel(tiles_ref, out_ref):
    for z in range(4):
        for th in range(8):
            tiles = [tiles_ref[4 * th + tl, z] for tl in range(4)]
            for yh, row in enumerate(swap_groups(tiles)):
                out_ref[z, pl.ds(8 * yh, 8), pl.ds(128 * th, 128)] = row


def matrices_kernel(place_ref, lat_ref, band_ref, z_fwd, z_bwd, x_fwd, x_bwd):
    tile, side = place_ref[0], place_ref[1]
    band = band_ref[...]
    band = band / jnp.sum(band)
    wide = jnp.broadcast_to(band, (NZ, 2 * NZ))
    back = pltpu.roll(wide, 0, 1, stride=1, stride_axis=0)[:, :NZ]
    for m, ref in ((back.T, z_fwd), (back, z_bwd)):
        hi, lo = split(m)
        ref[pl.ds(0, NZ), pl.ds(0, NZ)] = hi
        ref[pl.ds(NZ, NZ), pl.ds(0, NZ)] = hi
        ref[pl.ds(0, NZ), pl.ds(NZ, NZ)] = lo
        ref[pl.ds(NZ, NZ), pl.ds(NZ, NZ)] = jnp.zeros_like(lo)
    total = lat_ref[0]
    for k in range(1, 2 * H + 1):
        total = total + lat_ref[k]
    row = lax.broadcasted_iota(jnp.int32, (T, NZ), 0)
    lane = lax.broadcasted_iota(jnp.int32, (T, NZ), 1)
    own, first = lane < 64, (lane & 32) == 0
    col = lane & 31
    here = T * tile
    shifted = here + H * side
    wrap = lambda v: v & (NX - 1)
    src_f = wrap(jnp.where(own, here, here + T * side) + col)
    dst_f = wrap(shifted + row)
    src_b = wrap(jnp.where(own, shifted, shifted - T * side) + col)
    dst_b = wrap(here + row)
    for d, ref in ((src_f - dst_f, x_fwd), (dst_b - src_b, x_bwd)):
        m = jnp.zeros((T, NZ), F32)
        for k in range(2 * H + 1):
            m = jnp.where(d == k - H, lat_ref[k], m)
        scale = jnp.full((T, NZ), total, F32)
        m = m / scale / scale
        hi, lo = split(m)
        ref[pl.ds(0, T), :] = hi
        ref[pl.ds(T, T), :] = jnp.where(first, lo.astype(F32), 0.0).astype(BF16)


def z_pass(v, m):
    r = jnp.dot(jnp.concatenate(split(v), axis=1), m, preferred_element_type=F32)
    return r[:, :NZ] + r[:, NZ:]


def x_pass(own, nbr, m):
    columns = []
    for o, n in zip(own, nbr):
        columns.append(jnp.concatenate([*split(o), *split(n)], axis=0))
    r = jnp.dot(m, jnp.concatenate(columns, axis=1), preferred_element_type=F32)
    r = r[:T] + r[T:]
    return [r[:, NZ * i : NZ * (i + 1)] for i in range(len(own))]


def y_pass(parts, taps_ref, flip, emit):
    def source(e, x8):
        part, r = divmod(e + 1, HALF)
        return parts[part][r, pl.ds(x8, 8), :]

    taps = [taps_ref[2 * H - k if flip else k] for k in range(2 * H + 1)]

    @pl.loop(0, T // 8)
    def _(i):
        x8 = pl.multiple_of(i * 8, 8)
        for y0 in range(0, T, 8):
            acc = [None] * 8
            for e in range(8 + 2 * H):
                v = source(y0 + e, x8)
                for j in range(max(0, e - 2 * H), min(8, e + 1)):
                    term = taps[e - j] * v
                    acc[j] = term if acc[j] is None else acc[j] + term
            for j in range(8):
                emit(y0 + j, x8, acc[j])


def half(y, first, second):
    return (first, y) if y < HALF else (second, y - HALF)


def arrive_kernel(tiles_ref, m_ref, cur_ref, a_ref, b_ref):
    m = m_ref[...]
    for lo in range(8):
        v = tiles_ref[pl.ds(lo, NZ, stride=8), :].T
        w = z_pass(v, m)
        for hi in range(4):
            y = 8 * hi + lo
            cur_ref[y] = v[T * hi : T * (hi + 1)]
            ref, r = half(y, a_ref, b_ref)
            ref[r] = w[T * hi : T * (hi + 1)]


def arrive_plain_kernel(tiles_ref, out_ref):
    for lo in range(8):
        v = tiles_ref[pl.ds(lo, NZ, stride=8), :].T
        for hi in range(4):
            out_ref[8 * hi + lo] = v[T * hi : T * (hi + 1)]


def y_kernel(taps_ref, up, first, second, down, out_ref):
    def emit(y, x8, v):
        out_ref[y, pl.ds(x8, 8), :] = v

    y_pass((up, first, second, down), taps_ref, False, emit)


def quotient_kernel(own_ref, nbr_ref, obs_ref, m_ref, q_ref):
    m = m_ref[...]
    for y in range(0, T, 2):
        pair = (y, y + 1)
        for i, r in zip(pair, x_pass([own_ref[i] for i in pair], [nbr_ref[i] for i in pair], m)):
            q_ref[i] = obs_ref[i] / r


def back_kernel(own_ref, nbr_ref, mx_ref, mz_ref, a_ref, b_ref):
    mx, mz = mx_ref[...], mz_ref[...]
    for y in range(0, T, 4):
        rows = []
        for i in (y, y + 2):
            pair = (i, i + 1)
            rows += x_pass([own_ref[k] for k in pair], [nbr_ref[k] for k in pair], mx)
        w = z_pass(jnp.concatenate(rows, axis=0), mz)
        for i in range(4):
            ref, r = half(y + i, a_ref, b_ref)
            ref[r] = w[T * i : T * (i + 1)]


def update_kernel(taps_ref, up, first, second, down, cur_ref, m_ref, out_ref, a_ref, b_ref):
    def emit(y, x8, v):
        at = (y, pl.ds(x8, 8), slice(None))
        out_ref[at] = cur_ref[at] * v

    y_pass((up, first, second, down), taps_ref, True, emit)
    m = m_ref[...]
    for y in range(0, T, 4):
        w = z_pass(jnp.concatenate([out_ref[y + i] for i in range(4)], axis=0), m)
        for i in range(4):
            ref, r = half(y + i, a_ref, b_ref)
            ref[r] = w[T * i : T * (i + 1)]


def leave_kernel(taps_ref, up, first, second, down, cur_ref, tiles_ref, work):
    def emit(y, x8, v):
        at = (y, pl.ds(x8, 8), slice(None))
        work[at] = cur_ref[at] * v

    y_pass((up, first, second, down), taps_ref, True, emit)
    for lo in range(8):
        v = jnp.concatenate([work[8 * hi + lo] for hi in range(4)], axis=0)
        tiles_ref[pl.ds(lo, NZ, stride=8), :] = v.T


def local(observed, estimate, psf_lateral, psf_axial):
    n_z, n_y = lax.axis_size("gz"), lax.axis_size("gy")
    gz, gy = lax.axis_index("gz").astype(jnp.int32), lax.axis_index("gy").astype(jnp.int32)
    side = 1 - 2 * (gy % 2)
    joint = ("gz", "gy")

    def turn(sign):
        pairs = []
        for z in range(n_z):
            for y in range(n_y):
                s = sign * (1 if y % 2 == 0 else -1)
                pairs.append(((z + s) % n_z * n_y + y, z * n_y + y))
        return pairs

    ahead, behind = turn(1), turn(-1)
    up = [(i, i + 1) for i in range(n_y - 1)]
    down = [(i + 1, i) for i in range(n_y - 1)]

    def y_parts(first, second):
        return lax.ppermute(second, "gy", up), first, second, lax.ppermute(first, "gy", down)

    def exchange(tiles):
        return lax.all_to_all(tiles, "gz", split_axis=0, concat_axis=0, tiled=True)

    tiles_shape = (TILES, 4, 8, 128)
    flat = (NZ * 8, 128)
    (est_tiles,) = call(to_tiles_kernel, [(tiles_shape, F32)], [estimate])
    shift = jnp.where(side > 0, NX - H, H).astype(jnp.int32).reshape(1)
    (obs_tiles,) = call(
        to_tiles_shifted_kernel,
        [(tiles_shape, F32)],
        [shift, observed],
        smem=(0,),
        scratch=[pltpu.VMEM((4, T, NX), F32)],
    )
    band = jnp.concatenate([psf_axial[G:], jnp.zeros((2 * NZ - 2 * G - 1,), F32), psf_axial[:G]])
    z_fwd, z_bwd, x_fwd, x_bwd = call(
        matrices_kernel,
        [((2 * NZ, 2 * NZ), BF16)] * 2 + [((2 * T, 4 * T), BF16)] * 2,
        [jnp.stack([gz, side]), psf_lateral, band.reshape(1, 2 * NZ)],
        smem=(0, 1),
    )
    est_tiles = exchange(est_tiles)
    obs_tiles = exchange(obs_tiles)
    current, first, second = call(
        arrive_kernel,
        [(TILE, F32), (PART, F32), (PART, F32)],
        [est_tiles.reshape(flat), z_fwd],
    )
    (obs,) = call(arrive_plain_kernel, [(TILE, F32)], [obs_tiles.reshape(flat)])
    for step in range(ITERS):
        (own,) = call(
            y_kernel, [(TILE, F32)], [psf_lateral, *y_parts(first, second)], smem=(0,)
        )
        (own,) = call(
            quotient_kernel, [(TILE, F32)], [own, lax.ppermute(own, joint, ahead), obs, x_fwd]
        )
        first, second = call(
            back_kernel,
            [(PART, F32)] * 2,
            [own, lax.ppermute(own, joint, behind), x_bwd, z_bwd],
        )
        operands = [psf_lateral, *y_parts(first, second), current]
        if step < ITERS - 1:
            current, first, second = call(
                update_kernel,
                [(TILE, F32), (PART, F32), (PART, F32)],
                [*operands, z_fwd],
                smem=(0,),
            )
        else:
            (tiles,) = call(
                leave_kernel, [(flat, F32)], operands, smem=(0,), scratch=[pltpu.VMEM(TILE, F32)]
            )
    tiles = exchange(tiles.reshape(tiles_shape))
    (out,) = call(from_tiles_kernel, [((4, T, NX), F32)], [tiles])
    return out


def solution(mesh):
    in_specs = (P("gz", "gy", None), P("gz", "gy", None), P(), P())
    out_specs = P("gz", "gy", None)
    return jax.shard_map(local, mesh=mesh, in_specs=in_specs, out_specs=out_specs, check_vma=False)
```

time: 740 us -> 215 us (0.29)
  blocking collectives: 268 us -> 35.2 us
  other arithmetic: 212 us -> 0.15 us
  local copies, waits for them, and re-layouts: 191 us -> 3.1 us
  waiting for transfers between devices: 20 us -> 101 us
  Pallas kernels: 0 us -> 17.9 us
  starting transfers between devices: 39.5 us -> 56.4 us
    all_to_all x7 -> x1, blocking collectives: 268 us -> 35.2 us  [exchange(): return lax.all_to_all(tiles, 'gz', split_axis=0, concat_axis=0, tiled=True)]
    gather x384 -> x0, local copies, waits for them, and re-layouts: 182 us -> none
    add x6 -> x0, other arithmetic: 151 us -> none  [the longest x4 94.3 us: lateral(): summed = summed + weights[tap] * padded[:, tap:tap + rows_y, :]]
    mul x2 -> x0, other arithmetic: 55.8 us -> none  [local(): current = current * correction]
    ppermute x8 -> x12, waiting for transfers between devices: 20 us -> 61.2 us  [the longest x4 27.7 us: y_parts(): lax.ppermute(first, 'gy', down)]
    all_to_all x1 -> x2, waiting for transfers between devices: 0.01 us -> 39.8 us  [exchange(): return lax.all_to_all(tiles, 'gz', split_axis=0, concat_axis=0, tiled=True)]
    pallas_call x0 -> x14, Pallas kernels: none -> 17.9 us  [call(): pl.pallas_call(body, out_shape=[jax.ShapeDtypeStruct(s, d) for s, d in ou...]
    ppermute x8 -> x12, starting transfers between devices: 22 us -> 32.6 us  [the longest x4 14 us: y_parts(): lax.ppermute(second, 'gy', up)]
  transfers between devices with their start and end apart: 9 -> 14, of which waited for: 5 -> 14; matrix products, arithmetic and copies ran while one was open for 26% -> 0% of each run, Pallas kernels for 0% -> 3%
where the time goes in v1:
time: 215 us; the launch traced here: 214 us
  waiting for transfers between devices  101 us (47%)
  starting transfers between devices  56.4 us (26%)
  blocking collectives  35.2 us (16%)
  Pallas kernels  17.9 us (8%)
  local copies, waits for them, and re-layouts  3.1 us (1%)
    all_to_all x2, waiting for transfers between devices, exchange(): return lax.all_to_all(tiles, 'gz', split_axis=0, concat_axis=0, tiled=True)  39.8 us
    all_to_all x1, blocking collectives, exchange(): return lax.all_to_all(tiles, 'gz', split_axis=0, concat_axis=0, tiled=True)  35.2 us
    ppermute x4, waiting for transfers between devices, y_parts(): lax.ppermute(first, 'gy', down)  27.7 us
    all_to_all x2, starting transfers between devices, exchange(): return lax.all_to_all(tiles, 'gz', split_axis=0, concat_axis=0, tiled=True)  23.8 us
    pallas_call x14, Pallas kernels, call(): pl.pallas_call(body, out_shape=[jax.ShapeDtypeStruct(s, d) for s, d in ou...  17.9 us
    ppermute x2, waiting for transfers between devices, local(): lax.ppermute(own, joint, behind)  14.6 us
    ppermute x4, starting transfers between devices, y_parts(): lax.ppermute(second, 'gy', up)  14 us
    ppermute x2, waiting for transfers between devices, local(): lax.ppermute(own, joint, ahead)  13.4 us
  transfers between devices with their start and end apart: 14, of which 14 were waited for; matrix products, arithmetic and copies ran while one was open for 0% of the time, Pallas kernels for 3%

profile of v1, /device:TPU:7, one launch (start us, length us, event | category | flops | bytes accessed | tf_op | source)
XLA Modules:
  0.0 213.9 jit_solution(15404425159750414900)
XLA Ops:
  0.0 1.0 copy-done
  1.0 2.2 %shard_map.46 = f32[32,4,8,128]{3,2,1,0:T(8,128)} custom-call(f32[4,32,1024]{2,1,0:T(8,128)S(1)} %copy-done), custom_call_target="tpu_custom_call" | custom-call | flops 4000000 | bytes 2000000 | tf_op jit(solution)/shard_map/pallas_call | solution.py:27
  3.3 18.0 %all-to-all-start = ((f32[32,4,8,128]{3,2,1,0:T(8,128)}), f32[32,4,8,128]{3,2,1,0:T(8,128)S(1)}, u32[]{:S(2)}, u32[]{:S(2)}) async-start(f32[32,4,8,128]{3,2,1,0:T(8,128)} %shard_map.46), calls=%async_computation | async-start | bytes 1048576 | tf_op jit(solution)/shard_map/all_to_all | solution.py:246
  21.3 2.9 %shard_map.50 = f32[32,4,8,128]{3,2,1,0:T(8,128)} custom-call(s32[1]{0:T(128)} %bitcast.4.shift_ref, f32[4,32,1024]{2,1,0:T(8,128)S(1)} %copy-done.1), custom_call_target="tpu_custom_call" | custom-call | flops 4000000 | bytes 2000000 | tf_op jit(solution)/shard_map/pallas_call | solution.py:27
  24.2 29.3 %all-to-all-done = f32[32,4,8,128]{3,2,1,0:T(8,128)S(1)} async-done(((f32[32,4,8,128]{3,2,1,0:T(8,128)}), f32[32,4,8,128]{3,2,1,0:T(8,128)S(1)}, u32[]{:S(2)}, u32[]{:S(2)}) %all-to-all-start) | async-done | bytes 524320 | tf_op jit(solution)/shard_map/all_to_all | solution.py:246
  53.4 5.8 %all-to-all-start.1 = ((f32[32,4,8,128]{3,2,1,0:T(8,128)}), f32[32,4,8,128]{3,2,1,0:T(8,128)S(1)}, u32[]{:S(2)}, u32[]{:S(2)}) async-start(f32[32,4,8,128]{3,2,1,0:T(8,128)} %shard_map.50), calls=%async_computation.1 | async-start | bytes 1048576 | tf_op jit(solution)/shard_map/all_to_all | solution.py:246
  59.3 0.7 copy-done.3
  60.1 0.7 slice-done
  60.8 0.1 pad_maximum_fusion
  60.8 0.7 copy-done.2
  61.5 0.8 shard_map.47
  62.3 0.3 shard_map.48
  62.7 3.0 %collective-permute-start = (f32[16,32,128]{2,1,0:T(8,128)S(1)}, f32[16,32,128]{2,1,0:T(8,128)S(1)}, u32[]{:S(2)}, u32[]{:S(2)}) collective-permute-start(f32[16,32,128]{2,1,0:T(8,128)S(1)} %get-tuple-element.20.second), channel_id=1, source_target_pairs={{0,1},{1,2},{2,3},{3,4},{4,5},{5,6},{6,7},{7,8},{8,9},{9,10},{10,1... | collective-permute-start | bytes 786440 | tf_op jit(solution)/shard_map/ppermute | solution.py:243
  65.7 1.9 collective-permute-start.1
  67.6 1.8 collective-permute-done.up
  69.4 6.7 %collective-permute-done.1.down = f32[16,32,128]{2,1,0:T(8,128)S(1)} collective-permute-done((f32[16,32,128]{2,1,0:T(8,128)S(1)}, f32[16,32,128]{2,1,0:T(8,128)S(1)}, u32[]{:S(2)}, u32[]{:S(2)}) %collective-permute-start.1) | collective-permute-done | bytes 262176 | tf_op jit(solution)/shard_map/ppermute | solution.py:243
  76.1 1.7 shard_map.49.own_ref
  77.8 3.1 %collective-permute-start.2 = (f32[32,32,128]{2,1,0:T(8,128)S(1)}, f32[32,32,128]{2,1,0:T(8,128)S(1)}, u32[]{:S(2)}, u32[]{:S(2)}) collective-permute-start(f32[32,32,128]{2,1,0:T(8,128)S(1)} %shard_map.49.own_ref), channel_id=1, source_target_pairs={{16,0},{497,1},{18,2},{499,3},{20,4},{501,5},{22,6},{503,7},{24,8}... | collective-permute-start | bytes 1572872 | tf_op jit(solution)/shard_map/ppermute | solution.py:279
  80.9 10.6 %all-to-all-done.1 = f32[32,4,8,128]{3,2,1,0:T(8,128)S(1)} async-done(((f32[32,4,8,128]{3,2,1,0:T(8,128)}), f32[32,4,8,128]{3,2,1,0:T(8,128)S(1)}, u32[]{:S(2)}, u32[]{:S(2)}) %all-to-all-start.1) | async-done | bytes 524320 | tf_op jit(solution)/shard_map/all_to_all | solution.py:246
  91.5 0.2 shard_map.51.obs_ref
  91.7 1.8 collective-permute-done.2.nbr_ref
  93.5 0.3 shard_map.52.own_ref
  93.8 3.6 %collective-permute-start.3 = (f32[32,32,128]{2,1,0:T(8,128)S(1)}, f32[32,32,128]{2,1,0:T(8,128)S(1)}, u32[]{:S(2)}, u32[]{:S(2)}) collective-permute-start(f32[32,32,128]{2,1,0:T(8,128)S(1)} %shard_map.52.own_ref), channel_id=1, source_target_pairs={{496,0},{17,1},{498,2},{19,3},{500,4},{21,5},{502,6},{23,7},{504,8... | collective-permute-start | bytes 1572872 | tf_op jit(solution)/shard_map/ppermute | solution.py:284
  97.4 6.6 %collective-permute-done.3.nbr_ref = f32[32,32,128]{2,1,0:T(8,128)S(1)} collective-permute-done((f32[32,32,128]{2,1,0:T(8,128)S(1)}, f32[32,32,128]{2,1,0:T(8,128)S(1)}, u32[]{:S(2)}, u32[]{:S(2)}) %collective-permute-start.3) | collective-permute-done | bytes 524320 | tf_op jit(solution)/shard_map/ppermute | solution.py:284
  104.0 0.5 shard_map.53
  104.6 6.2 %collective-permute-start.4 = (f32[16,32,128]{2,1,0:T(8,128)S(1)}, f32[16,32,128]{2,1,0:T(8,128)S(1)}, u32[]{:S(2)}, u32[]{:S(2)}) collective-permute-start(f32[16,32,128]{2,1,0:T(8,128)S(1)} %get-tuple-element.25.second), channel_id=1, source_target_pairs={{0,1},{1,2},{2,3},{3,4},{4,5},{5,6},{6,7},{7,8},{8,9},{9,10},{10,1... | collective-permute-start | bytes 786440 | tf_op jit(solution)/shard_map/ppermute | solution.py:243
  110.8 1.9 collective-permute-start.5
  112.8 1.4 collective-permute-done.4.up
  114.1 6.5 %collective-permute-done.5.down = f32[16,32,128]{2,1,0:T(8,128)S(1)} collective-permute-done((f32[16,32,128]{2,1,0:T(8,128)S(1)}, f32[16,32,128]{2,1,0:T(8,128)S(1)}, u32[]{:S(2)}, u32[]{:S(2)}) %collective-permute-start.5) | collective-permute-done | bytes 262176 | tf_op jit(solution)/shard_map/ppermute | solution.py:243
  120.6 2.1 shard_map.54
  122.7 1.9 collective-permute-start.6
  124.6 2.4 %collective-permute-start.7 = (f32[16,32,128]{2,1,0:T(8,128)S(1)}, f32[16,32,128]{2,1,0:T(8,128)S(1)}, u32[]{:S(2)}, u32[]{:S(2)}) collective-permute-start(f32[16,32,128]{2,1,0:T(8,128)S(1)} %get-tuple-element.29.first), channel_id=1, source_target_pairs={{1,0},{2,1},{3,2},{4,3},{5,4},{6,5},{7,6},{8,7},{9,8},{10,9},{11,1... | collective-permute-start | bytes 786440 | tf_op jit(solution)/shard_map/ppermute | solution.py:243
  127.0 0.9 collective-permute-done.6.up
  127.9 7.7 %collective-permute-done.7.down = f32[16,32,128]{2,1,0:T(8,128)S(1)} collective-permute-done((f32[16,32,128]{2,1,0:T(8,128)S(1)}, f32[16,32,128]{2,1,0:T(8,128)S(1)}, u32[]{:S(2)}, u32[]{:S(2)}) %collective-permute-start.7) | collective-permute-done | bytes 262176 | tf_op jit(solution)/shard_map/ppermute | solution.py:243
  135.6 1.7 shard_map.55.own_ref
  137.3 1.9 collective-permute-start.8
  139.3 11.6 %collective-permute-done.8.nbr_ref = f32[32,32,128]{2,1,0:T(8,128)S(1)} collective-permute-done((f32[32,32,128]{2,1,0:T(8,128)S(1)}, f32[32,32,128]{2,1,0:T(8,128)S(1)}, u32[]{:S(2)}, u32[]{:S(2)}) %collective-permute-start.8) | collective-permute-done | bytes 524320 | tf_op jit(solution)/shard_map/ppermute | solution.py:279
  150.9 0.3 shard_map.56.own_ref
  151.2 1.9 collective-permute-start.9
  153.1 8.0 %collective-permute-done.9.nbr_ref = f32[32,32,128]{2,1,0:T(8,128)S(1)} collective-permute-done((f32[32,32,128]{2,1,0:T(8,128)S(1)}, f32[32,32,128]{2,1,0:T(8,128)S(1)}, u32[]{:S(2)}, u32[]{:S(2)}) %collective-permute-start.9) | collective-permute-done | bytes 524320 | tf_op jit(solution)/shard_map/ppermute | solution.py:284
  161.1 0.5 shard_map.57
  161.6 2.9 %collective-permute-start.10 = (f32[16,32,128]{2,1,0:T(8,128)S(1)}, f32[16,32,128]{2,1,0:T(8,128)S(1)}, u32[]{:S(2)}, u32[]{:S(2)}) collective-permute-start(f32[16,32,128]{2,1,0:T(8,128)S(1)} %get-tuple-element.30.second), channel_id=1, source_target_pairs={{0,1},{1,2},{2,3},{3,4},{4,5},{5,6},{6,7},{7,8},{8,9},{9,10},{10,1... | collective-permute-start | bytes 786440 | tf_op jit(solution)/shard_map/ppermute | solution.py:243
  164.5 1.9 collective-permute-start.11
  166.4 1.4 collective-permute-done.10.up
  167.8 6.8 %collective-permute-done.11.down = f32[16,32,128]{2,1,0:T(8,128)S(1)} collective-permute-done((f32[16,32,128]{2,1,0:T(8,128)S(1)}, f32[16,32,128]{2,1,0:T(8,128)S(1)}, u32[]{:S(2)}, u32[]{:S(2)}) %collective-permute-start.11) | collective-permute-done | bytes 262176 | tf_op jit(solution)/shard_map/ppermute | solution.py:243
  174.6 2.0 shard_map.58
  176.5 35.2 %all_to_all.15.tiles_ref = f32[32,4,8,128]{3,2,1,0:T(8,128)S(1)} all-to-all(f32[32,4,8,128]{3,2,1,0:T(8,128)S(1)} %bitcast.7), channel_id=1, replica_groups=mesh['gz'=32,'gy'=16] {'gz'}, dimensions={0} | all-to-all | bytes 1048576 | tf_op jit(solution)/shard_map/all_to_all | solution.py:246
  211.7 2.3 %shard_map.59 = f32[4,32,1024]{2,1,0:T(8,128)} custom-call(f32[32,4,8,128]{3,2,1,0:T(8,128)S(1)} %all_to_all.15.tiles_ref), custom_call_target="tpu_custom_call" | custom-call | flops 4000000 | bytes 2000000 | tf_op jit(solution)/shard_map/pallas_call | solution.py:27
  (9 shorter events, 0.2 us)
Async XLA Ops:
  0.0 1.0 copy-start
  3.3 18.0 %copy-start.1 = (f32[4,32,1024]{2,1,0:T(8,128)S(1)}, f32[4,32,1024]{2,1,0:T(8,128)}, u32[]{:S(2)}) copy-start(f32[4,32,1024]{2,1,0:T(8,128)} %block_ref.3) | copy-start | bytes 1572868
  3.3 50.1 %all-to-all-start = ((f32[32,4,8,128]{3,2,1,0:T(8,128)}), f32[32,4,8,128]{3,2,1,0:T(8,128)S(1)}, u32[]{:S(2)}, u32[]{:S(2)}) async-start(f32[32,4,8,128]{3,2,1,0:T(8,128)} %shard_map.46), calls=%async_computation | async-start | bytes 1048576 | tf_op jit(solution)/shard_map/all_to_all | solution.py:246
  53.4 38.0 %all-to-all-start.1 = ((f32[32,4,8,128]{3,2,1,0:T(8,128)}), f32[32,4,8,128]{3,2,1,0:T(8,128)S(1)}, u32[]{:S(2)}, u32[]{:S(2)}) async-start(f32[32,4,8,128]{3,2,1,0:T(8,128)} %shard_map.50), calls=%async_computation.1 | async-start | bytes 1048576 | tf_op jit(solution)/shard_map/all_to_all | solution.py:246
  59.3 0.7 copy-start.3
  60.1 0.7 slice-start
  60.8 0.7 copy-start.2
  62.7 6.7 %collective-permute-start = (f32[16,32,128]{2,1,0:T(8,128)S(1)}, f32[16,32,128]{2,1,0:T(8,128)S(1)}, u32[]{:S(2)}, u32[]{:S(2)}) collective-permute-start(f32[16,32,128]{2,1,0:T(8,128)S(1)} %get-tuple-element.20.second), channel_id=1, source_target_pairs={{0,1},{1,2},{2,3},{3,4},{4,5},{5,6},{6,7},{7,8},{8,9},{9,10},{10,1... | collective-permute-start | bytes 786440 | tf_op jit(solution)/shard_map/ppermute | solution.py:243
  65.7 10.4 %collective-permute-start.1 = (f32[16,32,128]{2,1,0:T(8,128)S(1)}, f32[16,32,128]{2,1,0:T(8,128)S(1)}, u32[]{:S(2)}, u32[]{:S(2)}) collective-permute-start(f32[16,32,128]{2,1,0:T(8,128)S(1)} %get-tuple-element.21.first), channel_id=1, source_target_pairs={{1,0},{2,1},{3,2},{4,3},{5,4},{6,5},{7,6},{8,7},{9,8},{10,9},{11,1... | collective-permute-start | bytes 786440 | tf_op jit(solution)/shard_map/ppermute | solution.py:243
  77.8 15.7 %collective-permute-start.2 = (f32[32,32,128]{2,1,0:T(8,128)S(1)}, f32[32,32,128]{2,1,0:T(8,128)S(1)}, u32[]{:S(2)}, u32[]{:S(2)}) collective-permute-start(f32[32,32,128]{2,1,0:T(8,128)S(1)} %shard_map.49.own_ref), channel_id=1, source_target_pairs={{16,0},{497,1},{18,2},{499,3},{20,4},{501,5},{22,6},{503,7},{24,8}... | collective-permute-start | bytes 1572872 | tf_op jit(solution)/shard_map/ppermute | solution.py:279
  93.8 10.2 %collective-permute-start.3 = (f32[32,32,128]{2,1,0:T(8,128)S(1)}, f32[32,32,128]{2,1,0:T(8,128)S(1)}, u32[]{:S(2)}, u32[]{:S(2)}) collective-permute-start(f32[32,32,128]{2,1,0:T(8,128)S(1)} %shard_map.52.own_ref), channel_id=1, source_target_pairs={{496,0},{17,1},{498,2},{19,3},{500,4},{21,5},{502,6},{23,7},{504,8... | collective-permute-start | bytes 1572872 | tf_op jit(solution)/shard_map/ppermute | solution.py:284
  104.6 9.5 %collective-permute-start.4 = (f32[16,32,128]{2,1,0:T(8,128)S(1)}, f32[16,32,128]{2,1,0:T(8,128)S(1)}, u32[]{:S(2)}, u32[]{:S(2)}) collective-permute-start(f32[16,32,128]{2,1,0:T(8,128)S(1)} %get-tuple-element.25.second), channel_id=1, source_target_pairs={{0,1},{1,2},{2,3},{3,4},{4,5},{5,6},{6,7},{7,8},{8,9},{9,10},{10,1... | collective-permute-start | bytes 786440 | tf_op jit(solution)/shard_map/ppermute | solution.py:243
  110.8 9.8 %collective-permute-start.5 = (f32[16,32,128]{2,1,0:T(8,128)S(1)}, f32[16,32,128]{2,1,0:T(8,128)S(1)}, u32[]{:S(2)}, u32[]{:S(2)}) collective-permute-start(f32[16,32,128]{2,1,0:T(8,128)S(1)} %get-tuple-element.26.first), channel_id=1, source_target_pairs={{1,0},{2,1},{3,2},{4,3},{5,4},{6,5},{7,6},{8,7},{9,8},{10,9},{11,1... | collective-permute-start | bytes 786440 | tf_op jit(solution)/shard_map/ppermute | solution.py:243
  122.7 5.2 %collective-permute-start.6 = (f32[16,32,128]{2,1,0:T(8,128)S(1)}, f32[16,32,128]{2,1,0:T(8,128)S(1)}, u32[]{:S(2)}, u32[]{:S(2)}) collective-permute-start(f32[16,32,128]{2,1,0:T(8,128)S(1)} %get-tuple-element.28.second), channel_id=1, source_target_pairs={{0,1},{1,2},{2,3},{3,4},{4,5},{5,6},{6,7},{7,8},{8,9},{9,10},{10,1... | collective-permute-start | bytes 786440 | tf_op jit(solution)/shard_map/ppermute | solution.py:243
  124.6 11.0 %collective-permute-start.7 = (f32[16,32,128]{2,1,0:T(8,128)S(1)}, f32[16,32,128]{2,1,0:T(8,128)S(1)}, u32[]{:S(2)}, u32[]{:S(2)}) collective-permute-start(f32[16,32,128]{2,1,0:T(8,128)S(1)} %get-tuple-element.29.first), channel_id=1, source_target_pairs={{1,0},{2,1},{3,2},{4,3},{5,4},{6,5},{7,6},{8,7},{9,8},{10,9},{11,1... | collective-permute-start | bytes 786440 | tf_op jit(solution)/shard_map/ppermute | solution.py:243
  137.3 13.5 %collective-permute-start.8 = (f32[32,32,128]{2,1,0:T(8,128)S(1)}, f32[32,32,128]{2,1,0:T(8,128)S(1)}, u32[]{:S(2)}, u32[]{:S(2)}) collective-permute-start(f32[32,32,128]{2,1,0:T(8,128)S(1)} %shard_map.55.own_ref), channel_id=1, source_target_pairs={{16,0},{497,1},{18,2},{499,3},{20,4},{501,5},{22,6},{503,7},{24,8}... | collective-permute-start | bytes 1572872 | tf_op jit(solution)/shard_map/ppermute | solution.py:279
  151.2 9.9 %collective-permute-start.9 = (f32[32,32,128]{2,1,0:T(8,128)S(1)}, f32[32,32,128]{2,1,0:T(8,128)S(1)}, u32[]{:S(2)}, u32[]{:S(2)}) collective-permute-start(f32[32,32,128]{2,1,0:T(8,128)S(1)} %shard_map.56.own_ref), channel_id=1, source_target_pairs={{496,0},{17,1},{498,2},{19,3},{500,4},{21,5},{502,6},{23,7},{504,8... | collective-permute-start | bytes 1572872 | tf_op jit(solution)/shard_map/ppermute | solution.py:284
  161.6 6.2 %collective-permute-start.10 = (f32[16,32,128]{2,1,0:T(8,128)S(1)}, f32[16,32,128]{2,1,0:T(8,128)S(1)}, u32[]{:S(2)}, u32[]{:S(2)}) collective-permute-start(f32[16,32,128]{2,1,0:T(8,128)S(1)} %get-tuple-element.30.second), channel_id=1, source_target_pairs={{0,1},{1,2},{2,3},{3,4},{4,5},{5,6},{6,7},{7,8},{8,9},{9,10},{10,1... | collective-permute-start | bytes 786440 | tf_op jit(solution)/shard_map/ppermute | solution.py:243
  164.5 10.1 %collective-permute-start.11 = (f32[16,32,128]{2,1,0:T(8,128)S(1)}, f32[16,32,128]{2,1,0:T(8,128)S(1)}, u32[]{:S(2)}, u32[]{:S(2)}) collective-permute-start(f32[16,32,128]{2,1,0:T(8,128)S(1)} %get-tuple-element.31.first), channel_id=1, source_target_pairs={{1,0},{2,1},{3,2},{4,3},{5,4},{6,5},{7,6},{8,7},{9,8},{10,9},{11,1... | collective-permute-start | bytes 786440 | tf_op jit(solution)/shard_map/ppermute | solution.py:243

commit v2 on v1

v2 whole, which is shorter than its diff:
```python
import functools
import jax
import jax.numpy as jnp
from jax import lax
from jax.experimental import pallas as pl
from jax.experimental.pallas import tpu as pltpu
from jax.sharding import PartitionSpec as P

ITERS = 2
F32 = jnp.float32
BF16 = jnp.bfloat16
H = 15
TAPS = 2 * H + 1
G = 64
T = 32
HALF = T // 2
NX = 1024
TILES = NX // T
NZ = 128
TILE = (T, T, NZ)

VMEM = pl.BlockSpec(memory_space=pltpu.VMEM)
SMEM = pl.BlockSpec(memory_space=pltpu.SMEM)


def call(body, outs, operands, smem=(), flops=4_000_000, moved=2_000_000, scratch=()):
    return pl.pallas_call(
        body,
        out_shape=[jax.ShapeDtypeStruct(s, d) for s, d in outs],
        in_specs=[SMEM if i in smem else VMEM for i in range(len(operands))],
        out_specs=[VMEM] * len(outs),
        scratch_shapes=list(scratch),
        cost_estimate=pl.CostEstimate(flops=flops, bytes_accessed=moved, transcendentals=0),
        compiler_params=pltpu.CompilerParams(vmem_limit_bytes=24 * 1024 * 1024),
    )(*operands)


def split(v):
    hi = v.astype(BF16)
    return hi, (v - hi.astype(F32)).astype(BF16)


def swap_groups(rows):
    lane = lax.broadcasted_iota(jnp.int32, rows[0].shape, 1)
    low64, low32 = lane < 64, (lane & 32) == 0
    a, b, c, d = rows
    a, c = jnp.where(low64, a, pltpu.roll(c, 64, 1)), jnp.where(low64, pltpu.roll(a, 64, 1), c)
    b, d = jnp.where(low64, b, pltpu.roll(d, 64, 1)), jnp.where(low64, pltpu.roll(b, 64, 1), d)
    a, b = jnp.where(low32, a, pltpu.roll(b, 32, 1)), jnp.where(low32, pltpu.roll(a, 96, 1), b)
    c, d = jnp.where(low32, c, pltpu.roll(d, 32, 1)), jnp.where(low32, pltpu.roll(c, 96, 1), d)
    return a, b, c, d


def tiles_of(read, write):
    for th in range(8):
        rows = [read(pl.ds(8 * yh, 8), pl.ds(128 * th, 128)) for yh in range(4)]
        for tl, tile in enumerate(swap_groups(rows)):
            write(4 * th + tl, tile)


def to_tiles_kernel(block_ref, out_ref):
    def write(t, tile):
        out_ref[t, 0] = tile

    tiles_of(lambda rows, lanes: block_ref[0, rows, lanes], write)


def from_tiles_kernel(tiles_ref, out_ref):
    for th in range(8):
        tiles = [tiles_ref[4 * th + tl, 0] for tl in range(4)]
        for yh, row in enumerate(swap_groups(tiles)):
            out_ref[0, pl.ds(8 * yh, 8), pl.ds(128 * th, 128)] = row


def per_plane(body, out_shape, in_block, out_block, operand):
    def spec(block):
        shape, dim = block
        return pl.BlockSpec(shape, lambda z: tuple(z if d == dim else 0 for d in range(len(shape))))

    return pl.pallas_call(
        body,
        grid=(4,),
        out_shape=jax.ShapeDtypeStruct(out_shape, F32),
        in_specs=[spec(in_block)],
        out_specs=spec(out_block),
        cost_estimate=pl.CostEstimate(flops=1_000_000, bytes_accessed=2_000_000, transcendentals=0),
        compiler_params=pltpu.CompilerParams(vmem_limit_bytes=24 * 1024 * 1024),
    )(operand)


def prepare_kernel(
    place_ref, lat_ref, ax_ref, obs_ref, obs_tiles, z_fwd, z_bwd, x_fwd, x_bwd, y_fwd, y_bwd, rolled
):
    tile, side = place_ref[0], place_ref[1]
    for z in range(4):
        rolled[z] = pltpu.roll(obs_ref[z], place_ref[2], 1)

        def write(t, v, z=z):
            obs_tiles[t, z] = v

        tiles_of(lambda rows, lanes, z=z: rolled[z, rows, lanes], write)
    band = pltpu.roll(ax_ref[...], 2 * NZ - G, 1)
    band = band / jnp.sum(band)
    wide = jnp.broadcast_to(band, (NZ, 2 * NZ))
    back = pltpu.roll(wide, 0, 1, stride=1, stride_axis=0)[:, :NZ]
    for m, ref in ((back.T, z_fwd), (back, z_bwd)):
        hi, lo = split(m)
        ref[pl.ds(0, NZ), pl.ds(0, NZ)] = hi
        ref[pl.ds(NZ, NZ), pl.ds(0, NZ)] = hi
        ref[pl.ds(0, NZ), pl.ds(NZ, NZ)] = lo
        ref[pl.ds(NZ, NZ), pl.ds(NZ, NZ)] = jnp.zeros_like(lo)
    total = lat_ref[0]
    for k in range(TAPS):
        tap = jnp.full((8, NZ), lat_ref[k], F32)
        y_fwd[k] = tap
        y_bwd[TAPS - 1 - k] = tap
        if k > 0:
            total = total + lat_ref[k]
    row = lax.broadcasted_iota(jnp.int32, (T, NZ), 0)
    lane = lax.broadcasted_iota(jnp.int32, (T, NZ), 1)
    own, first = lane < 64, (lane & 32) == 0
    col = lane & 31
    here = T * tile
    shifted = here + H * side
    wrap = lambda v: v & (NX - 1)
    src_f = wrap(jnp.where(own, here, here + T * side) + col)
    dst_f = wrap(shifted + row)
    src_b = wrap(jnp.where(own, shifted, shifted - T * side) + col)
    dst_b = wrap(here + row)
    for d, ref in ((src_f - dst_f, x_fwd), (dst_b - src_b, x_bwd)):
        m = jnp.zeros((T, NZ), F32)
        for k in range(TAPS):
            m = jnp.where(d == k - H, lat_ref[k], m)
        scale = jnp.full((T, NZ), total, F32)
        m = m / scale / scale
        hi, lo = split(m)
        ref[pl.ds(0, T), :] = hi
        ref[pl.ds(T, T), :] = jnp.where(first, lo.astype(F32), 0.0).astype(BF16)


def z_pass(v, m):
    r = jnp.dot(jnp.concatenate(split(v), axis=1), m, preferred_element_type=F32)
    return r[:, :NZ] + r[:, NZ:]


def x_pass(own, nbr, m):
    columns = []
    for o, n in zip(own, nbr):
        columns.append(jnp.concatenate([*split(o), *split(n)], axis=0))
    r = jnp.dot(m, jnp.concatenate(columns, axis=1), preferred_element_type=F32)
    r = r[:T] + r[T:]
    return [r[:, NZ * i : NZ * (i + 1)] for i in range(len(own))]


def y_pass(read, rows, taps_ref, emit):
    taps = [taps_ref[k] for k in range(TAPS)]
    for y0 in range(0, rows, 8):
        acc = [None] * 8
        for e in range(8 + TAPS - 1):
            v = read(y0 + e)
            for j in range(max(0, e - TAPS + 1), min(8, e + 1)):
                term = taps[e - j] * v
                acc[j] = term if acc[j] is None else acc[j] + term
        for j in range(8):
            emit(y0 + j, acc[j])


def rows_of(parts, skip, x8):
    sizes = [p.shape[0] for p in parts]

    def read(e):
        e = e + skip
        for part, size in zip(parts, sizes):
            if e < size:
                return part[e, pl.ds(x8, 8), :]
            e -= size

    return read


def each_x8(body):
    @pl.loop(0, T // 8)
    def _(i):
        body(pl.multiple_of(i * 8, 8))


def z_rows(src_ref, m, out_ref):
    for y in range(0, T, 4):
        w = z_pass(jnp.concatenate([src_ref[y + i] for i in range(4)], axis=0), m)
        for i in range(4):
            out_ref[y + i] = w[T * i : T * (i + 1)]


def arrive_kernel(tiles_ref, out_ref):
    for lo in range(8):
        v = tiles_ref[pl.ds(lo, NZ, stride=8), :].T
        for hi in range(4):
            out_ref[8 * hi + lo] = v[T * hi : T * (hi + 1)]


def blur_kernel(taps_ref, up, cur, down, m_ref, out_ref, work):
    def body(x8):
        def emit(y, v):
            work[y, pl.ds(x8, 8), :] = v

        y_pass(rows_of((up, cur, down), 1, x8), T, taps_ref, emit)

    each_x8(body)
    z_rows(work, m_ref[...], out_ref)


def quotient_kernel(own_ref, nbr_ref, obs_ref, m_ref, q_ref):
    m = m_ref[...]
    for y in range(0, T, 2):
        pair = (y, y + 1)
        for i, r in zip(pair, x_pass([own_ref[i] for i in pair], [nbr_ref[i] for i in pair], m)):
            q_ref[i] = obs_ref[i] / r


def back_kernel(own_ref, nbr_ref, mx_ref, mz_ref, out_ref):
    mx, mz = mx_ref[...], mz_ref[...]
    for y in range(0, T, 4):
        rows = []
        for i in (y, y + 2):
            pair = (i, i + 1)
            rows += x_pass([own_ref[k] for k in pair], [nbr_ref[k] for k in pair], mx)
        w = z_pass(jnp.concatenate(rows, axis=0), mz)
        for i in range(4):
            out_ref[y + i] = w[T * i : T * (i + 1)]


def update_kernel(
    back_ref, fwd_ref, up, own, down, cur_up, cur, cur_down, m_ref, new_ref, out_ref, wide, work
):
    def body(x8):
        at = pl.ds(x8, 8)
        before = rows_of((cur_up, cur, cur_down), 0, x8)

        def emit(r, v):
            v = before(r) * v
            wide[r, at, :] = v
            if HALF <= r < HALF + T:
                new_ref[r - HALF, at, :] = v

        y_pass(rows_of((up, own, down), T - HALF - H, x8), 2 * T, back_ref, emit)

        def emit_blur(y, v):
            work[y, at, :] = v

        y_pass(rows_of((wide,), 1, x8), T, fwd_ref, emit_blur)

    each_x8(body)
    z_rows(work, m_ref[...], out_ref)


def leave_kernel(taps_ref, up, own, down, cur_ref, tiles_ref, work):
    def body(x8):
        def emit(y, v):
            work[y, pl.ds(x8, 8), :] = cur_ref[y, pl.ds(x8, 8), :] * v

        y_pass(rows_of((up, own, down), 1, x8), T, taps_ref, emit)

    each_x8(body)
    for lo in range(8):
        v = jnp.concatenate([work[8 * hi + lo] for hi in range(4)], axis=0)
        tiles_ref[pl.ds(lo, NZ, stride=8), :] = v.T


def local(observed, estimate, psf_lateral, psf_axial):
    n_z, n_y = lax.axis_size("gz"), lax.axis_size("gy")
    gz, gy = lax.axis_index("gz").astype(jnp.int32), lax.axis_index("gy").astype(jnp.int32)
    odd = gy % 2 == 1
    side = 1 - 2 * (gy % 2)
    joint = ("gz", "gy")

    def turn(sign):
        pairs = []
        for z in range(n_z):
            for y in range(n_y):
                s = sign * (1 if y % 2 == 0 else -1)
                pairs.append(((z + s) % n_z * n_y + y, z * n_y + y))
        return pairs

    ahead, behind = turn(1), turn(-1)
    outer = [p for i in range(1, n_y - 1, 2) for p in ((i, i + 1), (i + 1, i))]
    inner = [p for i in range(0, n_y, 2) for p in ((i, i + 1), (i + 1, i))]

    def y_swap(to_outer, to_inner):
        from_outer = lax.ppermute(to_outer, "gy", outer)
        from_inner = lax.ppermute(to_inner, "gy", inner)
        return jnp.where(odd, from_inner, from_outer), jnp.where(odd, from_outer, from_inner)

    def y_halves(v):
        first, second = v[:HALF], v[HALF:]
        return y_swap(jnp.where(odd, second, first), jnp.where(odd, first, second))

    def exchange(tiles):
        return lax.all_to_all(tiles, "gz", split_axis=0, concat_axis=0, tiled=True)

    tiles_shape = (TILES, 4, 8, 128)
    flat = (NZ * 8, 128)
    tile_block = ((TILES, 1, 8, 128), 1)
    row_block = ((1, T, NX), 0)
    est_tiles = per_plane(to_tiles_kernel, tiles_shape, row_block, tile_block, estimate)
    place = jnp.stack([gz, side, jnp.where(odd, H, NX - H).astype(jnp.int32)])
    obs_tiles, z_fwd, z_bwd, x_fwd, x_bwd, y_fwd, y_bwd = call(
        prepare_kernel,
        [(tiles_shape, F32)]
        + [((2 * NZ, 2 * NZ), BF16)] * 2
        + [((2 * T, 4 * T), BF16)] * 2
        + [((TAPS, 8, NZ), F32)] * 2,
        [place, psf_lateral, jnp.pad(psf_axial, (0, 2 * NZ - 2 * G - 1)).reshape(1, 2 * NZ), observed],
        smem=(0, 1),
        scratch=[pltpu.VMEM((4, T, NX), F32)],
    )
    est_tiles = exchange(est_tiles)
    obs_tiles = exchange(obs_tiles)
    (current,) = call(arrive_kernel, [(TILE, F32)], [est_tiles.reshape(flat)])
    (obs,) = call(arrive_kernel, [(TILE, F32)], [obs_tiles.reshape(flat)])
    work = pltpu.VMEM(TILE, F32)
    above, below = y_halves(current)
    (own,) = call(
        blur_kernel, [(TILE, F32)], [y_fwd, above, current, below, z_fwd], scratch=[work]
    )
    for step in range(ITERS):
        (own,) = call(
            quotient_kernel, [(TILE, F32)], [own, lax.ppermute(own, joint, ahead), obs, x_fwd]
        )
        (own,) = call(
            back_kernel, [(TILE, F32)], [own, lax.ppermute(own, joint, behind), x_bwd, z_bwd]
        )
        if step < ITERS - 1:
            up, down = y_swap(own, own)
            current, own = call(
                update_kernel,
                [(TILE, F32)] * 2,
                [y_bwd, y_fwd, up, own, down, above, current, below, z_fwd],
                scratch=[pltpu.VMEM((2 * T, T, NZ), F32), work],
            )
        else:
            up, down = y_halves(own)
            (tiles,) = call(
                leave_kernel, [(flat, F32)], [y_bwd, up, own, down, current], scratch=[work]
            )
    tiles = exchange(tiles.reshape(tiles_shape))
    return per_plane(from_tiles_kernel, (4, T, NX), tile_block, row_block, tiles)


def solution(mesh):
    in_specs = (P("gz", "gy", None), P("gz", "gy", None), P(), P())
    out_specs = P("gz", "gy", None)
    return jax.shard_map(local, mesh=mesh, in_specs=in_specs, out_specs=out_specs, check_vma=False)
```

time: 215 us -> 201 us (0.935)
  waiting for transfers between devices: 101 us -> 85.2 us
  blocking collectives: 35.2 us -> 38 us
  Pallas kernels: 17.9 us -> 15.6 us
    ppermute x8 -> x6, waiting for transfers between devices: 33.1 us -> 13 us  [the longest x3 13 us: y_swap(): from_outer = lax.ppermute(to_outer, 'gy', outer)]
    pallas_call x14 -> x10, Pallas kernels: 17.9 us -> 11.8 us  [call(): pl.pallas_call(body, out_shape=[jax.ShapeDtypeStruct(s, d) for s, d in ou...]
    all_to_all x2, waiting for transfers between devices: 39.8 us -> 43.8 us  [exchange(): return lax.all_to_all(tiles, 'gz', split_axis=0, concat_axis=0, tiled=True)]
    pallas_call x0 -> x2, Pallas kernels: none -> 3.77 us  [per_plane(): pl.pallas_call(body, grid=(4,), out_shape=jax.ShapeDtypeStruct(out_shape,...]
    all_to_all x1, blocking collectives: 35.2 us -> 38 us  [exchange(): return lax.all_to_all(tiles, 'gz', split_axis=0, concat_axis=0, tiled=True)]
    ppermute x8 -> x6, starting transfers between devices: 22.1 us -> 23 us  [the longest x3 17.3 us: y_swap(): from_outer = lax.ppermute(to_outer, 'gy', outer)]
  transfers between devices with their start and end apart: 14 -> 12, of which waited for: 14 -> 9; matrix products, arithmetic and copies ran while one was open for 0% -> 0% of each run, Pallas kernels for 3% -> 3%
where the time goes in v2:
time: 201 us; the launch traced here: 199 us
  waiting for transfers between devices  85.2 us (42%)
  starting transfers between devices  57.1 us (28%)
  blocking collectives  38 us (19%)
  Pallas kernels  15.6 us (8%)
  local copies, waits for them, and re-layouts  2.38 us (1%)
    all_to_all x2, waiting for transfers between devices, exchange(): return lax.all_to_all(tiles, 'gz', split_axis=0, concat_axis=0, tiled=True)  43.8 us
    all_to_all x1, blocking collectives, exchange(): return lax.all_to_all(tiles, 'gz', split_axis=0, concat_axis=0, tiled=True)  38 us
    all_to_all x2, starting transfers between devices, exchange(): return lax.all_to_all(tiles, 'gz', split_axis=0, concat_axis=0, tiled=True)  23.8 us
    ppermute x3, starting transfers between devices, y_swap(): from_outer = lax.ppermute(to_outer, 'gy', outer)  17.3 us
    ppermute x2, waiting for transfers between devices, local(): lax.ppermute(own, joint, behind)  15.1 us
    ppermute x2, waiting for transfers between devices, local(): lax.ppermute(own, joint, ahead)  13.3 us
    ppermute x3, waiting for transfers between devices, y_swap(): from_outer = lax.ppermute(to_outer, 'gy', outer)  13 us
    pallas_call x10, Pallas kernels, call(): pl.pallas_call(body, out_shape=[jax.ShapeDtypeStruct(s, d) for s, d in ou...  11.8 us
  transfers between devices with their start and end apart: 12, of which 9 were waited for; matrix products, arithmetic and copies ran while one was open for 0% of the time, Pallas kernels for 3%

profile of v2, /device:TPU:7, one launch (start us, length us, event | category | flops | bytes accessed | tf_op | source)
XLA Modules:
  0.0 198.9 jit_solution(9368987930521441088)
XLA Ops:
  0.0 0.0 copy-start
  0.0 1.0 copy-done
  1.0 1.9 shard_map.47
  2.9 0.0 copy-start.1
  2.9 18.0 %all-to-all-start = ((f32[32,4,8,128]{3,2,1,0:T(8,128)}), f32[32,4,8,128]{3,2,1,0:T(8,128)S(1)}, u32[]{:S(2)}, u32[]{:S(2)}) async-start(f32[32,4,8,128]{3,2,1,0:T(8,128)} %shard_map.47), calls=%async_computation | async-start | bytes 1048576 | tf_op jit(solution)/shard_map/all_to_all | solution.py:298
  20.9 0.0 copy-start.3
  20.9 0.7 copy-done.3
  21.6 0.1 pad_add_fusion.place_ref
  21.7 0.0 copy-start.2
  21.7 0.0 copy-done.1
  21.7 0.7 copy-done.2
  22.3 3.5 %shard_map.46 = (f32[32,4,8,128]{3,2,1,0:T(8,128)}, bf16[256,256]{1,0:T(8,128)(2,1)S(1)}, bf16[256,256]{1,0:T(8,128)(2,1)S(1)}, bf16[64,128]{1,0:T(8,128)(2,1)S(...) custom-call(s32[3]{0:T(128)S(1)} %pad_add_fusion.place_ref, ...), custom_call_target="tpu_custom_call" | custom-call | flops 4000000 | bytes 2000000 | tf_op jit(solution)/shard_map/pallas_call | solution.py:27
  25.8 27.3 %all-to-all-done = f32[32,4,8,128]{3,2,1,0:T(8,128)S(1)} async-done(((f32[32,4,8,128]{3,2,1,0:T(8,128)}), f32[32,4,8,128]{3,2,1,0:T(8,128)S(1)}, u32[]{:S(2)}, u32[]{:S(2)}) %all-to-all-start) | async-done | bytes 524320 | tf_op jit(solution)/shard_map/all_to_all | solution.py:298
  53.0 5.8 %all-to-all-start.1 = ((f32[32,4,8,128]{3,2,1,0:T(8,128)}), f32[32,4,8,128]{3,2,1,0:T(8,128)S(1)}, u32[]{:S(2)}, u32[]{:S(2)}) async-start(f32[32,4,8,128]{3,2,1,0:T(8,128)} %get-tuple-element.17), calls=%async_computation.1 | async-start | bytes 1048576 | tf_op jit(solution)/shard_map/all_to_all | solution.py:298
  58.9 0.2 shard_map.48.cur
  59.1 3.0 %collective-permute-start.1 = (f32[16,32,128]{2,1,0:T(8,128)S(1)}, f32[16,32,128]{2,1,0:T(8,128)S(1)}, u32[]{:S(2)}, u32[]{:S(2)}) collective-permute-start(f32[16,32,128]{2,1,0:T(8,128)S(1)} %get-tuple-element.31), channel_id=1, source_target_pairs={{1,2},{2,1},{3,4},{4,3},{5,6},{6,5},{7,8},{8,7},{9,10},{10,9},{11,... | collective-permute-start | bytes 786440 | tf_op jit(solution)/shard_map/ppermute | solution.py:289
  62.1 1.9 collective-permute-start
  64.0 5.9 %collective-permute-done.1 = f32[16,32,128]{2,1,0:T(8,128)S(1)} collective-permute-done((f32[16,32,128]{2,1,0:T(8,128)S(1)}, f32[16,32,128]{2,1,0:T(8,128)S(1)}, u32[]{:S(2)}, u32[]{:S(2)}) %collective-permute-start.1) | collective-permute-done | bytes 262176 | tf_op jit(solution)/shard_map/ppermute | solution.py:289
  70.0 0.0 collective-permute-done
  70.0 1.5 shard_map.49.own_ref
  71.5 3.0 %collective-permute-start.2 = (f32[32,32,128]{2,1,0:T(8,128)S(1)}, f32[32,32,128]{2,1,0:T(8,128)S(1)}, u32[]{:S(2)}, u32[]{:S(2)}) collective-permute-start(f32[32,32,128]{2,1,0:T(8,128)S(1)} %shard_map.49.own_ref), channel_id=1, source_target_pairs={{16,0},{497,1},{18,2},{499,3},{20,4},{501,5},{22,6},{503,7},{24,8}... | collective-permute-start | bytes 1572872 | tf_op jit(solution)/shard_map/ppermute | solution.py:327
  74.5 16.5 %all-to-all-done.1 = f32[32,4,8,128]{3,2,1,0:T(8,128)S(1)} async-done(((f32[32,4,8,128]{3,2,1,0:T(8,128)}), f32[32,4,8,128]{3,2,1,0:T(8,128)S(1)}, u32[]{:S(2)}, u32[]{:S(2)}) %all-to-all-start.1) | async-done | bytes 524320 | tf_op jit(solution)/shard_map/all_to_all | solution.py:298
  91.1 0.2 shard_map.50.obs_ref
  91.3 1.7 collective-permute-done.2.nbr_ref
  93.0 0.3 shard_map.51.own_ref
  93.3 3.1 %collective-permute-start.3 = (f32[32,32,128]{2,1,0:T(8,128)S(1)}, f32[32,32,128]{2,1,0:T(8,128)S(1)}, u32[]{:S(2)}, u32[]{:S(2)}) collective-permute-start(f32[32,32,128]{2,1,0:T(8,128)S(1)} %shard_map.51.own_ref), channel_id=1, source_target_pairs={{496,0},{17,1},{498,2},{19,3},{500,4},{21,5},{502,6},{23,7},{504,8... | collective-permute-start | bytes 1572872 | tf_op jit(solution)/shard_map/ppermute | solution.py:330
  96.4 7.1 %collective-permute-done.3.nbr_ref = f32[32,32,128]{2,1,0:T(8,128)S(1)} collective-permute-done((f32[32,32,128]{2,1,0:T(8,128)S(1)}, f32[32,32,128]{2,1,0:T(8,128)S(1)}, u32[]{:S(2)}, u32[]{:S(2)}) %collective-permute-start.3) | collective-permute-done | bytes 524320 | tf_op jit(solution)/shard_map/ppermute | solution.py:330
  103.5 0.5 shard_map.52.own
  104.0 6.6 %collective-permute-start.5 = (f32[32,32,128]{2,1,0:T(8,128)S(1)}, f32[32,32,128]{2,1,0:T(8,128)S(1)}, u32[]{:S(2)}, u32[]{:S(2)}) collective-permute-start(f32[32,32,128]{2,1,0:T(8,128)S(1)} %shard_map.52.own), channel_id=1, source_target_pairs={{1,2},{2,1},{3,4},{4,3},{5,6},{6,5},{7,8},{8,7},{9,10},{10,9},{11,... | collective-permute-start | bytes 1572872 | tf_op jit(solution)/shard_map/ppermute | solution.py:289
  110.6 1.9 collective-permute-start.4
  112.5 4.9 %collective-permute-done.5 = f32[32,32,128]{2,1,0:T(8,128)S(1)} collective-permute-done((f32[32,32,128]{2,1,0:T(8,128)S(1)}, f32[32,32,128]{2,1,0:T(8,128)S(1)}, u32[]{:S(2)}, u32[]{:S(2)}) %collective-permute-start.5) | collective-permute-done | bytes 524320 | tf_op jit(solution)/shard_map/ppermute | solution.py:289
  117.4 0.0 collective-permute-done.4
  117.5 0.1 broadcast_select_fusion
  117.6 3.4 %shard_map.53 = (f32[32,32,128]{2,1,0:T(8,128)S(1)}, f32[32,32,128]{2,1,0:T(8,128)S(1)}) custom-call(f32[31,8,128]{2,1,0:T(8,128)S(1)} %get-tuple-element.14.back_ref.taps_ref, f32[31,8,128]{2,1,0:T(8,128)S(1)} %get-tuple-element.15.taps_ref.fwd_ref, f32[32,32,128]{2,1,0:T(8,128)S(1)} %get-tuple-element.24.up, f32[32,32,128]{2,1,0:T(8,128)S(1)} %shard_map.52.own, ...), custom_call_target="tpu_custom_call" | custom-call | flops 4000000 | bytes 2000000 | tf_op jit(solution)/shard_map/pallas_call | solution.py:27
  121.0 1.9 collective-permute-start.6
  122.9 11.6 %collective-permute-done.6.nbr_ref = f32[32,32,128]{2,1,0:T(8,128)S(1)} collective-permute-done((f32[32,32,128]{2,1,0:T(8,128)S(1)}, f32[32,32,128]{2,1,0:T(8,128)S(1)}, u32[]{:S(2)}, u32[]{:S(2)}) %collective-permute-start.6) | collective-permute-done | bytes 524320 | tf_op jit(solution)/shard_map/ppermute | solution.py:327
  134.5 0.3 shard_map.54.own_ref
  134.9 2.3 %collective-permute-start.7 = (f32[32,32,128]{2,1,0:T(8,128)S(1)}, f32[32,32,128]{2,1,0:T(8,128)S(1)}, u32[]{:S(2)}, u32[]{:S(2)}) collective-permute-start(f32[32,32,128]{2,1,0:T(8,128)S(1)} %shard_map.54.own_ref), channel_id=1, source_target_pairs={{496,0},{17,1},{498,2},{19,3},{500,4},{21,5},{502,6},{23,7},{504,8... | collective-permute-start | bytes 1572872 | tf_op jit(solution)/shard_map/ppermute | solution.py:330
  137.1 7.9 %collective-permute-done.7.nbr_ref = f32[32,32,128]{2,1,0:T(8,128)S(1)} collective-permute-done((f32[32,32,128]{2,1,0:T(8,128)S(1)}, f32[32,32,128]{2,1,0:T(8,128)S(1)}, u32[]{:S(2)}, u32[]{:S(2)}) %collective-permute-start.7) | collective-permute-done | bytes 524320 | tf_op jit(solution)/shard_map/ppermute | solution.py:330
  145.1 0.5 shard_map.55.own
  145.7 7.8 %collective-permute-start.9 = (f32[16,32,128]{2,1,0:T(8,128)S(1)}, f32[16,32,128]{2,1,0:T(8,128)S(1)}, u32[]{:S(2)}, u32[]{:S(2)}) collective-permute-start(f32[16,32,128]{2,1,0:T(8,128)S(1)} %get-tuple-element.27), channel_id=1, source_target_pairs={{1,2},{2,1},{3,4},{4,3},{5,6},{6,5},{7,8},{8,7},{9,10},{10,9},{11,... | collective-permute-start | bytes 786440 | tf_op jit(solution)/shard_map/ppermute | solution.py:289
  153.4 1.9 collective-permute-start.8
  155.4 2.1 %collective-permute-done.9 = f32[16,32,128]{2,1,0:T(8,128)S(1)} collective-permute-done((f32[16,32,128]{2,1,0:T(8,128)S(1)}, f32[16,32,128]{2,1,0:T(8,128)S(1)}, u32[]{:S(2)}, u32[]{:S(2)}) %collective-permute-start.9) | collective-permute-done | bytes 262176 | tf_op jit(solution)/shard_map/ppermute | solution.py:289
  157.5 0.0 collective-permute-done.8
  157.5 1.4 shard_map.56
  159.0 38.0 %all_to_all.15.tiles_ref = f32[32,4,8,128]{3,2,1,0:T(8,128)S(1)} all-to-all(f32[32,4,8,128]{3,2,1,0:T(8,128)S(1)} %bitcast.9), channel_id=1, replica_groups=mesh['gz'=32,'gy'=16] {'gz'}, dimensions={0} | all-to-all | bytes 1048576 | tf_op jit(solution)/shard_map/all_to_all | solution.py:298
  197.0 1.9 shard_map.57
  (5 shorter events, 0.2 us)
Async XLA Ops:
  0.0 1.0 copy-start
  2.9 18.8 %copy-start.1 = (f32[4,32,1024]{2,1,0:T(8,128)S(1)}, f32[4,32,1024]{2,1,0:T(8,128)}, u32[]{:S(2)}) copy-start(f32[4,32,1024]{2,1,0:T(8,128)} %obs_ref.1) | copy-start | bytes 1572868
  2.9 50.1 %all-to-all-start = ((f32[32,4,8,128]{3,2,1,0:T(8,128)}), f32[32,4,8,128]{3,2,1,0:T(8,128)S(1)}, u32[]{:S(2)}, u32[]{:S(2)}) async-start(f32[32,4,8,128]{3,2,1,0:T(8,128)} %shard_map.47), calls=%async_computation | async-start | bytes 1048576 | tf_op jit(solution)/shard_map/all_to_all | solution.py:298
  20.9 0.7 copy-start.3
  21.7 0.7 copy-start.2
  53.0 38.0 %all-to-all-start.1 = ((f32[32,4,8,128]{3,2,1,0:T(8,128)}), f32[32,4,8,128]{3,2,1,0:T(8,128)S(1)}, u32[]{:S(2)}, u32[]{:S(2)}) async-start(f32[32,4,8,128]{3,2,1,0:T(8,128)} %get-tuple-element.17), calls=%async_computation.1 | async-start | bytes 1048576 | tf_op jit(solution)/shard_map/all_to_all | solution.py:298
  59.1 10.8 %collective-permute-start.1 = (f32[16,32,128]{2,1,0:T(8,128)S(1)}, f32[16,32,128]{2,1,0:T(8,128)S(1)}, u32[]{:S(2)}, u32[]{:S(2)}) collective-permute-start(f32[16,32,128]{2,1,0:T(8,128)S(1)} %get-tuple-element.31), channel_id=1, source_target_pairs={{1,2},{2,1},{3,4},{4,3},{5,6},{6,5},{7,8},{8,7},{9,10},{10,9},{11,... | collective-permute-start | bytes 786440 | tf_op jit(solution)/shard_map/ppermute | solution.py:289
  62.1 7.9 %collective-permute-start = (f32[16,32,128]{2,1,0:T(8,128)S(1)}, f32[16,32,128]{2,1,0:T(8,128)S(1)}, u32[]{:S(2)}, u32[]{:S(2)}) collective-permute-start(f32[16,32,128]{2,1,0:T(8,128)S(1)} %get-tuple-element.32), channel_id=1, source_target_pairs={{0,1},{1,0},{2,3},{3,2},{4,5},{5,4},{6,7},{7,6},{8,9},{9,8},{10,11... | collective-permute-start | bytes 786440 | tf_op jit(solution)/shard_map/ppermute | solution.py:290
  71.5 21.5 %collective-permute-start.2 = (f32[32,32,128]{2,1,0:T(8,128)S(1)}, f32[32,32,128]{2,1,0:T(8,128)S(1)}, u32[]{:S(2)}, u32[]{:S(2)}) collective-permute-start(f32[32,32,128]{2,1,0:T(8,128)S(1)} %shard_map.49.own_ref), channel_id=1, source_target_pairs={{16,0},{497,1},{18,2},{499,3},{20,4},{501,5},{22,6},{503,7},{24,8}... | collective-permute-start | bytes 1572872 | tf_op jit(solution)/shard_map/ppermute | solution.py:327
  93.3 10.2 %collective-permute-start.3 = (f32[32,32,128]{2,1,0:T(8,128)S(1)}, f32[32,32,128]{2,1,0:T(8,128)S(1)}, u32[]{:S(2)}, u32[]{:S(2)}) collective-permute-start(f32[32,32,128]{2,1,0:T(8,128)S(1)} %shard_map.51.own_ref), channel_id=1, source_target_pairs={{496,0},{17,1},{498,2},{19,3},{500,4},{21,5},{502,6},{23,7},{504,8... | collective-permute-start | bytes 1572872 | tf_op jit(solution)/shard_map/ppermute | solution.py:330
  104.0 13.4 %collective-permute-start.5 = (f32[32,32,128]{2,1,0:T(8,128)S(1)}, f32[32,32,128]{2,1,0:T(8,128)S(1)}, u32[]{:S(2)}, u32[]{:S(2)}) collective-permute-start(f32[32,32,128]{2,1,0:T(8,128)S(1)} %shard_map.52.own), channel_id=1, source_target_pairs={{1,2},{2,1},{3,4},{4,3},{5,6},{6,5},{7,8},{8,7},{9,10},{10,9},{11,... | collective-permute-start | bytes 1572872 | tf_op jit(solution)/shard_map/ppermute | solution.py:289
  110.6 6.9 %collective-permute-start.4 = (f32[32,32,128]{2,1,0:T(8,128)S(1)}, f32[32,32,128]{2,1,0:T(8,128)S(1)}, u32[]{:S(2)}, u32[]{:S(2)}) collective-permute-start(f32[32,32,128]{2,1,0:T(8,128)S(1)} %shard_map.52.own), channel_id=1, source_target_pairs={{0,1},{1,0},{2,3},{3,2},{4,5},{5,4},{6,7},{7,6},{8,9},{9,8},{10,11... | collective-permute-start | bytes 1572872 | tf_op jit(solution)/shard_map/ppermute | solution.py:290
  121.0 13.5 %collective-permute-start.6 = (f32[32,32,128]{2,1,0:T(8,128)S(1)}, f32[32,32,128]{2,1,0:T(8,128)S(1)}, u32[]{:S(2)}, u32[]{:S(2)}) collective-permute-start(f32[32,32,128]{2,1,0:T(8,128)S(1)} %get-tuple-element.21.own_ref), channel_id=1, source_target_pairs={{16,0},{497,1},{18,2},{499,3},{20,4},{501,5},{22,6},{503,7},{24,8}... | collective-permute-start | bytes 1572872 | tf_op jit(solution)/shard_map/ppermute | solution.py:327
  134.9 10.2 %collective-permute-start.7 = (f32[32,32,128]{2,1,0:T(8,128)S(1)}, f32[32,32,128]{2,1,0:T(8,128)S(1)}, u32[]{:S(2)}, u32[]{:S(2)}) collective-permute-start(f32[32,32,128]{2,1,0:T(8,128)S(1)} %shard_map.54.own_ref), channel_id=1, source_target_pairs={{496,0},{17,1},{498,2},{19,3},{500,4},{21,5},{502,6},{23,7},{504,8... | collective-permute-start | bytes 1572872 | tf_op jit(solution)/shard_map/ppermute | solution.py:330
  145.7 11.8 %collective-permute-start.9 = (f32[16,32,128]{2,1,0:T(8,128)S(1)}, f32[16,32,128]{2,1,0:T(8,128)S(1)}, u32[]{:S(2)}, u32[]{:S(2)}) collective-permute-start(f32[16,32,128]{2,1,0:T(8,128)S(1)} %get-tuple-element.27), channel_id=1, source_target_pairs={{1,2},{2,1},{3,4},{4,3},{5,6},{6,5},{7,8},{8,7},{9,10},{10,9},{11,... | collective-permute-start | bytes 786440 | tf_op jit(solution)/shard_map/ppermute | solution.py:289
  153.4 4.0 %collective-permute-start.8 = (f32[16,32,128]{2,1,0:T(8,128)S(1)}, f32[16,32,128]{2,1,0:T(8,128)S(1)}, u32[]{:S(2)}, u32[]{:S(2)}) collective-permute-start(f32[16,32,128]{2,1,0:T(8,128)S(1)} %get-tuple-element.28), channel_id=1, source_target_pairs={{0,1},{1,0},{2,3},{3,2},{4,5},{5,4},{6,7},{7,6},{8,9},{9,8},{10,11... | collective-permute-start | bytes 786440 | tf_op jit(solution)/shard_map/ppermute | solution.py:290

commit v3 on v2

--- a/solution.py
+++ b/solution.py
@@ -17,7 +17,6 @@
 NX = 1024
 TILES = NX // T
 NZ = 128
-TILE = (T, T, NZ)
 
 VMEM = pl.BlockSpec(memory_space=pltpu.VMEM)
 SMEM = pl.BlockSpec(memory_space=pltpu.SMEM)
@@ -58,11 +57,23 @@
             write(4 * th + tl, tile)
 
 
-def to_tiles_kernel(block_ref, out_ref):
-    def write(t, tile):
-        out_ref[t, 0] = tile
-
-    tiles_of(lambda rows, lanes: block_ref[0, rows, lanes], write)
+def depart_kernel(block_hbm, tiles_hbm, block, tiles, in_sems, out_sems):
+    copies = [pltpu.make_async_copy(block_hbm.at[z], block.at[z], in_sems.at[z]) for z in range(4)]
+    for c in copies:
+        c.start()
+    sent = []
+    for z in range(4):
+        copies[z].wait()
+        for th in range(8):
+            rows = [block[z, pl.ds(8 * yh, 8), pl.ds(128 * th, 128)] for yh in range(4)]
+            for tl, tile in enumerate(swap_groups(rows)):
+                tiles[4 * th + tl, z] = tile
+            if z == 3 and th % 2 == 1:
+                group = pl.ds(4 * (th - 1), 8)
+                sent.append(pltpu.make_async_copy(tiles.at[group], tiles_hbm.at[group], out_sems.at[th // 2]))
+                sent[-1].start()
+    for c in sent:
+        c.wait()
 
 
 def from_tiles_kernel(tiles_ref, out_ref):
@@ -89,7 +100,7 @@
 
 
 def prepare_kernel(
-    place_ref, lat_ref, ax_ref, obs_ref, obs_tiles, z_fwd, z_bwd, x_fwd, x_bwd, y_fwd, y_bwd, rolled
+    place_ref, lat_ref, ax_ref, obs_ref, obs_tiles, z_fwd, z_bwd, x_fwd, x_bwd, y_fwd, y_bwd, y_wide, rolled
 ):
     tile, side = place_ref[0], place_ref[1]
     for z in range(4):
@@ -110,12 +121,19 @@
         ref[pl.ds(0, NZ), pl.ds(NZ, NZ)] = lo
         ref[pl.ds(NZ, NZ), pl.ds(NZ, NZ)] = jnp.zeros_like(lo)
     total = lat_ref[0]
-    for k in range(TAPS):
-        tap = jnp.full((8, NZ), lat_ref[k], F32)
-        y_fwd[k] = tap
-        y_bwd[TAPS - 1 - k] = tap
-        if k > 0:
-            total = total + lat_ref[k]
+    for k in range(1, TAPS):
+        total = total + lat_ref[k]
+    for flip, outs, ins, ref in ((0, T, 2 * T, y_fwd), (1, T, 2 * T, y_bwd), (1, 2 * T, 3 * T, y_wide)):
+        row = lax.broadcasted_iota(jnp.int32, (outs, 2 * NZ), 0)
+        lane = lax.broadcasted_iota(jnp.int32, (outs, 2 * NZ), 1)
+        high = lane < ins
+        d = jnp.where(high, lane, lane - ins) - row - 1
+        m = jnp.zeros((outs, 2 * NZ), F32)
+        for k in range(TAPS):
+            m = jnp.where(d == k, lat_ref[TAPS - 1 - k if flip else k], m)
+        hi, lo = split(m)
+        ref[pl.ds(0, outs), :] = hi[:, : 2 * ins]
+        ref[pl.ds(outs, outs), :] = jnp.where(high, lo.astype(F32), 0.0).astype(BF16)[:, : 2 * ins]
     row = lax.broadcasted_iota(jnp.int32, (T, NZ), 0)
     lane = lax.broadcasted_iota(jnp.int32, (T, NZ), 1)
     own, first = lane < 64, (lane & 32) == 0
@@ -152,118 +170,110 @@
     return [r[:, NZ * i : NZ * (i + 1)] for i in range(len(own))]
 
 
-def y_pass(read, rows, taps_ref, emit):
-    taps = [taps_ref[k] for k in range(TAPS)]
-    for y0 in range(0, rows, 8):
-        acc = [None] * 8
-        for e in range(8 + TAPS - 1):
-            v = read(y0 + e)
-            for j in range(max(0, e - TAPS + 1), min(8, e + 1)):
-                term = taps[e - j] * v
-                acc[j] = term if acc[j] is None else acc[j] + term
-        for j in range(8):
-            emit(y0 + j, acc[j])
-
-
-def rows_of(parts, skip, x8):
-    sizes = [p.shape[0] for p in parts]
-
-    def read(e):
-        e = e + skip
-        for part, size in zip(parts, sizes):
-            if e < size:
-                return part[e, pl.ds(x8, 8), :]
-            e -= size
-
-    return read
-
-
-def each_x8(body):
-    @pl.loop(0, T // 8)
-    def _(i):
-        body(pl.multiple_of(i * 8, 8))
-
-
-def z_rows(src_ref, m, out_ref):
-    for y in range(0, T, 4):
-        w = z_pass(jnp.concatenate([src_ref[y + i] for i in range(4)], axis=0), m)
-        for i in range(4):
-            out_ref[y + i] = w[T * i : T * (i + 1)]
-
-
-def arrive_kernel(tiles_ref, out_ref):
+def y_pass(columns, m):
+    outs = m.shape[0] // 2
+    stacked = [jnp.concatenate(split(c), axis=0) for c in columns]
+    r = jnp.dot(m, jnp.concatenate(stacked, axis=1), preferred_element_type=F32)
+    return r[:outs] + r[outs:]
+
+
+def part(ref, i, n):
+    return ref[pl.ds(i * n, n), :]
+
+
+def put_across(ref, i, v):
+    ref[pl.ds(i, T, stride=T), :] = v
+
+
+def arrive_xy_kernel(tiles_ref, out_ref):
     for lo in range(8):
         v = tiles_ref[pl.ds(lo, NZ, stride=8), :].T
         for hi in range(4):
-            out_ref[8 * hi + lo] = v[T * hi : T * (hi + 1)]
-
-
-def blur_kernel(taps_ref, up, cur, down, m_ref, out_ref, work):
-    def body(x8):
-        def emit(y, v):
-            work[y, pl.ds(x8, 8), :] = v
-
-        y_pass(rows_of((up, cur, down), 1, x8), T, taps_ref, emit)
-
-    each_x8(body)
-    z_rows(work, m_ref[...], out_ref)
-
-
-def quotient_kernel(own_ref, nbr_ref, obs_ref, m_ref, q_ref):
+            put_across(out_ref, 8 * hi + lo, v[T * hi : T * (hi + 1)])
+
+
+def arrive_yx_kernel(tiles_ref, out_ref):
+    for lo in range(8):
+        v = tiles_ref[pl.ds(lo, NZ, stride=8), :].T
+        for hi in range(4):
+            out_ref[pl.ds(T * (8 * hi + lo), T), :] = v[T * hi : T * (hi + 1)]
+
+
+def blur_kernel(my_ref, mz_ref, up, cur, down, out_ref):
+    my, mz = my_ref[...], mz_ref[...]
+    for x in range(0, T, 4):
+        rows = []
+        for i in (x, x + 2):
+            columns = [
+                jnp.concatenate([part(up, k, HALF), part(cur, k, T), part(down, k, HALF)], axis=0)
+                for k in (i, i + 1)
+            ]
+            r = y_pass(columns, my)
+            rows += [r[:, :NZ], r[:, NZ:]]
+        w = z_pass(jnp.concatenate(rows, axis=0), mz)
+        for i in range(4):
+            put_across(out_ref, x + i, w[T * i : T * (i + 1)])
+
+
+def quotient_kernel(m_ref, own_ref, nbr_ref, obs_ref, q_ref):
     m = m_ref[...]
     for y in range(0, T, 2):
         pair = (y, y + 1)
-        for i, r in zip(pair, x_pass([own_ref[i] for i in pair], [nbr_ref[i] for i in pair], m)):
-            q_ref[i] = obs_ref[i] / r
-
-
-def back_kernel(own_ref, nbr_ref, mx_ref, mz_ref, out_ref):
+        blurred = x_pass([part(own_ref, k, T) for k in pair], [part(nbr_ref, k, T) for k in pair], m)
+        for k, b in zip(pair, blurred):
+            q_ref[pl.ds(k * T, T), :] = part(obs_ref, k, T) / b
+
+
+def back_kernel(mx_ref, mz_ref, own_ref, nbr_ref, out_ref):
     mx, mz = mx_ref[...], mz_ref[...]
     for y in range(0, T, 4):
         rows = []
         for i in (y, y + 2):
             pair = (i, i + 1)
-            rows += x_pass([own_ref[k] for k in pair], [nbr_ref[k] for k in pair], mx)
+            rows += x_pass([part(own_ref, k, T) for k in pair], [part(nbr_ref, k, T) for k in pair], mx)
         w = z_pass(jnp.concatenate(rows, axis=0), mz)
         for i in range(4):
-            out_ref[y + i] = w[T * i : T * (i + 1)]
+            put_across(out_ref, y + i, w[T * i : T * (i + 1)])
 
 
 def update_kernel(
-    back_ref, fwd_ref, up, own, down, cur_up, cur, cur_down, m_ref, new_ref, out_ref, wide, work
+    back_ref, fwd_ref, mz_ref, up, own, down, cur_up, cur, cur_down, new_ref, out_ref
 ):
-    def body(x8):
-        at = pl.ds(x8, 8)
-        before = rows_of((cur_up, cur, cur_down), 0, x8)
-
-        def emit(r, v):
-            v = before(r) * v
-            wide[r, at, :] = v
-            if HALF <= r < HALF + T:
-                new_ref[r - HALF, at, :] = v
-
-        y_pass(rows_of((up, own, down), T - HALF - H, x8), 2 * T, back_ref, emit)
-
-        def emit_blur(y, v):
-            work[y, at, :] = v
-
-        y_pass(rows_of((wide,), 1, x8), T, fwd_ref, emit_blur)
-
-    each_x8(body)
-    z_rows(work, m_ref[...], out_ref)
-
-
-def leave_kernel(taps_ref, up, own, down, cur_ref, tiles_ref, work):
-    def body(x8):
-        def emit(y, v):
-            work[y, pl.ds(x8, 8), :] = cur_ref[y, pl.ds(x8, 8), :] * v
-
-        y_pass(rows_of((up, own, down), 1, x8), T, taps_ref, emit)
-
-    each_x8(body)
+    back, fwd, mz = back_ref[...], fwd_ref[...], mz_ref[...]
+    for x in range(0, T, 4):
+        rows = []
+        for i in (x, x + 2):
+            pair = (i, i + 1)
+            r = y_pass([jnp.concatenate([part(p, k, T) for p in (up, own, down)], axis=0) for k in pair], back)
+            wide = []
+            for n, k in enumerate(pair):
+                old = jnp.concatenate(
+                    [part(cur_up, k, HALF), part(cur, k, T), part(cur_down, k, HALF)], axis=0
+                )
+                new = old * r[:, NZ * n : NZ * (n + 1)]
+                new_ref[pl.ds(k * T, T), :] = new[HALF : HALF + T]
+                wide.append(new)
+            r = y_pass(wide, fwd)
+            rows += [r[:, :NZ], r[:, NZ:]]
+        w = z_pass(jnp.concatenate(rows, axis=0), mz)
+        for i in range(4):
+            put_across(out_ref, x + i, w[T * i : T * (i + 1)])
+
+
+def leave_kernel(m_ref, up, own, down, cur_ref, tiles_ref, work):
+    m = m_ref[...]
+    for x in range(0, T, 2):
+        pair = (x, x + 1)
+        columns = [
+            jnp.concatenate([part(up, k, HALF), part(own, k, T), part(down, k, HALF)], axis=0)
+            for k in pair
+        ]
+        r = y_pass(columns, m)
+        for n, k in enumerate(pair):
+            work[pl.ds(k * T, T), :] = part(cur_ref, k, T) * r[:, NZ * n : NZ * (n + 1)]
     for lo in range(8):
-        v = jnp.concatenate([work[8 * hi + lo] for hi in range(4)], axis=0)
-        tiles_ref[pl.ds(lo, NZ, stride=8), :] = v.T
+        v = [work[pl.ds(8 * hi + lo, T, stride=T), :] for hi in range(4)]
+        tiles_ref[pl.ds(lo, NZ, stride=8), :] = jnp.concatenate(v, axis=0).T
 
 
 def local(observed, estimate, psf_lateral, psf_axial):
@@ -291,59 +301,65 @@
         return jnp.where(odd, from_inner, from_outer), jnp.where(odd, from_outer, from_inner)
 
     def y_halves(v):
-        first, second = v[:HALF], v[HALF:]
-        return y_swap(jnp.where(odd, second, first), jnp.where(odd, first, second))
+        v = v.reshape(T, T, NZ)
+        first, second = v[:, :HALF], v[:, HALF:]
+        swapped = y_swap(jnp.where(odd, second, first), jnp.where(odd, first, second))
+        return [h.reshape(T * HALF, NZ) for h in swapped]
 
     def exchange(tiles):
         return lax.all_to_all(tiles, "gz", split_axis=0, concat_axis=0, tiled=True)
 
     tiles_shape = (TILES, 4, 8, 128)
     flat = (NZ * 8, 128)
-    tile_block = ((TILES, 1, 8, 128), 1)
-    row_block = ((1, T, NX), 0)
-    est_tiles = per_plane(to_tiles_kernel, tiles_shape, row_block, tile_block, estimate)
+    block_shape = (4, T, NX)
+    dma = lambda n: pltpu.SemaphoreType.DMA((n,))
+    est_tiles = pl.pallas_call(
+        depart_kernel,
+        out_shape=jax.ShapeDtypeStruct(tiles_shape, F32),
+        in_specs=[pl.BlockSpec(memory_space=pl.ANY)],
+        out_specs=pl.BlockSpec(memory_space=pl.ANY),
+        scratch_shapes=[pltpu.VMEM(block_shape, F32), pltpu.VMEM(tiles_shape, F32), dma(4), dma(4)],
+        cost_estimate=pl.CostEstimate(flops=1_000_000, bytes_accessed=2_000_000, transcendentals=0),
+        compiler_params=pltpu.CompilerParams(vmem_limit_bytes=60 * 1024 * 1024),
+    )(estimate)
     place = jnp.stack([gz, side, jnp.where(odd, H, NX - H).astype(jnp.int32)])
-    obs_tiles, z_fwd, z_bwd, x_fwd, x_bwd, y_fwd, y_bwd = call(
+    obs_tiles, z_fwd, z_bwd, x_fwd, x_bwd, y_fwd, y_bwd, y_wide = call(
         prepare_kernel,
         [(tiles_shape, F32)]
         + [((2 * NZ, 2 * NZ), BF16)] * 2
         + [((2 * T, 4 * T), BF16)] * 2
-        + [((TAPS, 8, NZ), F32)] * 2,
+        + [((2 * T, 4 * T), BF16)] * 2
+        + [((4 * T, 6 * T), BF16)],
         [place, psf_lateral, jnp.pad(psf_axial, (0, 2 * NZ - 2 * G - 1)).reshape(1, 2 * NZ), observed],
         smem=(0, 1),
         scratch=[pltpu.VMEM((4, T, NX), F32)],
     )
     est_tiles = exchange(est_tiles)
     obs_tiles = exchange(obs_tiles)
-    (current,) = call(arrive_kernel, [(TILE, F32)], [est_tiles.reshape(flat)])
-    (obs,) = call(arrive_kernel, [(TILE, F32)], [obs_tiles.reshape(flat)])
-    work = pltpu.VMEM(TILE, F32)
+    whole = [(flat, F32)]
+    (current,) = call(arrive_xy_kernel, whole, [est_tiles.reshape(flat)])
+    (obs,) = call(arrive_yx_kernel, whole, [obs_tiles.reshape(flat)])
     above, below = y_halves(current)
-    (own,) = call(
-        blur_kernel, [(TILE, F32)], [y_fwd, above, current, below, z_fwd], scratch=[work]
-    )
+    (own,) = call(blur_kernel, whole, [y_fwd, z_fwd, above, current, below])
     for step in range(ITERS):
-        (own,) = call(
-            quotient_kernel, [(TILE, F32)], [own, lax.ppermute(own, joint, ahead), obs, x_fwd]
-        )
-        (own,) = call(
-            back_kernel, [(TILE, F32)], [own, lax.ppermute(own, joint, behind), x_bwd, z_bwd]
-        )
+        (own,) = call(quotient_kernel, whole, [x_fwd, own, lax.ppermute(own, joint, ahead), obs])
+        (own,) = call(back_kernel, whole, [x_bwd, z_bwd, own, lax.ppermute(own, joint, behind)])
         if step < ITERS - 1:
             up, down = y_swap(own, own)
             current, own = call(
                 update_kernel,
-                [(TILE, F32)] * 2,
-                [y_bwd, y_fwd, up, own, down, above, current, below, z_fwd],
-                scratch=[pltpu.VMEM((2 * T, T, NZ), F32), work],
+                whole * 2,
+                [y_wide, y_fwd, z_fwd, up, own, down, above, current, below],
             )
         else:
             up, down = y_halves(own)
             (tiles,) = call(
-                leave_kernel, [(flat, F32)], [y_bwd, up, own, down, current], scratch=[work]
+                leave_kernel, whole, [y_bwd, up, own, down, current], scratch=[pltpu.VMEM(flat, F32)]
             )
     tiles = exchange(tiles.reshape(tiles_shape))
-    return per_plane(from_tiles_kernel, (4, T, NX), tile_block, row_block, tiles)
+    tile_block = ((TILES, 1, 8, 128), 1)
+    row_block = ((1, T, NX), 0)
+    return per_plane(from_tiles_kernel, block_shape, tile_block, row_block, tiles)
 
 
 def solution(mesh):

time: 201 us -> 199 us (0.990)
    pallas_call x0 -> x1, Pallas kernels: none -> 2.44 us  [local(): pl.pallas_call(depart_kernel, out_shape=jax.ShapeDtypeStruct(tiles_shape,...]
where the time goes in v3:
time: 199 us; the launch traced here: 197 us
  waiting for transfers between devices  85.3 us (43%)
  starting transfers between devices  57.2 us (29%)
  blocking collectives  38 us (19%)
  Pallas kernels  14.8 us (7%)
    all_to_all x2, waiting for transfers between devices, exchange(): return lax.all_to_all(tiles, 'gz', split_axis=0, concat_axis=0, tiled=True)  43.9 us
    all_to_all x1, blocking collectives, exchange(): return lax.all_to_all(tiles, 'gz', split_axis=0, concat_axis=0, tiled=True)  38 us
    all_to_all x2, starting transfers between devices, exchange(): return lax.all_to_all(tiles, 'gz', split_axis=0, concat_axis=0, tiled=True)  23.8 us
    ppermute x3, starting transfers between devices, y_swap(): from_outer = lax.ppermute(to_outer, 'gy', outer)  17.3 us
    ppermute x2, waiting for transfers between devices, local(): lax.ppermute(own, joint, behind)  15.1 us
    ppermute x2, waiting for transfers between devices, local(): lax.ppermute(own, joint, ahead)  13.3 us
    ppermute x3, waiting for transfers between devices, y_swap(): from_outer = lax.ppermute(to_outer, 'gy', outer)  12.9 us
    pallas_call x10, Pallas kernels, call(): pl.pallas_call(body, out_shape=[jax.ShapeDtypeStruct(s, d) for s, d in ou...  10.4 us
  transfers between devices with their start and end apart: 12, of which 9 were waited for; matrix products, arithmetic and copies ran while one was open for 0% of the time, Pallas kernels for 3%

profile of v3, /device:TPU:7, one launch (start us, length us, event | category | flops | bytes accessed | tf_op | source)
XLA Modules:
  0.0 197.2 jit_solution(5709637925668128943)
XLA Ops:
  0.0 2.4 %shard_map.47 = f32[32,4,8,128]{3,2,1,0:T(8,128)} custom-call(f32[4,32,1024]{2,1,0:T(8,128)} %block_hbm.1), custom_call_target="tpu_custom_call" | custom-call | flops 1000000 | bytes 2000000 | tf_op jit(solution)/shard_map/pallas_call | solution.py:316
  2.4 0.0 copy-start
  2.5 18.0 %all-to-all-start = ((f32[32,4,8,128]{3,2,1,0:T(8,128)}), f32[32,4,8,128]{3,2,1,0:T(8,128)S(1)}, u32[]{:S(2)}, u32[]{:S(2)}) async-start(f32[32,4,8,128]{3,2,1,0:T(8,128)} %shard_map.47), calls=%async_computation | async-start | bytes 1048576 | tf_op jit(solution)/shard_map/all_to_all | solution.py:310
  20.5 0.0 copy-start.2
  20.5 0.7 copy-done.2
  21.1 0.1 pad_add_fusion.place_ref
  21.2 0.0 copy-start.1
  21.2 0.0 copy-done
  21.2 0.7 copy-done.1
  21.9 3.7 %shard_map.46 = (f32[32,4,8,128]{3,2,1,0:T(8,128)}, bf16[256,256]{1,0:T(8,128)(2,1)S(1)}, bf16[256,256]{1,0:T(8,128)(2,1)S(1)}, bf16[64,128]{1,0:T(8,128)(2,1)S(...) custom-call(s32[3]{0:T(128)S(1)} %pad_add_fusion.place_ref, ...), custom_call_target="tpu_custom_call" | custom-call | flops 4000000 | bytes 2000000 | tf_op jit(solution)/shard_map/pallas_call | solution.py:26
  25.6 27.0 %all-to-all-done = f32[32,4,8,128]{3,2,1,0:T(8,128)S(1)} async-done(((f32[32,4,8,128]{3,2,1,0:T(8,128)}), f32[32,4,8,128]{3,2,1,0:T(8,128)S(1)}, u32[]{:S(2)}, u32[]{:S(2)}) %all-to-all-start) | async-done | bytes 524320 | tf_op jit(solution)/shard_map/all_to_all | solution.py:310
  52.6 5.8 %all-to-all-start.1 = ((f32[32,4,8,128]{3,2,1,0:T(8,128)}), f32[32,4,8,128]{3,2,1,0:T(8,128)S(1)}, u32[]{:S(2)}, u32[]{:S(2)}) async-start(f32[32,4,8,128]{3,2,1,0:T(8,128)} %get-tuple-element.22), calls=%async_computation.1 | async-start | bytes 1048576 | tf_op jit(solution)/shard_map/all_to_all | solution.py:310
  58.5 0.4 shard_map.48.cur
  58.9 3.0 %collective-permute-start.1 = (f32[32,16,128]{2,1,0:T(8,128)S(1)}, f32[32,16,128]{2,1,0:T(8,128)S(1)}, u32[]{:S(2)}, u32[]{:S(2)}) collective-permute-start(f32[32,16,128]{2,1,0:T(8,128)S(1)} %get-tuple-element.33), channel_id=1, source_target_pairs={{1,2},{2,1},{3,4},{4,3},{5,6},{6,5},{7,8},{8,7},{9,10},{10,9},{11,... | collective-permute-start | bytes 786440 | tf_op jit(solution)/shard_map/ppermute | solution.py:299
  61.9 1.9 collective-permute-start
  63.8 5.9 %collective-permute-done.1 = f32[32,16,128]{2,1,0:T(8,128)S(1)} collective-permute-done((f32[32,16,128]{2,1,0:T(8,128)S(1)}, f32[32,16,128]{2,1,0:T(8,128)S(1)}, u32[]{:S(2)}, u32[]{:S(2)}) %collective-permute-start.1) | collective-permute-done | bytes 262176 | tf_op jit(solution)/shard_map/ppermute | solution.py:299
  69.7 0.0 collective-permute-done
  69.8 0.8 shard_map.49.own_ref
  70.6 3.1 %collective-permute-start.2 = (f32[1024,128]{1,0:T(8,128)S(1)}, f32[1024,128]{1,0:T(8,128)S(1)}, u32[]{:S(2)}, u32[]{:S(2)}) collective-permute-start(f32[1024,128]{1,0:T(8,128)S(1)} %shard_map.49.own_ref), channel_id=1, source_target_pairs={{16,0},{497,1},{18,2},{499,3},{20,4},{501,5},{22,6},{503,7},{24,8}... | collective-permute-start | bytes 1572872 | tf_op jit(solution)/shard_map/ppermute | solution.py:345
  73.8 16.8 %all-to-all-done.1 = f32[32,4,8,128]{3,2,1,0:T(8,128)S(1)} async-done(((f32[32,4,8,128]{3,2,1,0:T(8,128)}), f32[32,4,8,128]{3,2,1,0:T(8,128)S(1)}, u32[]{:S(2)}, u32[]{:S(2)}) %all-to-all-start.1) | async-done | bytes 524320 | tf_op jit(solution)/shard_map/all_to_all | solution.py:310
  90.6 0.2 shard_map.50.obs_ref
  90.8 1.7 collective-permute-done.2.nbr_ref
  92.5 0.3 shard_map.51.own_ref
  92.8 3.1 %collective-permute-start.3 = (f32[1024,128]{1,0:T(8,128)S(1)}, f32[1024,128]{1,0:T(8,128)S(1)}, u32[]{:S(2)}, u32[]{:S(2)}) collective-permute-start(f32[1024,128]{1,0:T(8,128)S(1)} %shard_map.51.own_ref), channel_id=1, source_target_pairs={{496,0},{17,1},{498,2},{19,3},{500,4},{21,5},{502,6},{23,7},{504,8... | collective-permute-start | bytes 1572872 | tf_op jit(solution)/shard_map/ppermute | solution.py:346
  95.9 7.1 %collective-permute-done.3.nbr_ref = f32[1024,128]{1,0:T(8,128)S(1)} collective-permute-done((f32[1024,128]{1,0:T(8,128)S(1)}, f32[1024,128]{1,0:T(8,128)S(1)}, u32[]{:S(2)}, u32[]{:S(2)}) %collective-permute-start.3) | collective-permute-done | bytes 524320 | tf_op jit(solution)/shard_map/ppermute | solution.py:346
  103.1 0.8 shard_map.52.own
  103.9 6.6 %collective-permute-start.5 = (f32[1024,128]{1,0:T(8,128)S(1)}, f32[1024,128]{1,0:T(8,128)S(1)}, u32[]{:S(2)}, u32[]{:S(2)}) collective-permute-start(f32[1024,128]{1,0:T(8,128)S(1)} %shard_map.52.own), channel_id=1, source_target_pairs={{1,2},{2,1},{3,4},{4,3},{5,6},{6,5},{7,8},{8,7},{9,10},{10,9},{11,... | collective-permute-start | bytes 1572872 | tf_op jit(solution)/shard_map/ppermute | solution.py:299
  110.5 1.9 collective-permute-start.4
  112.4 4.9 %collective-permute-done.5 = f32[1024,128]{1,0:T(8,128)S(1)} collective-permute-done((f32[1024,128]{1,0:T(8,128)S(1)}, f32[1024,128]{1,0:T(8,128)S(1)}, u32[]{:S(2)}, u32[]{:S(2)}) %collective-permute-start.5) | collective-permute-done | bytes 524320 | tf_op jit(solution)/shard_map/ppermute | solution.py:299
  117.4 0.0 collective-permute-done.4
  117.4 0.1 broadcast_select_fusion
  117.4 2.3 %shard_map.53 = (f32[1024,128]{1,0:T(8,128)S(1)}, f32[1024,128]{1,0:T(8,128)S(1)}) custom-call(bf16[128,192]{1,0:T(8,128)(2,1)S(1)} %get-tuple-element.19.back_ref, bf16[64,128]{1,0:T(8,128)(2,1)S(1)} %get-tuple-element.20.my_ref.fwd_ref, bf16[256,256]{1,0:T(8,128)(2,1)S(1)} %get-tuple-element.21.mz_ref, f32[1024,128]{1,0:T(8,128)S(1)} %get-tuple-element.26.up, ...), custom_call_target="tpu_custom_call" | custom-call | flops 4000000 | bytes 2000000 | tf_op jit(solution)/shard_map/pallas_call | solution.py:26
  119.8 1.9 collective-permute-start.6
  121.7 11.6 %collective-permute-done.6.nbr_ref = f32[1024,128]{1,0:T(8,128)S(1)} collective-permute-done((f32[1024,128]{1,0:T(8,128)S(1)}, f32[1024,128]{1,0:T(8,128)S(1)}, u32[]{:S(2)}, u32[]{:S(2)}) %collective-permute-start.6) | collective-permute-done | bytes 524320 | tf_op jit(solution)/shard_map/ppermute | solution.py:345
  133.3 0.3 shard_map.54.own_ref
  133.6 2.2 %collective-permute-start.7 = (f32[1024,128]{1,0:T(8,128)S(1)}, f32[1024,128]{1,0:T(8,128)S(1)}, u32[]{:S(2)}, u32[]{:S(2)}) collective-permute-start(f32[1024,128]{1,0:T(8,128)S(1)} %shard_map.54.own_ref), channel_id=1, source_target_pairs={{496,0},{17,1},{498,2},{19,3},{500,4},{21,5},{502,6},{23,7},{504,8... | collective-permute-start | bytes 1572872 | tf_op jit(solution)/shard_map/ppermute | solution.py:346
  135.9 8.0 %collective-permute-done.7.nbr_ref = f32[1024,128]{1,0:T(8,128)S(1)} collective-permute-done((f32[1024,128]{1,0:T(8,128)S(1)}, f32[1024,128]{1,0:T(8,128)S(1)}, u32[]{:S(2)}, u32[]{:S(2)}) %collective-permute-start.7) | collective-permute-done | bytes 524320 | tf_op jit(solution)/shard_map/ppermute | solution.py:346
  143.8 0.8 shard_map.55.own
  144.7 7.8 %collective-permute-start.9 = (f32[32,16,128]{2,1,0:T(8,128)S(1)}, f32[32,16,128]{2,1,0:T(8,128)S(1)}, u32[]{:S(2)}, u32[]{:S(2)}) collective-permute-start(f32[32,16,128]{2,1,0:T(8,128)S(1)} %get-tuple-element.29), channel_id=1, source_target_pairs={{1,2},{2,1},{3,4},{4,3},{5,6},{6,5},{7,8},{8,7},{9,10},{10,9},{11,... | collective-permute-start | bytes 786440 | tf_op jit(solution)/shard_map/ppermute | solution.py:299
  152.5 1.9 collective-permute-start.8
  154.4 2.1 %collective-permute-done.9 = f32[32,16,128]{2,1,0:T(8,128)S(1)} collective-permute-done((f32[32,16,128]{2,1,0:T(8,128)S(1)}, f32[32,16,128]{2,1,0:T(8,128)S(1)}, u32[]{:S(2)}, u32[]{:S(2)}) %collective-permute-start.9) | collective-permute-done | bytes 262176 | tf_op jit(solution)/shard_map/ppermute | solution.py:299
  156.5 0.0 collective-permute-done.8
  156.6 0.7 shard_map.56
  157.2 38.0 %all_to_all.15.tiles_ref = f32[32,4,8,128]{3,2,1,0:T(8,128)S(1)} all-to-all(f32[32,4,8,128]{3,2,1,0:T(8,128)S(1)} %bitcast.21), channel_id=1, replica_groups=mesh['gz'=32,'gy'=16] {'gz'}, dimensions={0} | all-to-all | bytes 1048576 | tf_op jit(solution)/shard_map/all_to_all | solution.py:310
  195.3 1.9 shard_map.57
  (5 shorter events, 0.2 us)
Async XLA Ops:
  2.4 18.8 %copy-start = (f32[4,32,1024]{2,1,0:T(8,128)S(1)}, f32[4,32,1024]{2,1,0:T(8,128)}, u32[]{:S(2)}) copy-start(f32[4,32,1024]{2,1,0:T(8,128)} %obs_ref.1) | copy-start | bytes 1572868
  2.5 50.2 %all-to-all-start = ((f32[32,4,8,128]{3,2,1,0:T(8,128)}), f32[32,4,8,128]{3,2,1,0:T(8,128)S(1)}, u32[]{:S(2)}, u32[]{:S(2)}) async-start(f32[32,4,8,128]{3,2,1,0:T(8,128)} %shard_map.47), calls=%async_computation | async-start | bytes 1048576 | tf_op jit(solution)/shard_map/all_to_all | solution.py:310
  20.5 0.7 copy-start.2
  21.2 0.7 copy-start.1
  52.6 38.0 %all-to-all-start.1 = ((f32[32,4,8,128]{3,2,1,0:T(8,128)}), f32[32,4,8,128]{3,2,1,0:T(8,128)S(1)}, u32[]{:S(2)}, u32[]{:S(2)}) async-start(f32[32,4,8,128]{3,2,1,0:T(8,128)} %get-tuple-element.22), calls=%async_computation.1 | async-start | bytes 1048576 | tf_op jit(solution)/shard_map/all_to_all | solution.py:310
  58.9 10.8 %collective-permute-start.1 = (f32[32,16,128]{2,1,0:T(8,128)S(1)}, f32[32,16,128]{2,1,0:T(8,128)S(1)}, u32[]{:S(2)}, u32[]{:S(2)}) collective-permute-start(f32[32,16,128]{2,1,0:T(8,128)S(1)} %get-tuple-element.33), channel_id=1, source_target_pairs={{1,2},{2,1},{3,4},{4,3},{5,6},{6,5},{7,8},{8,7},{9,10},{10,9},{11,... | collective-permute-start | bytes 786440 | tf_op jit(solution)/shard_map/ppermute | solution.py:299
  61.9 7.8 %collective-permute-start = (f32[32,16,128]{2,1,0:T(8,128)S(1)}, f32[32,16,128]{2,1,0:T(8,128)S(1)}, u32[]{:S(2)}, u32[]{:S(2)}) collective-permute-start(f32[32,16,128]{2,1,0:T(8,128)S(1)} %get-tuple-element.34), channel_id=1, source_target_pairs={{0,1},{1,0},{2,3},{3,2},{4,5},{5,4},{6,7},{7,6},{8,9},{9,8},{10,11... | collective-permute-start | bytes 786440 | tf_op jit(solution)/shard_map/ppermute | solution.py:300
  70.6 21.9 %collective-permute-start.2 = (f32[1024,128]{1,0:T(8,128)S(1)}, f32[1024,128]{1,0:T(8,128)S(1)}, u32[]{:S(2)}, u32[]{:S(2)}) collective-permute-start(f32[1024,128]{1,0:T(8,128)S(1)} %shard_map.49.own_ref), channel_id=1, source_target_pairs={{16,0},{497,1},{18,2},{499,3},{20,4},{501,5},{22,6},{503,7},{24,8}... | collective-permute-start | bytes 1572872 | tf_op jit(solution)/shard_map/ppermute | solution.py:345
  92.8 10.2 %collective-permute-start.3 = (f32[1024,128]{1,0:T(8,128)S(1)}, f32[1024,128]{1,0:T(8,128)S(1)}, u32[]{:S(2)}, u32[]{:S(2)}) collective-permute-start(f32[1024,128]{1,0:T(8,128)S(1)} %shard_map.51.own_ref), channel_id=1, source_target_pairs={{496,0},{17,1},{498,2},{19,3},{500,4},{21,5},{502,6},{23,7},{504,8... | collective-permute-start | bytes 1572872 | tf_op jit(solution)/shard_map/ppermute | solution.py:346
  103.9 13.5 %collective-permute-start.5 = (f32[1024,128]{1,0:T(8,128)S(1)}, f32[1024,128]{1,0:T(8,128)S(1)}, u32[]{:S(2)}, u32[]{:S(2)}) collective-permute-start(f32[1024,128]{1,0:T(8,128)S(1)} %shard_map.52.own), channel_id=1, source_target_pairs={{1,2},{2,1},{3,4},{4,3},{5,6},{6,5},{7,8},{8,7},{9,10},{10,9},{11,... | collective-permute-start | bytes 1572872 | tf_op jit(solution)/shard_map/ppermute | solution.py:299
  110.5 6.9 %collective-permute-start.4 = (f32[1024,128]{1,0:T(8,128)S(1)}, f32[1024,128]{1,0:T(8,128)S(1)}, u32[]{:S(2)}, u32[]{:S(2)}) collective-permute-start(f32[1024,128]{1,0:T(8,128)S(1)} %shard_map.52.own), channel_id=1, source_target_pairs={{0,1},{1,0},{2,3},{3,2},{4,5},{5,4},{6,7},{7,6},{8,9},{9,8},{10,11... | collective-permute-start | bytes 1572872 | tf_op jit(solution)/shard_map/ppermute | solution.py:300
  119.8 13.5 %collective-permute-start.6 = (f32[1024,128]{1,0:T(8,128)S(1)}, f32[1024,128]{1,0:T(8,128)S(1)}, u32[]{:S(2)}, u32[]{:S(2)}) collective-permute-start(f32[1024,128]{1,0:T(8,128)S(1)} %get-tuple-element.23.own_ref), channel_id=1, source_target_pairs={{16,0},{497,1},{18,2},{499,3},{20,4},{501,5},{22,6},{503,7},{24,8}... | collective-permute-start | bytes 1572872 | tf_op jit(solution)/shard_map/ppermute | solution.py:345
  133.6 10.2 %collective-permute-start.7 = (f32[1024,128]{1,0:T(8,128)S(1)}, f32[1024,128]{1,0:T(8,128)S(1)}, u32[]{:S(2)}, u32[]{:S(2)}) collective-permute-start(f32[1024,128]{1,0:T(8,128)S(1)} %shard_map.54.own_ref), channel_id=1, source_target_pairs={{496,0},{17,1},{498,2},{19,3},{500,4},{21,5},{502,6},{23,7},{504,8... | collective-permute-start | bytes 1572872 | tf_op jit(solution)/shard_map/ppermute | solution.py:346
  144.7 11.8 %collective-permute-start.9 = (f32[32,16,128]{2,1,0:T(8,128)S(1)}, f32[32,16,128]{2,1,0:T(8,128)S(1)}, u32[]{:S(2)}, u32[]{:S(2)}) collective-permute-start(f32[32,16,128]{2,1,0:T(8,128)S(1)} %get-tuple-element.29), channel_id=1, source_target_pairs={{1,2},{2,1},{3,4},{4,3},{5,6},{6,5},{7,8},{8,7},{9,10},{10,9},{11,... | collective-permute-start | bytes 786440 | tf_op jit(solution)/shard_map/ppermute | solution.py:299
  152.5 4.0 %collective-permute-start.8 = (f32[32,16,128]{2,1,0:T(8,128)S(1)}, f32[32,16,128]{2,1,0:T(8,128)S(1)}, u32[]{:S(2)}, u32[]{:S(2)}) collective-permute-start(f32[32,16,128]{2,1,0:T(8,128)S(1)} %get-tuple-element.30), channel_id=1, source_target_pairs={{0,1},{1,0},{2,3},{3,2},{4,5},{5,4},{6,7},{7,6},{8,9},{9,8},{10,11... | collective-permute-start | bytes 786440 | tf_op jit(solution)/shard_map/ppermute | solution.py:300

commit v4 on v3

--- a/solution.py
+++ b/solution.py
@@ -17,6 +17,8 @@
 NX = 1024
 TILES = NX // T
 NZ = 128
+ORDER = [h * 16 + z for k in range(8) for z in (k, 15 - k) for h in range(2)]
+PLACE = [ORDER.index(t) for t in range(TILES)]
 
 VMEM = pl.BlockSpec(memory_space=pltpu.VMEM)
 SMEM = pl.BlockSpec(memory_space=pltpu.SMEM)
@@ -61,24 +63,24 @@
     copies = [pltpu.make_async_copy(block_hbm.at[z], block.at[z], in_sems.at[z]) for z in range(4)]
     for c in copies:
         c.start()
-    sent = []
     for z in range(4):
         copies[z].wait()
         for th in range(8):
             rows = [block[z, pl.ds(8 * yh, 8), pl.ds(128 * th, 128)] for yh in range(4)]
             for tl, tile in enumerate(swap_groups(rows)):
-                tiles[4 * th + tl, z] = tile
-            if z == 3 and th % 2 == 1:
-                group = pl.ds(4 * (th - 1), 8)
-                sent.append(pltpu.make_async_copy(tiles.at[group], tiles_hbm.at[group], out_sems.at[th // 2]))
-                sent[-1].start()
+                tiles[PLACE[4 * th + tl], z] = tile
+    sent = []
+    for i in range(4):
+        group = pl.ds(8 * i, 8)
+        sent.append(pltpu.make_async_copy(tiles.at[group], tiles_hbm.at[group], out_sems.at[i]))
+        sent[-1].start()
     for c in sent:
         c.wait()
 
 
 def from_tiles_kernel(tiles_ref, out_ref):
     for th in range(8):
-        tiles = [tiles_ref[4 * th + tl, 0] for tl in range(4)]
+        tiles = [tiles_ref[PLACE[4 * th + tl], 0] for tl in range(4)]
         for yh, row in enumerate(swap_groups(tiles)):
             out_ref[0, pl.ds(8 * yh, 8), pl.ds(128 * th, 128)] = row
 
@@ -107,7 +109,7 @@
         rolled[z] = pltpu.roll(obs_ref[z], place_ref[2], 1)
 
         def write(t, v, z=z):
-            obs_tiles[t, z] = v
+            obs_tiles[PLACE[t], z] = v
 
         tiles_of(lambda rows, lanes, z=z: rolled[z, rows, lanes], write)
     band = pltpu.roll(ax_ref[...], 2 * NZ - G, 1)
@@ -185,16 +187,23 @@
     ref[pl.ds(i, T, stride=T), :] = v
 
 
-def arrive_xy_kernel(tiles_ref, out_ref):
+def in_order(tiles_ref, planes):
+    for s in range(TILES):
+        planes[pl.ds(32 * s, 32), :] = part(tiles_ref, PLACE[s], 32)
+
+
+def arrive_xy_kernel(tiles_ref, out_ref, planes):
+    in_order(tiles_ref, planes)
     for lo in range(8):
-        v = tiles_ref[pl.ds(lo, NZ, stride=8), :].T
+        v = planes[pl.ds(lo, NZ, stride=8), :].T
         for hi in range(4):
             put_across(out_ref, 8 * hi + lo, v[T * hi : T * (hi + 1)])
 
 
-def arrive_yx_kernel(tiles_ref, out_ref):
+def arrive_yx_kernel(tiles_ref, out_ref, planes):
+    in_order(tiles_ref, planes)
     for lo in range(8):
-        v = tiles_ref[pl.ds(lo, NZ, stride=8), :].T
+        v = planes[pl.ds(lo, NZ, stride=8), :].T
         for hi in range(4):
             out_ref[pl.ds(T * (8 * hi + lo), T), :] = v[T * hi : T * (hi + 1)]
 
@@ -260,7 +269,7 @@
             put_across(out_ref, x + i, w[T * i : T * (i + 1)])
 
 
-def leave_kernel(m_ref, up, own, down, cur_ref, tiles_ref, work):
+def leave_kernel(m_ref, up, own, down, cur_ref, tiles_ref, work, planes):
     m = m_ref[...]
     for x in range(0, T, 2):
         pair = (x, x + 1)
@@ -273,7 +282,9 @@
             work[pl.ds(k * T, T), :] = part(cur_ref, k, T) * r[:, NZ * n : NZ * (n + 1)]
     for lo in range(8):
         v = [work[pl.ds(8 * hi + lo, T, stride=T), :] for hi in range(4)]
-        tiles_ref[pl.ds(lo, NZ, stride=8), :] = jnp.concatenate(v, axis=0).T
+        planes[pl.ds(lo, NZ, stride=8), :] = jnp.concatenate(v, axis=0).T
+    for s in range(TILES):
+        tiles_ref[pl.ds(32 * PLACE[s], 32), :] = part(planes, s, 32)
 
 
 def local(observed, estimate, psf_lateral, psf_axial):
@@ -307,7 +318,9 @@
         return [h.reshape(T * HALF, NZ) for h in swapped]
 
     def exchange(tiles):
-        return lax.all_to_all(tiles, "gz", split_axis=0, concat_axis=0, tiled=True)
+        return lax.all_to_all(
+            tiles, "gz", split_axis=0, concat_axis=0, tiled=True, axis_index_groups=[ORDER]
+        )
 
     tiles_shape = (TILES, 4, 8, 128)
     flat = (NZ * 8, 128)
@@ -337,8 +350,9 @@
     est_tiles = exchange(est_tiles)
     obs_tiles = exchange(obs_tiles)
     whole = [(flat, F32)]
-    (current,) = call(arrive_xy_kernel, whole, [est_tiles.reshape(flat)])
-    (obs,) = call(arrive_yx_kernel, whole, [obs_tiles.reshape(flat)])
+    planes = [pltpu.VMEM(flat, F32)]
+    (current,) = call(arrive_xy_kernel, whole, [est_tiles.reshape(flat)], scratch=planes)
+    (obs,) = call(arrive_yx_kernel, whole, [obs_tiles.reshape(flat)], scratch=planes)
     above, below = y_halves(current)
     (own,) = call(blur_kernel, whole, [y_fwd, z_fwd, above, current, below])
     for step in range(ITERS):
@@ -354,7 +368,7 @@
         else:
             up, down = y_halves(own)
             (tiles,) = call(
-                leave_kernel, whole, [y_bwd, up, own, down, current], scratch=[pltpu.VMEM(flat, F32)]
+                leave_kernel, whole, [y_bwd, up, own, down, current], scratch=planes * 2
             )
     tiles = exchange(tiles.reshape(tiles_shape))
     tile_block = ((TILES, 1, 8, 128), 1)

time: 199 us -> 198 us (level)
  the two profiles are of different devices: /device:TPU:7 before, /device:TPU:22 now
where the time goes in v4:
time: 198 us; the launch traced here: 197 us
  waiting for transfers between devices  90.6 us (46%)
  starting transfers between devices  51.3 us (26%)
  blocking collectives  38.8 us (20%)
  Pallas kernels  14.9 us (8%)
    all_to_all x2, waiting for transfers between devices, exchange(): lax.all_to_all(tiles, 'gz', split_axis=0, concat_axis=0, tiled=True, axis...  46.9 us
    all_to_all x1, blocking collectives, exchange(): lax.all_to_all(tiles, 'gz', split_axis=0, concat_axis=0, tiled=True, axis...  38.8 us
    ppermute x2, waiting for transfers between devices, local(): lax.ppermute(own, joint, behind)  25.5 us
    all_to_all x2, starting transfers between devices, exchange(): lax.all_to_all(tiles, 'gz', split_axis=0, concat_axis=0, tiled=True, axis...  23.5 us
    ppermute x3, starting transfers between devices, y_swap(): from_inner = lax.ppermute(to_inner, 'gy', inner)  11.7 us
    pallas_call x10, Pallas kernels, call(): pl.pallas_call(body, out_shape=[jax.ShapeDtypeStruct(s, d) for s, d in ou...  10.5 us
    ppermute x2, waiting for transfers between devices, local(): lax.ppermute(own, joint, ahead)  9.15 us
    ppermute x3, waiting for transfers between devices, y_swap(): from_outer = lax.ppermute(to_outer, 'gy', outer)  8.33 us
  transfers between devices with their start and end apart: 12, of which 9 were waited for; matrix products, arithmetic and copies ran while one was open for 0% of the time, Pallas kernels for 3%

profile of v4, /device:TPU:22, one launch (start us, length us, event | category | flops | bytes accessed | tf_op | source)
XLA Modules:
  0.0 197.5 jit_solution(15888837302622083946)
XLA Ops:
  0.0 2.5 %shard_map.47 = f32[32,4,8,128]{3,2,1,0:T(8,128)} custom-call(f32[4,32,1024]{2,1,0:T(8,128)} %block_hbm.1), custom_call_target="tpu_custom_call" | custom-call | flops 1000000 | bytes 2000000 | tf_op jit(solution)/shard_map/pallas_call | solution.py:329
  2.5 0.0 copy-start
  2.5 18.4 %all-to-all-start = ((f32[32,4,8,128]{3,2,1,0:T(8,128)}), f32[32,4,8,128]{3,2,1,0:T(8,128)S(1)}, u32[]{:S(2)}, u32[]{:S(2)}) async-start(f32[32,4,8,128]{3,2,1,0:T(8,128)} %shard_map.47), calls=%async_computation | async-start | bytes 1048576 | tf_op jit(solution)/shard_map/all_to_all | solution.py:321
  20.9 0.0 copy-start.2
  20.9 0.7 copy-done.2
  21.5 0.1 pad_add_fusion.place_ref
  21.6 0.0 copy-start.1
  21.6 0.0 copy-done
  21.6 0.7 copy-done.1
  22.3 3.7 %shard_map.46 = (f32[32,4,8,128]{3,2,1,0:T(8,128)}, bf16[256,256]{1,0:T(8,128)(2,1)S(1)}, bf16[256,256]{1,0:T(8,128)(2,1)S(1)}, bf16[64,128]{1,0:T(8,128)(2,1)S(...) custom-call(s32[3]{0:T(128)S(1)} %pad_add_fusion.place_ref, ...), custom_call_target="tpu_custom_call" | custom-call | flops 4000000 | bytes 2000000 | tf_op jit(solution)/shard_map/pallas_call | solution.py:28
  26.0 27.6 %all-to-all-done = f32[32,4,8,128]{3,2,1,0:T(8,128)S(1)} async-done(((f32[32,4,8,128]{3,2,1,0:T(8,128)}), f32[32,4,8,128]{3,2,1,0:T(8,128)S(1)}, u32[]{:S(2)}, u32[]{:S(2)}) %all-to-all-start) | async-done | bytes 524320 | tf_op jit(solution)/shard_map/all_to_all | solution.py:321
  53.6 5.1 %all-to-all-start.1 = ((f32[32,4,8,128]{3,2,1,0:T(8,128)}), f32[32,4,8,128]{3,2,1,0:T(8,128)S(1)}, u32[]{:S(2)}, u32[]{:S(2)}) async-start(f32[32,4,8,128]{3,2,1,0:T(8,128)} %get-tuple-element.22), calls=%async_computation.1 | async-start | bytes 1048576 | tf_op jit(solution)/shard_map/all_to_all | solution.py:321
  58.8 0.4 shard_map.48.cur
  59.3 1.9 collective-permute-start.1
  61.2 3.2 %collective-permute-start = (f32[32,16,128]{2,1,0:T(8,128)S(1)}, f32[32,16,128]{2,1,0:T(8,128)S(1)}, u32[]{:S(2)}, u32[]{:S(2)}) collective-permute-start(f32[32,16,128]{2,1,0:T(8,128)S(1)} %get-tuple-element.34), channel_id=1, source_target_pairs={{0,1},{1,0},{2,3},{3,2},{4,5},{5,4},{6,7},{7,6},{8,9},{9,8},{10,11... | collective-permute-start | bytes 786440 | tf_op jit(solution)/shard_map/ppermute | solution.py:311
  64.4 2.5 %collective-permute-done.1 = f32[32,16,128]{2,1,0:T(8,128)S(1)} collective-permute-done((f32[32,16,128]{2,1,0:T(8,128)S(1)}, f32[32,16,128]{2,1,0:T(8,128)S(1)}, u32[]{:S(2)}, u32[]{:S(2)}) %collective-permute-start.1) | collective-permute-done | bytes 262176 | tf_op jit(solution)/shard_map/ppermute | solution.py:310
  66.9 0.0 collective-permute-done
  67.0 0.8 shard_map.49.own_ref
  67.8 4.6 %collective-permute-start.2 = (f32[1024,128]{1,0:T(8,128)S(1)}, f32[1024,128]{1,0:T(8,128)S(1)}, u32[]{:S(2)}, u32[]{:S(2)}) collective-permute-start(f32[1024,128]{1,0:T(8,128)S(1)} %shard_map.49.own_ref), channel_id=1, source_target_pairs={{16,0},{497,1},{18,2},{499,3},{20,4},{501,5},{22,6},{503,7},{24,8}... | collective-permute-start | bytes 1572872 | tf_op jit(solution)/shard_map/ppermute | solution.py:359
  72.4 19.2 %all-to-all-done.1 = f32[32,4,8,128]{3,2,1,0:T(8,128)S(1)} async-done(((f32[32,4,8,128]{3,2,1,0:T(8,128)}), f32[32,4,8,128]{3,2,1,0:T(8,128)S(1)}, u32[]{:S(2)}, u32[]{:S(2)}) %all-to-all-start.1) | async-done | bytes 524320 | tf_op jit(solution)/shard_map/all_to_all | solution.py:321
  91.6 0.2 shard_map.50.obs_ref
  91.9 0.0 collective-permute-done.2.nbr_ref
  91.9 0.3 shard_map.51.own_ref
  92.2 1.9 collective-permute-start.3
  94.1 12.8 %collective-permute-done.3.nbr_ref = f32[1024,128]{1,0:T(8,128)S(1)} collective-permute-done((f32[1024,128]{1,0:T(8,128)S(1)}, f32[1024,128]{1,0:T(8,128)S(1)}, u32[]{:S(2)}, u32[]{:S(2)}) %collective-permute-start.3) | collective-permute-done | bytes 524320 | tf_op jit(solution)/shard_map/ppermute | solution.py:360
  106.9 0.8 shard_map.52.own
  107.7 1.9 collective-permute-start.5
  109.7 3.2 %collective-permute-start.4 = (f32[1024,128]{1,0:T(8,128)S(1)}, f32[1024,128]{1,0:T(8,128)S(1)}, u32[]{:S(2)}, u32[]{:S(2)}) collective-permute-start(f32[1024,128]{1,0:T(8,128)S(1)} %shard_map.52.own), channel_id=1, source_target_pairs={{0,1},{1,0},{2,3},{3,2},{4,5},{5,4},{6,7},{7,6},{8,9},{9,8},{10,11... | collective-permute-start | bytes 1572872 | tf_op jit(solution)/shard_map/ppermute | solution.py:311
  112.9 5.4 %collective-permute-done.5 = f32[1024,128]{1,0:T(8,128)S(1)} collective-permute-done((f32[1024,128]{1,0:T(8,128)S(1)}, f32[1024,128]{1,0:T(8,128)S(1)}, u32[]{:S(2)}, u32[]{:S(2)}) %collective-permute-start.5) | collective-permute-done | bytes 524320 | tf_op jit(solution)/shard_map/ppermute | solution.py:310
  118.2 0.0 collective-permute-done.4
  118.2 0.1 broadcast_select_fusion
  118.3 2.3 %shard_map.53 = (f32[1024,128]{1,0:T(8,128)S(1)}, f32[1024,128]{1,0:T(8,128)S(1)}) custom-call(bf16[128,192]{1,0:T(8,128)(2,1)S(1)} %get-tuple-element.19.back_ref, bf16[64,128]{1,0:T(8,128)(2,1)S(1)} %get-tuple-element.20.my_ref.fwd_ref, bf16[256,256]{1,0:T(8,128)(2,1)S(1)} %get-tuple-element.21.mz_ref, f32[1024,128]{1,0:T(8,128)S(1)} %get-tuple-element.26.up, ...), custom_call_target="tpu_custom_call" | custom-call | flops 4000000 | bytes 2000000 | tf_op jit(solution)/shard_map/pallas_call | solution.py:28
  120.6 1.9 collective-permute-start.6
  122.6 9.1 %collective-permute-done.6.nbr_ref = f32[1024,128]{1,0:T(8,128)S(1)} collective-permute-done((f32[1024,128]{1,0:T(8,128)S(1)}, f32[1024,128]{1,0:T(8,128)S(1)}, u32[]{:S(2)}, u32[]{:S(2)}) %collective-permute-start.6) | collective-permute-done | bytes 524320 | tf_op jit(solution)/shard_map/ppermute | solution.py:359
  131.7 0.3 shard_map.54.own_ref
  132.0 1.9 collective-permute-start.7
  134.0 12.8 %collective-permute-done.7.nbr_ref = f32[1024,128]{1,0:T(8,128)S(1)} collective-permute-done((f32[1024,128]{1,0:T(8,128)S(1)}, f32[1024,128]{1,0:T(8,128)S(1)}, u32[]{:S(2)}, u32[]{:S(2)}) %collective-permute-start.7) | collective-permute-done | bytes 524320 | tf_op jit(solution)/shard_map/ppermute | solution.py:360
  146.7 0.8 shard_map.55.own
  147.6 1.9 collective-permute-start.9
  149.5 5.3 %collective-permute-start.8 = (f32[32,16,128]{2,1,0:T(8,128)S(1)}, f32[32,16,128]{2,1,0:T(8,128)S(1)}, u32[]{:S(2)}, u32[]{:S(2)}) collective-permute-start(f32[32,16,128]{2,1,0:T(8,128)S(1)} %get-tuple-element.30), channel_id=1, source_target_pairs={{0,1},{1,0},{2,3},{3,2},{4,5},{5,4},{6,7},{7,6},{8,9},{9,8},{10,11... | collective-permute-start | bytes 786440 | tf_op jit(solution)/shard_map/ppermute | solution.py:311
  154.9 0.4 collective-permute-done.9
  155.3 0.7 collective-permute-done.8
  156.1 0.7 shard_map.56
  156.7 38.8 %all_to_all.15.tiles_ref = f32[32,4,8,128]{3,2,1,0:T(8,128)S(1)} all-to-all(f32[32,4,8,128]{3,2,1,0:T(8,128)S(1)} %bitcast.21), channel_id=1, replica_groups={{0,256,240,496,16,272,224,480,32,288,208,464,48,304,192,448,64,320,176,..., dimensions={0} | all-to-all | bytes 1048576 | tf_op jit(solution)/shard_map/all_to_all | solution.py:321
  195.6 1.9 shard_map.57
  (5 shorter events, 0.2 us)
Async XLA Ops:
  2.5 19.2 %copy-start = (f32[4,32,1024]{2,1,0:T(8,128)S(1)}, f32[4,32,1024]{2,1,0:T(8,128)}, u32[]{:S(2)}) copy-start(f32[4,32,1024]{2,1,0:T(8,128)} %obs_ref.1) | copy-start | bytes 1572868
  2.5 51.1 %all-to-all-start = ((f32[32,4,8,128]{3,2,1,0:T(8,128)}), f32[32,4,8,128]{3,2,1,0:T(8,128)S(1)}, u32[]{:S(2)}, u32[]{:S(2)}) async-start(f32[32,4,8,128]{3,2,1,0:T(8,128)} %shard_map.47), calls=%async_computation | async-start | bytes 1048576 | tf_op jit(solution)/shard_map/all_to_all | solution.py:321
  20.9 0.7 copy-start.2
  21.6 0.7 copy-start.1
  53.6 38.0 %all-to-all-start.1 = ((f32[32,4,8,128]{3,2,1,0:T(8,128)}), f32[32,4,8,128]{3,2,1,0:T(8,128)S(1)}, u32[]{:S(2)}, u32[]{:S(2)}) async-start(f32[32,4,8,128]{3,2,1,0:T(8,128)} %get-tuple-element.22), calls=%async_computation.1 | async-start | bytes 1048576 | tf_op jit(solution)/shard_map/all_to_all | solution.py:321
  59.3 7.7 %collective-permute-start.1 = (f32[32,16,128]{2,1,0:T(8,128)S(1)}, f32[32,16,128]{2,1,0:T(8,128)S(1)}, u32[]{:S(2)}, u32[]{:S(2)}) collective-permute-start(f32[32,16,128]{2,1,0:T(8,128)S(1)} %get-tuple-element.33), channel_id=1, source_target_pairs={{1,2},{2,1},{3,4},{4,3},{5,6},{6,5},{7,8},{8,7},{9,10},{10,9},{11,... | collective-permute-start | bytes 786440 | tf_op jit(solution)/shard_map/ppermute | solution.py:310
  61.2 5.8 %collective-permute-start = (f32[32,16,128]{2,1,0:T(8,128)S(1)}, f32[32,16,128]{2,1,0:T(8,128)S(1)}, u32[]{:S(2)}, u32[]{:S(2)}) collective-permute-start(f32[32,16,128]{2,1,0:T(8,128)S(1)} %get-tuple-element.34), channel_id=1, source_target_pairs={{0,1},{1,0},{2,3},{3,2},{4,5},{5,4},{6,7},{7,6},{8,9},{9,8},{10,11... | collective-permute-start | bytes 786440 | tf_op jit(solution)/shard_map/ppermute | solution.py:311
  67.8 24.0 %collective-permute-start.2 = (f32[1024,128]{1,0:T(8,128)S(1)}, f32[1024,128]{1,0:T(8,128)S(1)}, u32[]{:S(2)}, u32[]{:S(2)}) collective-permute-start(f32[1024,128]{1,0:T(8,128)S(1)} %shard_map.49.own_ref), channel_id=1, source_target_pairs={{16,0},{497,1},{18,2},{499,3},{20,4},{501,5},{22,6},{503,7},{24,8}... | collective-permute-start | bytes 1572872 | tf_op jit(solution)/shard_map/ppermute | solution.py:359
  92.2 14.7 %collective-permute-start.3 = (f32[1024,128]{1,0:T(8,128)S(1)}, f32[1024,128]{1,0:T(8,128)S(1)}, u32[]{:S(2)}, u32[]{:S(2)}) collective-permute-start(f32[1024,128]{1,0:T(8,128)S(1)} %shard_map.51.own_ref), channel_id=1, source_target_pairs={{496,0},{17,1},{498,2},{19,3},{500,4},{21,5},{502,6},{23,7},{504,8... | collective-permute-start | bytes 1572872 | tf_op jit(solution)/shard_map/ppermute | solution.py:360
  107.7 10.5 %collective-permute-start.5 = (f32[1024,128]{1,0:T(8,128)S(1)}, f32[1024,128]{1,0:T(8,128)S(1)}, u32[]{:S(2)}, u32[]{:S(2)}) collective-permute-start(f32[1024,128]{1,0:T(8,128)S(1)} %shard_map.52.own), channel_id=1, source_target_pairs={{1,2},{2,1},{3,4},{4,3},{5,6},{6,5},{7,8},{8,7},{9,10},{10,9},{11,... | collective-permute-start | bytes 1572872 | tf_op jit(solution)/shard_map/ppermute | solution.py:310
  109.7 8.6 %collective-permute-start.4 = (f32[1024,128]{1,0:T(8,128)S(1)}, f32[1024,128]{1,0:T(8,128)S(1)}, u32[]{:S(2)}, u32[]{:S(2)}) collective-permute-start(f32[1024,128]{1,0:T(8,128)S(1)} %shard_map.52.own), channel_id=1, source_target_pairs={{0,1},{1,0},{2,3},{3,2},{4,5},{5,4},{6,7},{7,6},{8,9},{9,8},{10,11... | collective-permute-start | bytes 1572872 | tf_op jit(solution)/shard_map/ppermute | solution.py:311
  120.6 11.1 %collective-permute-start.6 = (f32[1024,128]{1,0:T(8,128)S(1)}, f32[1024,128]{1,0:T(8,128)S(1)}, u32[]{:S(2)}, u32[]{:S(2)}) collective-permute-start(f32[1024,128]{1,0:T(8,128)S(1)} %get-tuple-element.23.own_ref), channel_id=1, source_target_pairs={{16,0},{497,1},{18,2},{499,3},{20,4},{501,5},{22,6},{503,7},{24,8}... | collective-permute-start | bytes 1572872 | tf_op jit(solution)/shard_map/ppermute | solution.py:359
  132.0 14.7 %collective-permute-start.7 = (f32[1024,128]{1,0:T(8,128)S(1)}, f32[1024,128]{1,0:T(8,128)S(1)}, u32[]{:S(2)}, u32[]{:S(2)}) collective-permute-start(f32[1024,128]{1,0:T(8,128)S(1)} %shard_map.54.own_ref), channel_id=1, source_target_pairs={{496,0},{17,1},{498,2},{19,3},{500,4},{21,5},{502,6},{23,7},{504,8... | collective-permute-start | bytes 1572872 | tf_op jit(solution)/shard_map/ppermute | solution.py:360
  147.6 7.7 %collective-permute-start.9 = (f32[32,16,128]{2,1,0:T(8,128)S(1)}, f32[32,16,128]{2,1,0:T(8,128)S(1)}, u32[]{:S(2)}, u32[]{:S(2)}) collective-permute-start(f32[32,16,128]{2,1,0:T(8,128)S(1)} %get-tuple-element.29), channel_id=1, source_target_pairs={{1,2},{2,1},{3,4},{4,3},{5,6},{6,5},{7,8},{8,7},{9,10},{10,9},{11,... | collective-permute-start | bytes 786440 | tf_op jit(solution)/shard_map/ppermute | solution.py:310
  149.5 6.5 %collective-permute-start.8 = (f32[32,16,128]{2,1,0:T(8,128)S(1)}, f32[32,16,128]{2,1,0:T(8,128)S(1)}, u32[]{:S(2)}, u32[]{:S(2)}) collective-permute-start(f32[32,16,128]{2,1,0:T(8,128)S(1)} %get-tuple-element.30), channel_id=1, source_target_pairs={{0,1},{1,0},{2,3},{3,2},{4,5},{5,4},{6,7},{7,6},{8,9},{9,8},{10,11... | collective-permute-start | bytes 786440 | tf_op jit(solution)/shard_map/ppermute | solution.py:311

commit v5 on v4

--- a/solution.py
+++ b/solution.py
@@ -17,7 +17,7 @@
 NX = 1024
 TILES = NX // T
 NZ = 128
-ORDER = [h * 16 + z for k in range(8) for z in (k, 15 - k) for h in range(2)]
+ORDER = [h * 16 + int(format(i, '04b')[::-1], 2) for i in range(16) for h in range(2)]
 PLACE = [ORDER.index(t) for t in range(TILES)]
 
 VMEM = pl.BlockSpec(memory_space=pltpu.VMEM)

time: 198 us -> 198 us (level)
  the two profiles are of different devices: /device:TPU:22 before, /device:TPU:38 now
where the time goes in v5:
time: 198 us
  waiting for transfers between devices  84.2 us (43%)
  starting transfers between devices  52.4 us (26%)
  blocking collectives  44.2 us (22%)
  Pallas kernels  14.9 us (8%)
    all_to_all x2, waiting for transfers between devices, exchange(): lax.all_to_all(tiles, 'gz', split_axis=0, concat_axis=0, tiled=True, axis...  50.1 us
    all_to_all x1, blocking collectives, exchange(): lax.all_to_all(tiles, 'gz', split_axis=0, concat_axis=0, tiled=True, axis...  44.2 us
    all_to_all x2, starting transfers between devices, exchange(): lax.all_to_all(tiles, 'gz', split_axis=0, concat_axis=0, tiled=True, axis...  22.6 us
    ppermute x2, waiting for transfers between devices, local(): lax.ppermute(own, joint, behind)  17.2 us
    pallas_call x10, Pallas kernels, call(): pl.pallas_call(body, out_shape=[jax.ShapeDtypeStruct(s, d) for s, d in ou...  10.5 us
    ppermute x3, waiting for transfers between devices, y_swap(): from_outer = lax.ppermute(to_outer, 'gy', outer)  10.1 us
    ppermute x2, starting transfers between devices, local(): lax.ppermute(own, joint, ahead)  8.75 us
    ppermute x3, starting transfers between devices, y_swap(): from_inner = lax.ppermute(to_inner, 'gy', inner)  8.53 us
  transfers between devices with their start and end apart: 12, of which 9 were waited for; matrix products, arithmetic and copies ran while one was open for 0% of the time, Pallas kernels for 3%

profile of v5, /device:TPU:38, one launch (start us, length us, event | category | flops | bytes accessed | tf_op | source)
XLA Modules:
  0.0 197.6 jit_solution(16950891684253268983)
XLA Ops:
  0.0 2.5 %shard_map.47 = f32[32,4,8,128]{3,2,1,0:T(8,128)} custom-call(f32[4,32,1024]{2,1,0:T(8,128)} %block_hbm.1), custom_call_target="tpu_custom_call" | custom-call | flops 1000000 | bytes 2000000 | tf_op jit(solution)/shard_map/pallas_call | solution.py:329
  2.5 0.0 copy-start
  2.5 18.1 %all-to-all-start = ((f32[32,4,8,128]{3,2,1,0:T(8,128)}), f32[32,4,8,128]{3,2,1,0:T(8,128)S(1)}, u32[]{:S(2)}, u32[]{:S(2)}) async-start(f32[32,4,8,128]{3,2,1,0:T(8,128)} %shard_map.47), calls=%async_computation | async-start | bytes 1048576 | tf_op jit(solution)/shard_map/all_to_all | solution.py:321
  20.6 0.0 copy-start.2
  20.6 0.7 copy-done.2
  21.3 0.1 pad_add_fusion.place_ref
  21.4 0.0 copy-start.1
  21.4 0.0 copy-done
  21.4 0.7 copy-done.1
  22.1 3.7 %shard_map.46 = (f32[32,4,8,128]{3,2,1,0:T(8,128)}, bf16[256,256]{1,0:T(8,128)(2,1)S(1)}, bf16[256,256]{1,0:T(8,128)(2,1)S(1)}, bf16[64,128]{1,0:T(8,128)(2,1)S(...) custom-call(s32[3]{0:T(128)S(1)} %pad_add_fusion.place_ref, ...), custom_call_target="tpu_custom_call" | custom-call | flops 4000000 | bytes 2000000 | tf_op jit(solution)/shard_map/pallas_call | solution.py:28
  25.8 28.3 %all-to-all-done = f32[32,4,8,128]{3,2,1,0:T(8,128)S(1)} async-done(((f32[32,4,8,128]{3,2,1,0:T(8,128)}), f32[32,4,8,128]{3,2,1,0:T(8,128)S(1)}, u32[]{:S(2)}, u32[]{:S(2)}) %all-to-all-start) | async-done | bytes 524320 | tf_op jit(solution)/shard_map/all_to_all | solution.py:321
  54.0 4.4 %all-to-all-start.1 = ((f32[32,4,8,128]{3,2,1,0:T(8,128)}), f32[32,4,8,128]{3,2,1,0:T(8,128)S(1)}, u32[]{:S(2)}, u32[]{:S(2)}) async-start(f32[32,4,8,128]{3,2,1,0:T(8,128)} %get-tuple-element.22), calls=%async_computation.1 | async-start | bytes 1048576 | tf_op jit(solution)/shard_map/all_to_all | solution.py:321
  58.5 0.4 shard_map.48.cur
  59.0 1.9 collective-permute-start.1
  60.9 2.6 %collective-permute-start = (f32[32,16,128]{2,1,0:T(8,128)S(1)}, f32[32,16,128]{2,1,0:T(8,128)S(1)}, u32[]{:S(2)}, u32[]{:S(2)}) collective-permute-start(f32[32,16,128]{2,1,0:T(8,128)S(1)} %get-tuple-element.34), channel_id=1, source_target_pairs={{0,1},{1,0},{2,3},{3,2},{4,5},{5,4},{6,7},{7,6},{8,9},{9,8},{10,11... | collective-permute-start | bytes 786440 | tf_op jit(solution)/shard_map/ppermute | solution.py:311
  63.5 3.2 %collective-permute-done.1 = f32[32,16,128]{2,1,0:T(8,128)S(1)} collective-permute-done((f32[32,16,128]{2,1,0:T(8,128)S(1)}, f32[32,16,128]{2,1,0:T(8,128)S(1)}, u32[]{:S(2)}, u32[]{:S(2)}) %collective-permute-start.1) | collective-permute-done | bytes 262176 | tf_op jit(solution)/shard_map/ppermute | solution.py:310
  66.7 0.0 collective-permute-done
  66.7 0.8 shard_map.49.own_ref
  67.6 2.1 %collective-permute-start.2 = (f32[1024,128]{1,0:T(8,128)S(1)}, f32[1024,128]{1,0:T(8,128)S(1)}, u32[]{:S(2)}, u32[]{:S(2)}) collective-permute-start(f32[1024,128]{1,0:T(8,128)S(1)} %shard_map.49.own_ref), channel_id=1, source_target_pairs={{16,0},{497,1},{18,2},{499,3},{20,4},{501,5},{22,6},{503,7},{24,8}... | collective-permute-start | bytes 1572872 | tf_op jit(solution)/shard_map/ppermute | solution.py:359
  69.7 21.8 %all-to-all-done.1 = f32[32,4,8,128]{3,2,1,0:T(8,128)S(1)} async-done(((f32[32,4,8,128]{3,2,1,0:T(8,128)}), f32[32,4,8,128]{3,2,1,0:T(8,128)S(1)}, u32[]{:S(2)}, u32[]{:S(2)}) %all-to-all-start.1) | async-done | bytes 524320 | tf_op jit(solution)/shard_map/all_to_all | solution.py:321
  91.5 0.2 shard_map.50.obs_ref
  91.7 0.0 collective-permute-done.2.nbr_ref
  91.7 0.3 shard_map.51.own_ref
  92.0 3.5 %collective-permute-start.3 = (f32[1024,128]{1,0:T(8,128)S(1)}, f32[1024,128]{1,0:T(8,128)S(1)}, u32[]{:S(2)}, u32[]{:S(2)}) collective-permute-start(f32[1024,128]{1,0:T(8,128)S(1)} %shard_map.51.own_ref), channel_id=1, source_target_pairs={{496,0},{17,1},{498,2},{19,3},{500,4},{21,5},{502,6},{23,7},{504,8... | collective-permute-start | bytes 1572872 | tf_op jit(solution)/shard_map/ppermute | solution.py:360
  95.5 7.6 %collective-permute-done.3.nbr_ref = f32[1024,128]{1,0:T(8,128)S(1)} collective-permute-done((f32[1024,128]{1,0:T(8,128)S(1)}, f32[1024,128]{1,0:T(8,128)S(1)}, u32[]{:S(2)}, u32[]{:S(2)}) %collective-permute-start.3) | collective-permute-done | bytes 524320 | tf_op jit(solution)/shard_map/ppermute | solution.py:360
  103.1 0.8 shard_map.52.own
  104.0 1.9 collective-permute-start.5
  105.9 2.6 %collective-permute-start.4 = (f32[1024,128]{1,0:T(8,128)S(1)}, f32[1024,128]{1,0:T(8,128)S(1)}, u32[]{:S(2)}, u32[]{:S(2)}) collective-permute-start(f32[1024,128]{1,0:T(8,128)S(1)} %shard_map.52.own), channel_id=1, source_target_pairs={{0,1},{1,0},{2,3},{3,2},{4,5},{5,4},{6,7},{7,6},{8,9},{9,8},{10,11... | collective-permute-start | bytes 1572872 | tf_op jit(solution)/shard_map/ppermute | solution.py:311
  108.5 6.0 %collective-permute-done.5 = f32[1024,128]{1,0:T(8,128)S(1)} collective-permute-done((f32[1024,128]{1,0:T(8,128)S(1)}, f32[1024,128]{1,0:T(8,128)S(1)}, u32[]{:S(2)}, u32[]{:S(2)}) %collective-permute-start.5) | collective-permute-done | bytes 524320 | tf_op jit(solution)/shard_map/ppermute | solution.py:310
  114.5 0.0 collective-permute-done.4
  114.5 0.1 broadcast_select_fusion
  114.5 2.3 %shard_map.53 = (f32[1024,128]{1,0:T(8,128)S(1)}, f32[1024,128]{1,0:T(8,128)S(1)}) custom-call(bf16[128,192]{1,0:T(8,128)(2,1)S(1)} %get-tuple-element.19.back_ref, bf16[64,128]{1,0:T(8,128)(2,1)S(1)} %get-tuple-element.20.my_ref.fwd_ref, bf16[256,256]{1,0:T(8,128)(2,1)S(1)} %get-tuple-element.21.mz_ref, f32[1024,128]{1,0:T(8,128)S(1)} %get-tuple-element.26.up, ...), custom_call_target="tpu_custom_call" | custom-call | flops 4000000 | bytes 2000000 | tf_op jit(solution)/shard_map/pallas_call | solution.py:28
  116.9 6.6 %collective-permute-start.6 = (f32[1024,128]{1,0:T(8,128)S(1)}, f32[1024,128]{1,0:T(8,128)S(1)}, u32[]{:S(2)}, u32[]{:S(2)}) collective-permute-start(f32[1024,128]{1,0:T(8,128)S(1)} %get-tuple-element.23.own_ref), channel_id=1, source_target_pairs={{16,0},{497,1},{18,2},{499,3},{20,4},{501,5},{22,6},{503,7},{24,8}... | collective-permute-start | bytes 1572872 | tf_op jit(solution)/shard_map/ppermute | solution.py:359
  123.5 6.7 %collective-permute-done.6.nbr_ref = f32[1024,128]{1,0:T(8,128)S(1)} collective-permute-done((f32[1024,128]{1,0:T(8,128)S(1)}, f32[1024,128]{1,0:T(8,128)S(1)}, u32[]{:S(2)}, u32[]{:S(2)}) %collective-permute-start.6) | collective-permute-done | bytes 524320 | tf_op jit(solution)/shard_map/ppermute | solution.py:359
  130.2 0.3 shard_map.54.own_ref
  130.5 1.9 collective-permute-start.7
  132.4 9.6 %collective-permute-done.7.nbr_ref = f32[1024,128]{1,0:T(8,128)S(1)} collective-permute-done((f32[1024,128]{1,0:T(8,128)S(1)}, f32[1024,128]{1,0:T(8,128)S(1)}, u32[]{:S(2)}, u32[]{:S(2)}) %collective-permute-start.7) | collective-permute-done | bytes 524320 | tf_op jit(solution)/shard_map/ppermute | solution.py:360
  142.0 0.8 shard_map.55.own
  142.9 3.4 %collective-permute-start.9 = (f32[32,16,128]{2,1,0:T(8,128)S(1)}, f32[32,16,128]{2,1,0:T(8,128)S(1)}, u32[]{:S(2)}, u32[]{:S(2)}) collective-permute-start(f32[32,16,128]{2,1,0:T(8,128)S(1)} %get-tuple-element.29), channel_id=1, source_target_pairs={{1,2},{2,1},{3,4},{4,3},{5,6},{6,5},{7,8},{8,7},{9,10},{10,9},{11,... | collective-permute-start | bytes 786440 | tf_op jit(solution)/shard_map/ppermute | solution.py:310
  146.3 3.3 %collective-permute-start.8 = (f32[32,16,128]{2,1,0:T(8,128)S(1)}, f32[32,16,128]{2,1,0:T(8,128)S(1)}, u32[]{:S(2)}, u32[]{:S(2)}) collective-permute-start(f32[32,16,128]{2,1,0:T(8,128)S(1)} %get-tuple-element.30), channel_id=1, source_target_pairs={{0,1},{1,0},{2,3},{3,2},{4,5},{5,4},{6,7},{7,6},{8,9},{9,8},{10,11... | collective-permute-start | bytes 786440 | tf_op jit(solution)/shard_map/ppermute | solution.py:311
  149.6 1.0 collective-permute-done.9
  150.6 0.2 collective-permute-done.8
  150.8 0.7 shard_map.56
  151.5 44.2 %all_to_all.15.tiles_ref = f32[32,4,8,128]{3,2,1,0:T(8,128)S(1)} all-to-all(f32[32,4,8,128]{3,2,1,0:T(8,128)S(1)} %bitcast.21), channel_id=1, replica_groups={{0,256,128,384,64,320,192,448,32,288,160,416,96,352,224,480,16,272,144,..., dimensions={0} | all-to-all | bytes 1048576 | tf_op jit(solution)/shard_map/all_to_all | solution.py:321
  195.7 1.9 shard_map.57
  (5 shorter events, 0.2 us)
Async XLA Ops:
  2.5 18.9 %copy-start = (f32[4,32,1024]{2,1,0:T(8,128)S(1)}, f32[4,32,1024]{2,1,0:T(8,128)}, u32[]{:S(2)}) copy-start(f32[4,32,1024]{2,1,0:T(8,128)} %obs_ref.1) | copy-start | bytes 1572868
  2.5 51.6 %all-to-all-start = ((f32[32,4,8,128]{3,2,1,0:T(8,128)}), f32[32,4,8,128]{3,2,1,0:T(8,128)S(1)}, u32[]{:S(2)}, u32[]{:S(2)}) async-start(f32[32,4,8,128]{3,2,1,0:T(8,128)} %shard_map.47), calls=%async_computation | async-start | bytes 1048576 | tf_op jit(solution)/shard_map/all_to_all | solution.py:321
  20.6 0.7 copy-start.2
  21.4 0.7 copy-start.1
  54.0 37.5 %all-to-all-start.1 = ((f32[32,4,8,128]{3,2,1,0:T(8,128)}), f32[32,4,8,128]{3,2,1,0:T(8,128)S(1)}, u32[]{:S(2)}, u32[]{:S(2)}) async-start(f32[32,4,8,128]{3,2,1,0:T(8,128)} %get-tuple-element.22), calls=%async_computation.1 | async-start | bytes 1048576 | tf_op jit(solution)/shard_map/all_to_all | solution.py:321
  59.0 7.7 %collective-permute-start.1 = (f32[32,16,128]{2,1,0:T(8,128)S(1)}, f32[32,16,128]{2,1,0:T(8,128)S(1)}, u32[]{:S(2)}, u32[]{:S(2)}) collective-permute-start(f32[32,16,128]{2,1,0:T(8,128)S(1)} %get-tuple-element.33), channel_id=1, source_target_pairs={{1,2},{2,1},{3,4},{4,3},{5,6},{6,5},{7,8},{8,7},{9,10},{10,9},{11,... | collective-permute-start | bytes 786440 | tf_op jit(solution)/shard_map/ppermute | solution.py:310
  60.9 5.8 %collective-permute-start = (f32[32,16,128]{2,1,0:T(8,128)S(1)}, f32[32,16,128]{2,1,0:T(8,128)S(1)}, u32[]{:S(2)}, u32[]{:S(2)}) collective-permute-start(f32[32,16,128]{2,1,0:T(8,128)S(1)} %get-tuple-element.34), channel_id=1, source_target_pairs={{0,1},{1,0},{2,3},{3,2},{4,5},{5,4},{6,7},{7,6},{8,9},{9,8},{10,11... | collective-permute-start | bytes 786440 | tf_op jit(solution)/shard_map/ppermute | solution.py:311
  67.6 24.2 %collective-permute-start.2 = (f32[1024,128]{1,0:T(8,128)S(1)}, f32[1024,128]{1,0:T(8,128)S(1)}, u32[]{:S(2)}, u32[]{:S(2)}) collective-permute-start(f32[1024,128]{1,0:T(8,128)S(1)} %shard_map.49.own_ref), channel_id=1, source_target_pairs={{16,0},{497,1},{18,2},{499,3},{20,4},{501,5},{22,6},{503,7},{24,8}... | collective-permute-start | bytes 1572872 | tf_op jit(solution)/shard_map/ppermute | solution.py:359
  92.0 11.1 %collective-permute-start.3 = (f32[1024,128]{1,0:T(8,128)S(1)}, f32[1024,128]{1,0:T(8,128)S(1)}, u32[]{:S(2)}, u32[]{:S(2)}) collective-permute-start(f32[1024,128]{1,0:T(8,128)S(1)} %shard_map.51.own_ref), channel_id=1, source_target_pairs={{496,0},{17,1},{498,2},{19,3},{500,4},{21,5},{502,6},{23,7},{504,8... | collective-permute-start | bytes 1572872 | tf_op jit(solution)/shard_map/ppermute | solution.py:360
  104.0 10.5 %collective-permute-start.5 = (f32[1024,128]{1,0:T(8,128)S(1)}, f32[1024,128]{1,0:T(8,128)S(1)}, u32[]{:S(2)}, u32[]{:S(2)}) collective-permute-start(f32[1024,128]{1,0:T(8,128)S(1)} %shard_map.52.own), channel_id=1, source_target_pairs={{1,2},{2,1},{3,4},{4,3},{5,6},{6,5},{7,8},{8,7},{9,10},{10,9},{11,... | collective-permute-start | bytes 1572872 | tf_op jit(solution)/shard_map/ppermute | solution.py:310
  105.9 8.6 %collective-permute-start.4 = (f32[1024,128]{1,0:T(8,128)S(1)}, f32[1024,128]{1,0:T(8,128)S(1)}, u32[]{:S(2)}, u32[]{:S(2)}) collective-permute-start(f32[1024,128]{1,0:T(8,128)S(1)} %shard_map.52.own), channel_id=1, source_target_pairs={{0,1},{1,0},{2,3},{3,2},{4,5},{5,4},{6,7},{7,6},{8,9},{9,8},{10,11... | collective-permute-start | bytes 1572872 | tf_op jit(solution)/shard_map/ppermute | solution.py:311
  116.9 13.3 %collective-permute-start.6 = (f32[1024,128]{1,0:T(8,128)S(1)}, f32[1024,128]{1,0:T(8,128)S(1)}, u32[]{:S(2)}, u32[]{:S(2)}) collective-permute-start(f32[1024,128]{1,0:T(8,128)S(1)} %get-tuple-element.23.own_ref), channel_id=1, source_target_pairs={{16,0},{497,1},{18,2},{499,3},{20,4},{501,5},{22,6},{503,7},{24,8}... | collective-permute-start | bytes 1572872 | tf_op jit(solution)/shard_map/ppermute | solution.py:359
  130.5 11.5 %collective-permute-start.7 = (f32[1024,128]{1,0:T(8,128)S(1)}, f32[1024,128]{1,0:T(8,128)S(1)}, u32[]{:S(2)}, u32[]{:S(2)}) collective-permute-start(f32[1024,128]{1,0:T(8,128)S(1)} %shard_map.54.own_ref), channel_id=1, source_target_pairs={{496,0},{17,1},{498,2},{19,3},{500,4},{21,5},{502,6},{23,7},{504,8... | collective-permute-start | bytes 1572872 | tf_op jit(solution)/shard_map/ppermute | solution.py:360
  142.9 7.7 %collective-permute-start.9 = (f32[32,16,128]{2,1,0:T(8,128)S(1)}, f32[32,16,128]{2,1,0:T(8,128)S(1)}, u32[]{:S(2)}, u32[]{:S(2)}) collective-permute-start(f32[32,16,128]{2,1,0:T(8,128)S(1)} %get-tuple-element.29), channel_id=1, source_target_pairs={{1,2},{2,1},{3,4},{4,3},{5,6},{6,5},{7,8},{8,7},{9,10},{10,9},{11,... | collective-permute-start | bytes 786440 | tf_op jit(solution)/shard_map/ppermute | solution.py:310
  146.3 4.5 %collective-permute-start.8 = (f32[32,16,128]{2,1,0:T(8,128)S(1)}, f32[32,16,128]{2,1,0:T(8,128)S(1)}, u32[]{:S(2)}, u32[]{:S(2)}) collective-permute-start(f32[32,16,128]{2,1,0:T(8,128)S(1)} %get-tuple-element.30), channel_id=1, source_target_pairs={{0,1},{1,0},{2,3},{3,2},{4,5},{5,4},{6,7},{7,6},{8,9},{9,8},{10,11... | collective-permute-start | bytes 786440 | tf_op jit(solution)/shard_map/ppermute | solution.py:311

commit v6 on v5

--- a/solution.py
+++ b/solution.py
@@ -17,7 +17,7 @@
 NX = 1024
 TILES = NX // T
 NZ = 128
-ORDER = [h * 16 + int(format(i, '04b')[::-1], 2) for i in range(16) for h in range(2)]
+ORDER = [h * 16 + int(format(i, '04b')[::-1], 2) for h in range(2) for i in range(16)]
 PLACE = [ORDER.index(t) for t in range(TILES)]
 
 VMEM = pl.BlockSpec(memory_space=pltpu.VMEM)

time: 198 us -> 197 us (level)
  the two profiles are of different devices: /device:TPU:38 before, /device:TPU:7 now
where the time goes in v6:
time: 197 us; the launch traced here: 196 us
  waiting for transfers between devices  81.1 us (41%)
  starting transfers between devices  60.3 us (31%)
  blocking collectives  38.2 us (19%)
  Pallas kernels  14.9 us (8%)
    all_to_all x2, waiting for transfers between devices, exchange(): lax.all_to_all(tiles, 'gz', split_axis=0, concat_axis=0, tiled=True, axis...  40.2 us
    all_to_all x1, blocking collectives, exchange(): lax.all_to_all(tiles, 'gz', split_axis=0, concat_axis=0, tiled=True, axis...  38.2 us
    all_to_all x2, starting transfers between devices, exchange(): lax.all_to_all(tiles, 'gz', split_axis=0, concat_axis=0, tiled=True, axis...  26.2 us
    ppermute x3, starting transfers between devices, y_swap(): from_outer = lax.ppermute(to_outer, 'gy', outer)  16.5 us
    ppermute x2, waiting for transfers between devices, local(): lax.ppermute(own, joint, ahead)  14.7 us
    ppermute x2, waiting for transfers between devices, local(): lax.ppermute(own, joint, behind)  13.8 us
    ppermute x3, waiting for transfers between devices, y_swap(): from_outer = lax.ppermute(to_outer, 'gy', outer)  12.4 us
    pallas_call x10, Pallas kernels, call(): pl.pallas_call(body, out_shape=[jax.ShapeDtypeStruct(s, d) for s, d in ou...  10.5 us
  transfers between devices with their start and end apart: 12, of which 9 were waited for; matrix products, arithmetic and copies ran while one was open for 0% of the time, Pallas kernels for 3%

profile of v6, /device:TPU:7, one launch (start us, length us, event | category | flops | bytes accessed | tf_op | source)
XLA Modules:
  0.0 196.4 jit_solution(17257792521914168378)
XLA Ops:
  0.0 2.5 %shard_map.47 = f32[32,4,8,128]{3,2,1,0:T(8,128)} custom-call(f32[4,32,1024]{2,1,0:T(8,128)} %block_hbm.1), custom_call_target="tpu_custom_call" | custom-call | flops 1000000 | bytes 2000000 | tf_op jit(solution)/shard_map/pallas_call | solution.py:329
  2.5 0.0 copy-start
  2.5 18.0 %all-to-all-start = ((f32[32,4,8,128]{3,2,1,0:T(8,128)}), f32[32,4,8,128]{3,2,1,0:T(8,128)S(1)}, u32[]{:S(2)}, u32[]{:S(2)}) async-start(f32[32,4,8,128]{3,2,1,0:T(8,128)} %shard_map.47), calls=%async_computation | async-start | bytes 1048576 | tf_op jit(solution)/shard_map/all_to_all | solution.py:321
  20.5 0.0 copy-start.2
  20.5 0.7 copy-done.2
  21.2 0.1 pad_add_fusion.place_ref
  21.2 0.0 copy-start.1
  21.2 0.0 copy-done
  21.2 0.7 copy-done.1
  21.9 3.7 %shard_map.46 = (f32[32,4,8,128]{3,2,1,0:T(8,128)}, bf16[256,256]{1,0:T(8,128)(2,1)S(1)}, bf16[256,256]{1,0:T(8,128)(2,1)S(1)}, bf16[64,128]{1,0:T(8,128)(2,1)S(...) custom-call(s32[3]{0:T(128)S(1)} %pad_add_fusion.place_ref, ...), custom_call_target="tpu_custom_call" | custom-call | flops 4000000 | bytes 2000000 | tf_op jit(solution)/shard_map/pallas_call | solution.py:28
  25.6 24.7 %all-to-all-done = f32[32,4,8,128]{3,2,1,0:T(8,128)S(1)} async-done(((f32[32,4,8,128]{3,2,1,0:T(8,128)}), f32[32,4,8,128]{3,2,1,0:T(8,128)S(1)}, u32[]{:S(2)}, u32[]{:S(2)}) %all-to-all-start) | async-done | bytes 524320 | tf_op jit(solution)/shard_map/all_to_all | solution.py:321
  50.3 8.2 %all-to-all-start.1 = ((f32[32,4,8,128]{3,2,1,0:T(8,128)}), f32[32,4,8,128]{3,2,1,0:T(8,128)S(1)}, u32[]{:S(2)}, u32[]{:S(2)}) async-start(f32[32,4,8,128]{3,2,1,0:T(8,128)} %get-tuple-element.22), calls=%async_computation.1 | async-start | bytes 1048576 | tf_op jit(solution)/shard_map/all_to_all | solution.py:321
  58.5 0.4 shard_map.48.cur
  59.0 2.9 %collective-permute-start.1 = (f32[32,16,128]{2,1,0:T(8,128)S(1)}, f32[32,16,128]{2,1,0:T(8,128)S(1)}, u32[]{:S(2)}, u32[]{:S(2)}) collective-permute-start(f32[32,16,128]{2,1,0:T(8,128)S(1)} %get-tuple-element.33), channel_id=1, source_target_pairs={{1,2},{2,1},{3,4},{4,3},{5,6},{6,5},{7,8},{8,7},{9,10},{10,9},{11,... | collective-permute-start | bytes 786440 | tf_op jit(solution)/shard_map/ppermute | solution.py:310
  61.9 1.9 collective-permute-start
  63.9 5.4 %collective-permute-done.1 = f32[32,16,128]{2,1,0:T(8,128)S(1)} collective-permute-done((f32[32,16,128]{2,1,0:T(8,128)S(1)}, f32[32,16,128]{2,1,0:T(8,128)S(1)}, u32[]{:S(2)}, u32[]{:S(2)}) %collective-permute-start.1) | collective-permute-done | bytes 262176 | tf_op jit(solution)/shard_map/ppermute | solution.py:310
  69.3 0.0 collective-permute-done
  69.3 0.8 shard_map.49.own_ref
  70.1 3.2 %collective-permute-start.2 = (f32[1024,128]{1,0:T(8,128)S(1)}, f32[1024,128]{1,0:T(8,128)S(1)}, u32[]{:S(2)}, u32[]{:S(2)}) collective-permute-start(f32[1024,128]{1,0:T(8,128)S(1)} %shard_map.49.own_ref), channel_id=1, source_target_pairs={{16,0},{497,1},{18,2},{499,3},{20,4},{501,5},{22,6},{503,7},{24,8}... | collective-permute-start | bytes 1572872 | tf_op jit(solution)/shard_map/ppermute | solution.py:359
  73.4 15.5 %all-to-all-done.1 = f32[32,4,8,128]{3,2,1,0:T(8,128)S(1)} async-done(((f32[32,4,8,128]{3,2,1,0:T(8,128)}), f32[32,4,8,128]{3,2,1,0:T(8,128)S(1)}, u32[]{:S(2)}, u32[]{:S(2)}) %all-to-all-start.1) | async-done | bytes 524320 | tf_op jit(solution)/shard_map/all_to_all | solution.py:321
  88.9 0.2 shard_map.50.obs_ref
  89.2 3.1 %collective-permute-done.2.nbr_ref = f32[1024,128]{1,0:T(8,128)S(1)} collective-permute-done((f32[1024,128]{1,0:T(8,128)S(1)}, f32[1024,128]{1,0:T(8,128)S(1)}, u32[]{:S(2)}, u32[]{:S(2)}) %collective-permute-start.2) | collective-permute-done | bytes 524320 | tf_op jit(solution)/shard_map/ppermute | solution.py:359
  92.3 0.3 shard_map.51.own_ref
  92.6 3.4 %collective-permute-start.3 = (f32[1024,128]{1,0:T(8,128)S(1)}, f32[1024,128]{1,0:T(8,128)S(1)}, u32[]{:S(2)}, u32[]{:S(2)}) collective-permute-start(f32[1024,128]{1,0:T(8,128)S(1)} %shard_map.51.own_ref), channel_id=1, source_target_pairs={{496,0},{17,1},{498,2},{19,3},{500,4},{21,5},{502,6},{23,7},{504,8... | collective-permute-start | bytes 1572872 | tf_op jit(solution)/shard_map/ppermute | solution.py:360
  95.9 6.8 %collective-permute-done.3.nbr_ref = f32[1024,128]{1,0:T(8,128)S(1)} collective-permute-done((f32[1024,128]{1,0:T(8,128)S(1)}, f32[1024,128]{1,0:T(8,128)S(1)}, u32[]{:S(2)}, u32[]{:S(2)}) %collective-permute-start.3) | collective-permute-done | bytes 524320 | tf_op jit(solution)/shard_map/ppermute | solution.py:360
  102.8 0.8 shard_map.52.own
  103.6 5.9 %collective-permute-start.5 = (f32[1024,128]{1,0:T(8,128)S(1)}, f32[1024,128]{1,0:T(8,128)S(1)}, u32[]{:S(2)}, u32[]{:S(2)}) collective-permute-start(f32[1024,128]{1,0:T(8,128)S(1)} %shard_map.52.own), channel_id=1, source_target_pairs={{1,2},{2,1},{3,4},{4,3},{5,6},{6,5},{7,8},{8,7},{9,10},{10,9},{11,... | collective-permute-start | bytes 1572872 | tf_op jit(solution)/shard_map/ppermute | solution.py:310
  109.5 1.9 collective-permute-start.4
  111.4 4.9 %collective-permute-done.5 = f32[1024,128]{1,0:T(8,128)S(1)} collective-permute-done((f32[1024,128]{1,0:T(8,128)S(1)}, f32[1024,128]{1,0:T(8,128)S(1)}, u32[]{:S(2)}, u32[]{:S(2)}) %collective-permute-start.5) | collective-permute-done | bytes 524320 | tf_op jit(solution)/shard_map/ppermute | solution.py:310
  116.4 0.0 collective-permute-done.4
  116.4 0.1 broadcast_select_fusion
  116.4 2.3 %shard_map.53 = (f32[1024,128]{1,0:T(8,128)S(1)}, f32[1024,128]{1,0:T(8,128)S(1)}) custom-call(bf16[128,192]{1,0:T(8,128)(2,1)S(1)} %get-tuple-element.19.back_ref, bf16[64,128]{1,0:T(8,128)(2,1)S(1)} %get-tuple-element.20.my_ref.fwd_ref, bf16[256,256]{1,0:T(8,128)(2,1)S(1)} %get-tuple-element.21.mz_ref, f32[1024,128]{1,0:T(8,128)S(1)} %get-tuple-element.26.up, ...), custom_call_target="tpu_custom_call" | custom-call | flops 4000000 | bytes 2000000 | tf_op jit(solution)/shard_map/pallas_call | solution.py:28
  118.8 1.9 collective-permute-start.6
  120.7 11.6 %collective-permute-done.6.nbr_ref = f32[1024,128]{1,0:T(8,128)S(1)} collective-permute-done((f32[1024,128]{1,0:T(8,128)S(1)}, f32[1024,128]{1,0:T(8,128)S(1)}, u32[]{:S(2)}, u32[]{:S(2)}) %collective-permute-start.6) | collective-permute-done | bytes 524320 | tf_op jit(solution)/shard_map/ppermute | solution.py:359
  132.3 0.3 shard_map.54.own_ref
  132.6 3.3 %collective-permute-start.7 = (f32[1024,128]{1,0:T(8,128)S(1)}, f32[1024,128]{1,0:T(8,128)S(1)}, u32[]{:S(2)}, u32[]{:S(2)}) collective-permute-start(f32[1024,128]{1,0:T(8,128)S(1)} %shard_map.54.own_ref), channel_id=1, source_target_pairs={{496,0},{17,1},{498,2},{19,3},{500,4},{21,5},{502,6},{23,7},{504,8... | collective-permute-start | bytes 1572872 | tf_op jit(solution)/shard_map/ppermute | solution.py:360
  135.9 6.9 %collective-permute-done.7.nbr_ref = f32[1024,128]{1,0:T(8,128)S(1)} collective-permute-done((f32[1024,128]{1,0:T(8,128)S(1)}, f32[1024,128]{1,0:T(8,128)S(1)}, u32[]{:S(2)}, u32[]{:S(2)}) %collective-permute-start.7) | collective-permute-done | bytes 524320 | tf_op jit(solution)/shard_map/ppermute | solution.py:360
  142.8 0.8 shard_map.55.own
  143.7 7.8 %collective-permute-start.9 = (f32[32,16,128]{2,1,0:T(8,128)S(1)}, f32[32,16,128]{2,1,0:T(8,128)S(1)}, u32[]{:S(2)}, u32[]{:S(2)}) collective-permute-start(f32[32,16,128]{2,1,0:T(8,128)S(1)} %get-tuple-element.29), channel_id=1, source_target_pairs={{1,2},{2,1},{3,4},{4,3},{5,6},{6,5},{7,8},{8,7},{9,10},{10,9},{11,... | collective-permute-start | bytes 786440 | tf_op jit(solution)/shard_map/ppermute | solution.py:310
  151.5 1.9 collective-permute-start.8
  153.4 2.1 %collective-permute-done.9 = f32[32,16,128]{2,1,0:T(8,128)S(1)} collective-permute-done((f32[32,16,128]{2,1,0:T(8,128)S(1)}, f32[32,16,128]{2,1,0:T(8,128)S(1)}, u32[]{:S(2)}, u32[]{:S(2)}) %collective-permute-start.9) | collective-permute-done | bytes 262176 | tf_op jit(solution)/shard_map/ppermute | solution.py:310
  155.5 0.0 collective-permute-done.8
  155.6 0.7 shard_map.56
  156.3 38.2 %all_to_all.15.tiles_ref = f32[32,4,8,128]{3,2,1,0:T(8,128)S(1)} all-to-all(f32[32,4,8,128]{3,2,1,0:T(8,128)S(1)} %bitcast.21), channel_id=1, replica_groups={{0,128,64,192,32,160,96,224,16,144,80,208,48,176,112,240,256,384,320,44..., dimensions={0} | all-to-all | bytes 1048576 | tf_op jit(solution)/shard_map/all_to_all | solution.py:321
  194.5 1.9 shard_map.57
  (5 shorter events, 0.2 us)
Async XLA Ops:
  2.5 18.8 %copy-start = (f32[4,32,1024]{2,1,0:T(8,128)S(1)}, f32[4,32,1024]{2,1,0:T(8,128)}, u32[]{:S(2)}) copy-start(f32[4,32,1024]{2,1,0:T(8,128)} %obs_ref.1) | copy-start | bytes 1572868
  2.5 47.8 %all-to-all-start = ((f32[32,4,8,128]{3,2,1,0:T(8,128)}), f32[32,4,8,128]{3,2,1,0:T(8,128)S(1)}, u32[]{:S(2)}, u32[]{:S(2)}) async-start(f32[32,4,8,128]{3,2,1,0:T(8,128)} %shard_map.47), calls=%async_computation | async-start | bytes 1048576 | tf_op jit(solution)/shard_map/all_to_all | solution.py:321
  20.5 0.7 copy-start.2
  21.2 0.7 copy-start.1
  50.3 38.6 %all-to-all-start.1 = ((f32[32,4,8,128]{3,2,1,0:T(8,128)}), f32[32,4,8,128]{3,2,1,0:T(8,128)S(1)}, u32[]{:S(2)}, u32[]{:S(2)}) async-start(f32[32,4,8,128]{3,2,1,0:T(8,128)} %get-tuple-element.22), calls=%async_computation.1 | async-start | bytes 1048576 | tf_op jit(solution)/shard_map/all_to_all | solution.py:321
  59.0 10.2 %collective-permute-start.1 = (f32[32,16,128]{2,1,0:T(8,128)S(1)}, f32[32,16,128]{2,1,0:T(8,128)S(1)}, u32[]{:S(2)}, u32[]{:S(2)}) collective-permute-start(f32[32,16,128]{2,1,0:T(8,128)S(1)} %get-tuple-element.33), channel_id=1, source_target_pairs={{1,2},{2,1},{3,4},{4,3},{5,6},{6,5},{7,8},{8,7},{9,10},{10,9},{11,... | collective-permute-start | bytes 786440 | tf_op jit(solution)/shard_map/ppermute | solution.py:310
  61.9 7.3 %collective-permute-start = (f32[32,16,128]{2,1,0:T(8,128)S(1)}, f32[32,16,128]{2,1,0:T(8,128)S(1)}, u32[]{:S(2)}, u32[]{:S(2)}) collective-permute-start(f32[32,16,128]{2,1,0:T(8,128)S(1)} %get-tuple-element.34), channel_id=1, source_target_pairs={{0,1},{1,0},{2,3},{3,2},{4,5},{5,4},{6,7},{7,6},{8,9},{9,8},{10,11... | collective-permute-start | bytes 786440 | tf_op jit(solution)/shard_map/ppermute | solution.py:311
  70.1 22.1 %collective-permute-start.2 = (f32[1024,128]{1,0:T(8,128)S(1)}, f32[1024,128]{1,0:T(8,128)S(1)}, u32[]{:S(2)}, u32[]{:S(2)}) collective-permute-start(f32[1024,128]{1,0:T(8,128)S(1)} %shard_map.49.own_ref), channel_id=1, source_target_pairs={{16,0},{497,1},{18,2},{499,3},{20,4},{501,5},{22,6},{503,7},{24,8}... | collective-permute-start | bytes 1572872 | tf_op jit(solution)/shard_map/ppermute | solution.py:359
  92.6 10.2 %collective-permute-start.3 = (f32[1024,128]{1,0:T(8,128)S(1)}, f32[1024,128]{1,0:T(8,128)S(1)}, u32[]{:S(2)}, u32[]{:S(2)}) collective-permute-start(f32[1024,128]{1,0:T(8,128)S(1)} %shard_map.51.own_ref), channel_id=1, source_target_pairs={{496,0},{17,1},{498,2},{19,3},{500,4},{21,5},{502,6},{23,7},{504,8... | collective-permute-start | bytes 1572872 | tf_op jit(solution)/shard_map/ppermute | solution.py:360
  103.6 12.7 %collective-permute-start.5 = (f32[1024,128]{1,0:T(8,128)S(1)}, f32[1024,128]{1,0:T(8,128)S(1)}, u32[]{:S(2)}, u32[]{:S(2)}) collective-permute-start(f32[1024,128]{1,0:T(8,128)S(1)} %shard_map.52.own), channel_id=1, source_target_pairs={{1,2},{2,1},{3,4},{4,3},{5,6},{6,5},{7,8},{8,7},{9,10},{10,9},{11,... | collective-permute-start | bytes 1572872 | tf_op jit(solution)/shard_map/ppermute | solution.py:310
  109.5 6.9 %collective-permute-start.4 = (f32[1024,128]{1,0:T(8,128)S(1)}, f32[1024,128]{1,0:T(8,128)S(1)}, u32[]{:S(2)}, u32[]{:S(2)}) collective-permute-start(f32[1024,128]{1,0:T(8,128)S(1)} %shard_map.52.own), channel_id=1, source_target_pairs={{0,1},{1,0},{2,3},{3,2},{4,5},{5,4},{6,7},{7,6},{8,9},{9,8},{10,11... | collective-permute-start | bytes 1572872 | tf_op jit(solution)/shard_map/ppermute | solution.py:311
  118.8 13.5 %collective-permute-start.6 = (f32[1024,128]{1,0:T(8,128)S(1)}, f32[1024,128]{1,0:T(8,128)S(1)}, u32[]{:S(2)}, u32[]{:S(2)}) collective-permute-start(f32[1024,128]{1,0:T(8,128)S(1)} %get-tuple-element.23.own_ref), channel_id=1, source_target_pairs={{16,0},{497,1},{18,2},{499,3},{20,4},{501,5},{22,6},{503,7},{24,8}... | collective-permute-start | bytes 1572872 | tf_op jit(solution)/shard_map/ppermute | solution.py:359
  132.6 10.2 %collective-permute-start.7 = (f32[1024,128]{1,0:T(8,128)S(1)}, f32[1024,128]{1,0:T(8,128)S(1)}, u32[]{:S(2)}, u32[]{:S(2)}) collective-permute-start(f32[1024,128]{1,0:T(8,128)S(1)} %shard_map.54.own_ref), channel_id=1, source_target_pairs={{496,0},{17,1},{498,2},{19,3},{500,4},{21,5},{502,6},{23,7},{504,8... | collective-permute-start | bytes 1572872 | tf_op jit(solution)/shard_map/ppermute | solution.py:360
  143.7 11.8 %collective-permute-start.9 = (f32[32,16,128]{2,1,0:T(8,128)S(1)}, f32[32,16,128]{2,1,0:T(8,128)S(1)}, u32[]{:S(2)}, u32[]{:S(2)}) collective-permute-start(f32[32,16,128]{2,1,0:T(8,128)S(1)} %get-tuple-element.29), channel_id=1, source_target_pairs={{1,2},{2,1},{3,4},{4,3},{5,6},{6,5},{7,8},{8,7},{9,10},{10,9},{11,... | collective-permute-start | bytes 786440 | tf_op jit(solution)/shard_map/ppermute | solution.py:310
  151.5 4.0 %collective-permute-start.8 = (f32[32,16,128]{2,1,0:T(8,128)S(1)}, f32[32,16,128]{2,1,0:T(8,128)S(1)}, u32[]{:S(2)}, u32[]{:S(2)}) collective-permute-start(f32[32,16,128]{2,1,0:T(8,128)S(1)} %get-tuple-element.30), channel_id=1, source_target_pairs={{0,1},{1,0},{2,3},{3,2},{4,5},{5,4},{6,7},{7,6},{8,9},{9,8},{10,11... | collective-permute-start | bytes 786440 | tf_op jit(solution)/shard_map/ppermute | solution.py:311
